TPU v7x, 32 devices: a whole 2x2x4 slice. The times are simulated.
32 devices in a mesh: dp: 16 (over z, y, x), twin: 2 (over core).
Axes of the slice: x: 2, y: 2, z: 4, core: 2. Of those that a mesh axis runs over, the one named last changes fastest.
Arguments:
- states: float32 [17, 262144], P(None, 'dp'), may hold values from -6 to 6
- actions: float32 [6, 262144], P(None, 'dp'), may hold values from -1 to 1
- rewards: float32 [262144], P('dp'), may hold values from -10 to 10
- next_states: float32 [17, 262144], P(None, 'dp'), may hold values from -6 to 6
- done_flags: int32 [262144], P('dp'), may hold values 0 or 1
- smoothing: float32 [6, 262144], P(None, 'dp'), may hold values from -6 to 6
- actor_weights: float32 [71942], replicated, may hold values from -1 to 1
- actor_first: float32 [71942], replicated, may hold values from -0.046875 to 0.046875
- actor_second: float32 [71942], replicated, may hold values from 5e-07 to 8e-06
- critic_weights: float32 [2, 72193], P('twin'), may hold values from -1 to 1
- critic_first: float32 [2, 72193], P('twin'), may hold values from -0.0034179688 to 0.0034179688
- critic_second: float32 [2, 72193], P('twin'), may hold values from 1.9073487e-09 to 3.051758e-08
- target_actor: float32 [71942], replicated, may hold values from -1 to 1
- target_critic: float32 [2, 72193], P('twin'), may hold values from -1 to 1
Outputs:
- new_actor: float32 [71942], replicated
- new_actor_first: float32 [71942], replicated
- new_actor_second: float32 [71942], replicated
- new_critic: float32 [2, 72193], P('twin')
- new_critic_first: float32 [2, 72193], P('twin')
- new_critic_second: float32 [2, 72193], P('twin')
- new_target_actor: float32 [71942], replicated
- new_target_critic: float32 [2, 72193], P('twin')
- critic_loss: float32 [2], P('twin')
- actor_loss: float32 [], replicated
All inputs are finite; a program needn't handle non-finite values. No bound on the sum of `done_flags` on one device may be relied on, other than what follows from the above.
Results may differ from a plain program's by a relative error of at most 0.0003.
The roundings to bfloat16 on the way count: a program that leaves them out, or rounds other values in their place, can miss the bound.
Values sent between devices are 32-bit elements; how exact they have to be, the bound alone decides.
No kernel may reach another device: no remote copies, remote signals or barrier semaphores. Data moves between devices by JAX's collectives and lax.ppermute only.
A program may use at most 192 MiB of HBM per device.

v0:
```python
import jax
import jax.numpy as jnp
from jax import lax
from jax.sharding import PartitionSpec as P

SDIM = 17
ADIM = 6
HID = 256
MB = 4
STEP = 10


DISCOUNT = 0.99
POLYAK_RATE = 0.005
LEARN_RATE = 0.05
BETA_ONE = 0.9
BETA_TWO = 0.999
EPSILON = 1e-08
WEIGHT_DECAY = 0.01
NOISE_SCALE = 0.2
NOISE_CLIP = 0.5


def partner(value, axis, bit):
    mask = 2**bit
    pairs = [(source, source ^ mask) for source in range(lax.axis_size(axis))]
    return lax.ppermute(value, axis, pairs)


def from_root(value, axis, source):
    kept = jnp.where(lax.axis_index(axis) == source, value, 0).astype(value.dtype)
    return lax.psum(kept, axis)


def actor_layers():
    return ((HID, SDIM), (HID, HID), (ADIM, HID))


def critic_layers():
    return ((HID, SDIM + ADIM), (HID, HID), (1, HID))


def unchanged(value):
    return value


def unpack(flat_vec, layers):
    params = []
    position = 0
    for out_size, in_size in layers:
        weight = (
            flat_vec[position : position + out_size * in_size]
            .reshape(out_size, in_size)
            .astype(jnp.bfloat16)
        )
        position += out_size * in_size
        params.append((weight, flat_vec[position : position + out_size][:, None]))
        position += out_size
    return params


def forward(params, inputs, final_act):
    kept_list = []
    hidden = inputs
    for layer_index, (weight, bias_term) in enumerate(params):
        moved_low = hidden.astype(jnp.bfloat16)
        pre_act = jnp.dot(weight, moved_low, preferred_element_type=jnp.float32) + bias_term
        kept_list.append((moved_low, pre_act))
        hidden = final_act(pre_act) if layer_index == len(params) - 1 else jax.nn.silu(pre_act)
    return (hidden, kept_list)


def silu_slope(pre_act):
    logistic = jax.nn.sigmoid(pre_act)
    return logistic * (1.0 + pre_act * (1.0 - logistic))


def backward(params, kept_list, grad_pre, weights_too, input_too):
    gradients = []
    grad_input = None
    for layer_index in range(len(params) - 1, -1, -1):
        weight = params[layer_index][0]
        moved_low = kept_list[layer_index][0]
        grad_low = grad_pre.astype(jnp.bfloat16)
        if weights_too:
            grad_weight = jnp.einsum(
                "on,in->oi", grad_low, moved_low, preferred_element_type=jnp.float32
            )
            gradients = [
                grad_weight.reshape(-1),
                jnp.sum(grad_low.astype(jnp.float32), axis=1),
            ] + gradients
        if layer_index > 0 or input_too:
            grad_input = jnp.einsum(
                "oi,on->in", weight, grad_low, preferred_element_type=jnp.float32
            )
            if layer_index > 0:
                grad_pre = grad_input * silu_slope(kept_list[layer_index - 1][1])
    flat_grad = jnp.concatenate(gradients) if weights_too else None
    return (flat_grad, grad_input)


def adamw_step(weight, gradient, moment_one, moment_two):
    moment_one = BETA_ONE * moment_one + (1.0 - BETA_ONE) * gradient
    moment_two = BETA_TWO * moment_two + (1.0 - BETA_TWO) * gradient * gradient
    corrected_one = moment_one / (1.0 - BETA_ONE**STEP)
    corrected_two = moment_two / (1.0 - BETA_TWO**STEP)
    weight = weight - LEARN_RATE * (
        corrected_one / (jnp.sqrt(corrected_two) + EPSILON) + WEIGHT_DECAY * weight
    )
    return (weight, moment_one, moment_two)


def polyak_mix(lagged, fresh):
    return POLYAK_RATE * fresh + (1.0 - POLYAK_RATE) * lagged


def on_device(
    states,
    actions,
    rewards,
    next_states,
    done_flags,
    smoothing,
    actor_weights,
    actor_first,
    actor_second,
    critic_weights,
    critic_first,
    critic_second,
    target_actor,
    target_critic,
):
    twin_index = lax.axis_index("twin")
    local_rows = states.shape[1]
    sub_batch = local_rows // MB
    halfway = sub_batch // 2
    row_total = local_rows * lax.axis_size("dp")
    actor_params = unpack(actor_weights, actor_layers())
    lagged_actor = unpack(target_actor, actor_layers())
    critic_params = unpack(critic_weights[0], critic_layers())
    lagged_critic = unpack(target_critic[0], critic_layers())
    critic_grad = jnp.zeros(critic_weights.shape[1:], jnp.float32)
    critic_sum = jnp.zeros((), jnp.float32)
    for micro_index in range(MB):
        low_col = micro_index * sub_batch
        high_col = low_col + sub_batch
        next_rows = next_states[:, low_col:high_col]
        lagged_out, unused = forward(lagged_actor, next_rows, jnp.tanh)
        jitter = jnp.clip(NOISE_SCALE * smoothing[:, low_col:high_col], -NOISE_CLIP, NOISE_CLIP)
        next_action = jnp.clip(lagged_out + jitter, -1.0, 1.0)
        lagged_q, unused = forward(
            lagged_critic, jnp.concatenate([next_rows, next_action], 0), unchanged
        )
        partner_q = partner(lagged_q[0], "twin", 0)
        keep_going = 1.0 - done_flags[low_col:high_col].astype(jnp.float32)
        target = rewards[low_col:high_col] + DISCOUNT * keep_going * jnp.minimum(
            lagged_q[0], partner_q
        )
        joined = jnp.concatenate([states[:, low_col:high_col], actions[:, low_col:high_col]], 0)
        critic_q, kept_list = forward(critic_params, joined, unchanged)
        q_error = critic_q[0] - target
        critic_sum = critic_sum + jnp.sum(q_error * q_error)
        gradients, unused = backward(
            critic_params, kept_list, 2.0 / row_total * q_error[None, :], True, False
        )
        critic_grad = critic_grad + gradients
    critic_grad = lax.psum(critic_grad, "dp")
    new_critic, critic_one, critic_two = adamw_step(
        critic_weights[0], critic_grad, critic_first[0], critic_second[0]
    )
    lagged_new = polyak_mix(target_critic[0], new_critic)
    shared = from_root(new_critic, "twin", 0)
    first_critic = unpack(shared, critic_layers())
    actor_grad = jnp.zeros(actor_weights.shape, jnp.float32)
    actor_sum = jnp.zeros((), jnp.float32)
    for micro_index in range(MB):
        state_rows = lax.dynamic_slice_in_dim(
            states, micro_index * sub_batch + twin_index * halfway, halfway, 1
        )
        action_out, actor_kept = forward(actor_params, state_rows, jnp.tanh)
        first_q, judge_kept = forward(
            first_critic, jnp.concatenate([state_rows, action_out], 0), unchanged
        )
        actor_sum = actor_sum + jnp.sum(first_q)
        unused, grad_input = backward(
            first_critic,
            judge_kept,
            jnp.full((1, halfway), -1.0 / row_total, jnp.float32),
            False,
            True,
        )
        grad_pre = grad_input[SDIM:] * (1.0 - action_out * action_out)
        gradients, unused = backward(actor_params, actor_kept, grad_pre, True, False)
        actor_grad = actor_grad + gradients
    actor_grad = lax.psum(actor_grad, ("dp", "twin"))
    new_actor, actor_one, actor_two = adamw_step(
        actor_weights, actor_grad, actor_first, actor_second
    )
    lagged_actor_new = polyak_mix(target_actor, new_actor)
    critic_vec = jnp.where(jnp.arange(2) == twin_index, critic_sum, 0.0)
    loss_pair, actor_loss = lax.psum((critic_vec, -actor_sum), ("dp", "twin"))
    critic_loss = lax.dynamic_slice_in_dim(loss_pair, twin_index, 1)
    return (
        new_actor,
        actor_one,
        actor_two,
        new_critic[None],
        critic_one[None],
        critic_two[None],
        lagged_actor_new,
        lagged_new[None],
        critic_loss,
        actor_loss,
    )


def solution(mesh):
    placed = (
        P(None, "dp"),
        P(None, "dp"),
        P("dp"),
        P(None, "dp"),
        P("dp"),
        P(None, "dp"),
        P(),
        P(),
        P(),
        P("twin", None),
        P("twin", None),
        P("twin", None),
        P(),
        P("twin", None),
    )
    return jax.shard_map(
        on_device,
        mesh=mesh,
        in_specs=placed,
        out_specs=(
            P(),
            P(),
            P(),
            P("twin", None),
            P("twin", None),
            P("twin", None),
            P(),
            P("twin", None),
            P("twin"),
            P(),
        ),
        check_vma=False,
    )
```

profile of v0, /device:TPU:0, one launch (start us, length us, event | category | flops | bytes accessed | tf_op | source)
XLA Modules:
  0.0 576.1 jit_solution(5649391370887908999)
XLA Ops:
  9.8 2.8 fusion.214
  16.0 2.6 multiply_convert_fusion.21
  18.6 3.0 fusion.44
  21.6 2.7 multiply_convert_fusion.19
  24.3 3.0 fusion.88
  29.0 2.6 multiply_convert_fusion.15
  31.7 3.0 fusion.45
  34.7 2.7 multiply_convert_fusion.13
  37.4 3.5 fusion.89
  42.2 2.6 multiply_convert_fusion.3
  44.8 3.0 fusion.47
  47.8 2.7 multiply_convert_fusion.1
  50.5 3.0 fusion.91
  55.2 2.6 multiply_convert_fusion.9
  57.9 3.0 fusion.46
  60.9 2.7 multiply_convert_fusion.7
  63.6 3.1 fusion.90
  72.0 3.2 multiply_convert_fusion.17
  75.3 3.2 multiply_convert_fusion.16
  79.8 3.3 multiply_convert_fusion.23
  83.1 3.2 multiply_convert_fusion.22
  87.6 3.3 multiply_convert_fusion.5
  90.9 3.3 multiply_convert_fusion.4
  95.5 3.4 multiply_convert_fusion.11
  98.8 3.4 multiply_convert_fusion.10
  118.8 2.7 multiply_convert_fusion.42
  123.5 2.8 multiply_reduce_fusion.5
  128.7 2.7 multiply_reduce_fusion.4
  132.6 10.8 %convert_reduce_fusion.4 = (f32[256]{0:T(256)}, bf16[256,4096]{0,1:T(8,128)(2,1)S(1)}, f32[256]{0:T(256)S(1)}, bf16[256,4096]{0,1:T(8,128)(2,1)}, f32[256]{0:T(2...) fusion(f32[256,4096]{0,1:T(8,128)} %get-tuple-element.87, f32[256]{0:T(256)S(1)} %convert.124, ...), kind=kLoop, calls=%fused_computation.108 | loop fusion | flops 50330624 | bytes 25236480 | tf_op jit(solution)/shard_map/reduce_sum | solution.py:91
  152.6 2.6 fusion.219
  155.1 3.2 convolution_bitcast_fusion.19
  165.1 2.5 fusion.218
  176.5 2.7 fusion.220
  200.6 3.4 multiply_reduce_fusion.1
  204.5 106.3 %all-reduce.5.cloned.1.call-done = f32[72193]{0:T(1024)} async-done(((f32[72193]{0:T(1024)}), f32[72193]{0:T(1024)}) %all-reduce.5.cloned.1.call-update) | async-done | bytes 288788 | tf_op jit(solution)/shard_map/psum | solution.py:168
  320.9 10.5 %all-reduce.7.cloned.1.call-done = f32[72193]{0:T(1024)} async-done(((f32[72193]{0:T(1024)}), f32[72193]{0:T(1024)}) %all-reduce.7.cloned.1.call-update) | async-done | bytes 288788 | tf_op jit(solution)/shard_map/psum | solution.py:32
  337.9 5.3 convert_reduce_fusion.18
  344.2 3.3 convert_reduce_fusion.12
  349.0 2.5 convert_reduce_fusion.13
  357.6 4.5 convert_reduce_fusion.19
  363.0 3.3 convert_reduce_fusion.14
  368.2 2.5 convert_reduce_fusion.15
  374.9 4.5 convert_reduce_fusion.17
  381.1 3.3 convert_reduce_fusion.10
  392.5 4.1 convert_reduce_fusion.16
  396.8 2.7 convert_reduce_fusion.8
  446.0 40.5 %all-reduce = (f32[2]{0:T(128)S(1)}, f32[]{:T(128)}) all-reduce(f32[2]{0:T(128)S(1)} %copy-done.133, f32[]{:T(128)S(6)} %neg.189), channel_id=1, replica_groups=mesh['dp'=16,'twin'=2] {'dp','twin'}, use_global_device_ids=true, to_apply=%region_31.32 | all-reduce | flops 3 | bytes 24 | tf_op jit(solution)/shard_map/psum | solution.py:202
  487.1 80.2 %all-reduce.9.cloned.1.call-done = f32[71942]{0:T(1024)} async-done(((f32[71942]{0:T(1024)}), f32[71942]{0:T(1024)}) %all-reduce.9.cloned.1.call-update) | async-done | bytes 287784 | tf_op jit(solution)/shard_map/psum | solution.py:196
  (531 shorter events, 173.8 us)
Async XLA Ops:
  7.2 303.5 %all-reduce.5.cloned.1.call-start = ((), (), s32[]{:S(2)}) async-start(), calls=%async_computation | async-start | bytes 581632 | tf_op jit(solution)/shard_map/psum | solution.py:168
  28.6 94.8 %collective-permute-start = (f32[4096]{0:T(1024)}, f32[4096]{0:T(1024)}, u32[]{:S(2)}, u32[]{:S(2)}) collective-permute-start(f32[4096]{0:T(1024)} %broadcast_add_fusion.3), channel_id=1, source_target_pairs={{0,1},{1,0},{2,3},{3,2},{4,5},{5,4},{6,7},{7,6},{8,9},{9,8},{10,11... | collective-permute-start | bytes 49160 | tf_op jit(solution)/shard_map/ppermute | solution.py:27
  42.1 81.3 %collective-permute-start.1 = (f32[4096]{0:T(1024)}, f32[4096]{0:T(1024)}, u32[]{:S(2)}, u32[]{:S(2)}) collective-permute-start(f32[4096]{0:T(1024)} %broadcast_add_fusion.2), channel_id=1, source_target_pairs={{0,1},{1,0},{2,3},{3,2},{4,5},{5,4},{6,7},{7,6},{8,9},{9,8},{10,11... | collective-permute-start | bytes 49160 | tf_op jit(solution)/shard_map/ppermute | solution.py:27
  54.8 68.6 %collective-permute-start.3 = (f32[4096]{0:T(1024)}, f32[4096]{0:T(1024)}, u32[]{:S(2)}, u32[]{:S(2)}) collective-permute-start(f32[4096]{0:T(1024)} %broadcast_add_fusion), channel_id=1, source_target_pairs={{0,1},{1,0},{2,3},{3,2},{4,5},{5,4},{6,7},{7,6},{8,9},{9,8},{10,11... | collective-permute-start | bytes 49160 | tf_op jit(solution)/shard_map/ppermute | solution.py:27
  68.0 60.7 %collective-permute-start.2 = (f32[4096]{0:T(1024)}, f32[4096]{0:T(1024)}, u32[]{:S(2)}, u32[]{:S(2)}) collective-permute-start(f32[4096]{0:T(1024)} %broadcast_add_fusion.1), channel_id=1, source_target_pairs={{0,1},{1,0},{2,3},{3,2},{4,5},{5,4},{6,7},{7,6},{8,9},{9,8},{10,11... | collective-permute-start | bytes 49160 | tf_op jit(solution)/shard_map/ppermute | solution.py:27
  69.8 32.4 %copy-start.32 = (bf16[1,72193]{1,0:T(2,128)(2,1)}, bf16[1,72193]{1,0:T(2,128)(2,1)S(1)}, u32[]{:S(2)}) copy-start(bf16[1,72193]{1,0:T(2,128)(2,1)S(1)} %get-tuple-element.68) | copy-start | bytes 433162
  71.8 15.8 %copy-start.59 = (bf16[17,4096]{1,0:T(8,128)(2,1)}, bf16[17,4096]{1,0:T(8,128)(2,1)S(1)}, u32[]{:S(2)}) copy-start(bf16[17,4096]{1,0:T(8,128)(2,1)S(1)} %get-tuple-element.53) | copy-start | bytes 417796
  71.8 23.6 %copy-start.61 = (bf16[17,4096]{1,0:T(8,128)(2,1)}, bf16[17,4096]{1,0:T(8,128)(2,1)S(1)}, u32[]{:S(2)}) copy-start(bf16[17,4096]{1,0:T(8,128)(2,1)S(1)} %get-tuple-element.54) | copy-start | bytes 417796
  71.9 15.7 %copy-start.94 = (bf16[6,4096]{1,0:T(8,128)(2,1)}, bf16[6,4096]{1,0:T(8,128)(2,1)S(1)}, u32[]{:S(2)}) copy-start(bf16[6,4096]{1,0:T(8,128)(2,1)S(1)} %get-tuple-element.71) | copy-start | bytes 147460
  72.0 23.5 %copy-start.96 = (bf16[6,4096]{1,0:T(8,128)(2,1)}, bf16[6,4096]{1,0:T(8,128)(2,1)S(1)}, u32[]{:S(2)}) copy-start(bf16[6,4096]{1,0:T(8,128)(2,1)S(1)} %get-tuple-element.72) | copy-start | bytes 147460
  72.0 26.8 %copy-start.75 = (bf16[256,256]{1,0:T(8,128)(2,1)}, bf16[256,256]{1,0:T(8,128)(2,1)S(1)}, u32[]{:S(2)}) copy-start(bf16[256,256]{1,0:T(8,128)(2,1)S(1)} %convert_element_type.380) | copy-start | bytes 393220
  118.8 9.9 %copy-start.86 = (f32[1,4096]{1,0:T(1,128)S(1)}, f32[1,4096]{1,0:T(1,128)}, u32[]{:S(2)}) copy-start(f32[1,4096]{1,0:T(1,128)} %fusion.152) | copy-start | bytes 49156
  132.6 10.8 %copy-start.143 = (bf16[256,4096]{0,1:T(8,128)(2,1)S(1)}, bf16[256,4096]{0,1:T(8,128)(2,1)}, u32[]{:S(2)}) copy-start(bf16[256,4096]{0,1:T(8,128)(2,1)} %copy-done.142) | copy-start | bytes 6291460
  188.1 8.5 %copy-start.112 = (f32[1,256]{1,0:T(1,128)S(1)}, f32[1,256]{1,0:T(1,128)}, u32[]{:S(2)}) copy-start(f32[1,256]{1,0:T(1,128)} %fusion.218) | copy-start | bytes 3076
  188.1 9.1 %copy-start.49 = (f32[72193]{0:T(1024)S(1)}, f32[72193]{0:T(1024)}, u32[]{:S(2)}) copy-start(f32[72193]{0:T(1024)} %custom-call.5) | copy-start | bytes 866320
  188.1 9.1 %copy-start.84 = (f32[5888]{0:T(1024)S(1)}, f32[5888]{0:T(1024)}, u32[]{:S(2)}) copy-start(f32[5888]{0:T(1024)} %reshape.274) | copy-start | bytes 70660
  188.1 9.1 %copy-start.121 = (f32[256]{0:T(256)S(1)}, f32[256]{0:T(256)}, u32[]{:S(2)}) copy-start(f32[256]{0:T(256)} %get-tuple-element.102) | copy-start | bytes 3076
  188.1 9.1 %copy-start.37 = (f32[32,2,8,128]{3,1,2,0:T(2,128)S(1)}, f32[32,2,8,128]{3,1,2,0:T(2,128)}, u32[]{:S(2)}) copy-start(f32[32,2,8,128]{3,1,2,0:T(2,128)} %copy.78) | copy-start | bytes 786436
  188.2 9.2 %copy-start.110 = (f32[1,256]{1,0:T(1,128)S(1)}, f32[1,256]{1,0:T(1,128)}, u32[]{:S(2)}) copy-start(f32[1,256]{1,0:T(1,128)} %fusion.220) | copy-start | bytes 3076
  188.2 9.8 %copy-start.48 = (f32[72193]{0:T(1024)S(1)}, f32[72193]{0:T(1024)}, u32[]{:S(2)}) copy-start(f32[72193]{0:T(1024)} %custom-call.4) | copy-start | bytes 866320
  188.2 9.8 %copy-start.85 = (f32[5888]{0:T(1024)S(1)}, f32[5888]{0:T(1024)}, u32[]{:S(2)}) copy-start(f32[5888]{0:T(1024)} %reshape.276) | copy-start | bytes 70660
  188.2 9.9 %copy-start.120 = (f32[256]{0:T(256)S(1)}, f32[256]{0:T(256)}, u32[]{:S(2)}) copy-start(f32[256]{0:T(256)} %get-tuple-element.100) | copy-start | bytes 3076
  188.2 9.9 %copy-start.36 = (f32[32,2,8,128]{3,1,2,0:T(2,128)S(1)}, f32[32,2,8,128]{3,1,2,0:T(2,128)}, u32[]{:S(2)}) copy-start(f32[32,2,8,128]{3,1,2,0:T(2,128)} %copy.79) | copy-start | bytes 786436
  188.6 12.0 %copy-start.51 = (f32[1,72193]{1,0:T(1,128)S(1)}, f32[1,72193]{1,0:T(1,128)}, u32[]{:S(2)}) copy-start(f32[1,72193]{1,0:T(1,128)} %param.25) | copy-start | bytes 866320
  198.1 112.6 %copy-start.28 = (f32[72193]{0:T(1024)S(1)}, f32[72193]{0:T(1024)}, u32[]{:S(2)}) copy-start(f32[72193]{0:T(1024)} %get-tuple-element.65) | copy-start | bytes 866320
  198.1 112.6 %copy-start.29 = (f32[72193]{0:T(1024)S(1)}, f32[72193]{0:T(1024)}, u32[]{:S(2)}) copy-start(f32[72193]{0:T(1024)} %get-tuple-element.69) | copy-start | bytes 866320
  200.6 130.9 %all-reduce.7.cloned.1.call-start = ((), (), s32[]{:S(2)}) async-start(), calls=%async_computation.1 | async-start | bytes 581632 | tf_op jit(solution)/shard_map/psum | solution.py:32
  204.5 113.7 %copy-start.55 = (f32[2048,6]{0,1:T(8,128)}, f32[2048,6]{0,1:T(8,128)S(1)}, u32[]{:S(2)}) copy-start(f32[2048,6]{0,1:T(8,128)S(1)} %fusion.83) | copy-start | bytes 147460
  312.9 21.0 %copy-start.23 = (bf16[17,2048]{1,0:T(8,128)(2,1)S(1)}, bf16[17,2048]{1,0:T(8,128)(2,1)}, u32[]{:S(2)}) copy-start(bf16[17,2048]{1,0:T(8,128)(2,1)} %copy-done.22) | copy-start | bytes 208900
  312.9 21.0 %copy-start.68 = (bf16[6,2048]{1,0:T(8,128)(2,1)S(1)}, bf16[6,2048]{1,0:T(8,128)(2,1)}, u32[]{:S(2)}) copy-start(bf16[6,2048]{1,0:T(8,128)(2,1)} %convert_bitcast_fusion.2) | copy-start | bytes 73732
  313.7 253.6 %all-reduce.9.cloned.1.call-start = ((), (), s32[]{:S(2)}) async-start(), calls=%async_computation.2 | async-start | bytes 581632 | tf_op jit(solution)/shard_map/psum | solution.py:196
  409.5 10.9 %copy-start.135 = (f32[6]{0:T(128)S(1)}, f32[6]{0:T(128)}, u32[]{:S(2)}) copy-start(f32[6]{0:T(128)} %get-tuple-element.138) | copy-start | bytes 76
  409.5 13.5 %copy-start.117 = (f32[256]{0:T(256)S(1)}, f32[256]{0:T(256)}, u32[]{:S(2)}) copy-start(f32[256]{0:T(256)} %get-tuple-element.126) | copy-start | bytes 3076
  409.5 16.5 %copy-start.114 = (f32[256]{0:T(256)S(1)}, f32[256]{0:T(256)}, u32[]{:S(2)}) copy-start(f32[256]{0:T(256)} %get-tuple-element.128) | copy-start | bytes 3076
  409.6 19.1 %copy-start.136 = (f32[6]{0:T(128)S(1)}, f32[6]{0:T(128)}, u32[]{:S(2)}) copy-start(f32[6]{0:T(128)} %get-tuple-element.130) | copy-start | bytes 76
  409.6 21.7 %copy-start.118 = (f32[256]{0:T(256)S(1)}, f32[256]{0:T(256)}, u32[]{:S(2)}) copy-start(f32[256]{0:T(256)} %get-tuple-element.118) | copy-start | bytes 3076
  411.3 23.0 %copy-start.115 = (f32[256]{0:T(256)S(1)}, f32[256]{0:T(256)}, u32[]{:S(2)}) copy-start(f32[256]{0:T(256)} %get-tuple-element.120) | copy-start | bytes 3076
  411.3 25.6 %copy-start.137 = (f32[6]{0:T(128)S(1)}, f32[6]{0:T(128)}, u32[]{:S(2)}) copy-start(f32[6]{0:T(128)} %get-tuple-element.122) | copy-start | bytes 76
  411.3 26.9 %copy-start.47 = (f32[71942]{0:T(1024)S(1)}, f32[71942]{0:T(1024)}, u32[]{:S(2)}) copy-start(f32[71942]{0:T(1024)} %custom-call) | copy-start | bytes 863308
  411.5 26.8 %copy-start.138 = (f32[6]{0:T(128)S(1)}, f32[6]{0:T(128)}, u32[]{:S(2)}) copy-start(f32[6]{0:T(128)} %get-tuple-element.114) | copy-start | bytes 76
  413.3 26.9 %copy-start.104 = (f32[1,2048]{1,0:T(1,128)S(1)}, f32[1,2048]{1,0:T(1,128)}, u32[]{:S(2)}) copy-start(f32[1,2048]{1,0:T(1,128)} %fusion.112) | copy-start | bytes 24580
  413.3 29.9 %copy-start.105 = (f32[1,2048]{1,0:T(1,128)S(1)}, f32[1,2048]{1,0:T(1,128)}, u32[]{:S(2)}) copy-start(f32[1,2048]{1,0:T(1,128)} %fusion.115) | copy-start | bytes 24580
  413.3 31.7 %copy-start.30 = (f32[72193]{0:T(1024)S(1)}, f32[72193]{0:T(1024)}, u32[]{:S(2)}) copy-start(f32[72193]{0:T(1024)} %get-tuple-element.20) | copy-start | bytes 866320
  417.7 28.3 %copy-start.133 = (f32[2]{0:T(128)S(1)}, f32[2]{0:T(128)}, u32[]{:S(2)}) copy-start(f32[2]{0:T(128)} %compare_select_fusion) | copy-start | bytes 28
  417.7 149.5 %copy-start.25 = (f32[71942]{0:T(1024)S(1)}, f32[71942]{0:T(1024)}, u32[]{:S(2)}) copy-start(f32[71942]{0:T(1024)} %param.26) | copy-start | bytes 863308
  417.7 149.5 %copy-start.27 = (f32[71942]{0:T(1024)S(1)}, f32[71942]{0:T(1024)}, u32[]{:S(2)}) copy-start(f32[71942]{0:T(1024)} %param.20) | copy-start | bytes 863308
  417.7 149.5 %copy-start.45 = (f32[71942]{0:T(1024)S(1)}, f32[71942]{0:T(1024)}, u32[]{:S(2)}) copy-start(f32[71942]{0:T(1024)} %param.21) | copy-start | bytes 863308
  417.7 149.5 %copy-start.46 = (f32[71942]{0:T(1024)S(1)}, f32[71942]{0:T(1024)}, u32[]{:S(2)}) copy-start(f32[71942]{0:T(1024)} %param.22) | copy-start | bytes 863308
  (112 other events, 394.3 us)
Sparse Core Ops, SparseCore 0:
  200.7 109.9 all-reduce.4
  313.8 17.5 all-reduce.6
  440.4 126.8 all-reduce.8
where the time goes:
time: 588 us; the launch traced here: 576 us
  waiting for transfers between devices  197 us (34%)
  matrix products  188 us (32%)
  local copies, waits for them, and re-layouts  79.7 us (14%)
  other arithmetic  49.3 us (8%)
  blocking collectives  40.5 us (7%)
  between operations  20.4 us (3%)
    psum x1, waiting for transfers between devices, on_device(): critic_grad = lax.psum(critic_grad, 'dp')  106 us
    dot_general x52, matrix products, forward(): jnp.dot(weight, moved_low, preferred_element_type=jnp.float32) + bias_term  102 us
    psum x1, waiting for transfers between devices, on_device(): actor_grad = lax.psum(actor_grad, ('dp', 'twin'))  80.2 us
    dot_general x16, matrix products, backward(): jnp.einsum('oi,on->in', weight, grad_low, preferred_element_type=jnp.floa...  49.6 us
    unnamed x352, local copies, waits for them, and re-layouts  45.9 us
    psum x1, blocking collectives, on_device(): loss_pair, actor_loss = lax.psum((critic_vec, -actor_sum), ('dp', 'twin'))  40.5 us
    dot_general x24, matrix products, backward(): jnp.einsum('on,in->oi', grad_low, moved_low, preferred_element_type=jnp.f...  36.7 us
    reduce_sum x4, other arithmetic, backward(): jnp.sum(grad_low.astype(jnp.float32), axis=1)  12.6 us
  transfers between devices with their start and end apart: 7, of which 3 were waited for; matrix products, arithmetic and copies ran while one was open for 19% of the time, Pallas kernels for 0%

commit v1 on v0

v1 whole, which is shorter than its diff:
```python
import jax
import jax.numpy as jnp
from jax import lax
from jax.experimental import pallas as pl
from jax.experimental.pallas import tpu as pltpu
from jax.sharding import PartitionSpec as P

SDIM = 17
ADIM = 6
HID = 256
STEP = 10

DISCOUNT = 0.99
POLYAK_RATE = 0.005
LEARN_RATE = 0.05
BETA_ONE = 0.9
BETA_TWO = 0.999
EPSILON = 1e-08
WEIGHT_DECAY = 0.01
NOISE_SCALE = 0.2
NOISE_CLIP = 0.5

LANES = 128
TILE = 2048
ONES_ROW = 17
ACTION_ROW = 24
IN_ROWS = 32
FLAT_ROWS = 576
HALF_ROWS = FLAT_ROWS // 2
VMEM_BYTES = 56 * 2**20

F32 = jnp.float32
BF16 = jnp.bfloat16


class Net:
    def __init__(self, in_size, out_size):
        self.in_size = in_size
        self.out_size = out_size
        self.bias1 = 2 * in_size
        self.weight2 = self.bias1 + 2
        self.bias2 = self.weight2 + 2 * HID
        self.weight3 = self.bias2 + 2
        self.rows = self.weight3 + 2 * out_size
        self.size = self.rows * LANES + out_size


ACTOR = Net(SDIM, ADIM)
CRITIC = Net(SDIM + ADIM, 1)


def dot(a, b):
    return jnp.dot(a, b, preferred_element_type=F32)


def dot_nt(a, b):
    return lax.dot_general(a, b, (((1,), (1,)), ((), ())), preferred_element_type=F32)


def wide(column, width):
    return jnp.concatenate([column] * (width // LANES), axis=1)


def iota(shape, axis):
    return lax.broadcasted_iota(jnp.int32, shape, axis)


def rows_to_lanes(block):
    return jnp.concatenate([block[row : row + 1] for row in range(block.shape[0])], axis=1)


def place_mask(net):
    shape = (IN_ROWS, LANES * net.in_size)
    position = iota(shape, 1).astype(F32)
    phase = position - net.in_size * jnp.floor((position + 0.5) * (1.0 / net.in_size))
    row = iota(shape, 0)
    source = jnp.where(row < SDIM, row, jnp.where(row >= ACTION_ROW, row - ACTION_ROW + SDIM, -1))
    source = jnp.where(source < net.in_size, source, -1)
    return phase == source.astype(F32)


def place_units(net):
    shape = (LANES * net.in_size, LANES)
    gap = iota(shape, 0) - net.in_size * iota(shape, 1)
    return jnp.where((gap >= 0) & (gap < net.in_size), 1.0, 0.0).astype(BF16)


def three_parts(value):
    high = value.astype(BF16).astype(F32)
    rest = value - high
    middle = rest.astype(BF16).astype(F32)
    return high, middle, rest - middle


def unpack_first(net, flat, mask, units):
    halves = []
    for half in range(2):
        pieces = [
            jnp.broadcast_to(
                flat[half * net.in_size + row : half * net.in_size + row + 1, :],
                (IN_ROWS, LANES),
            )
            for row in range(net.in_size)
        ]
        spread = jnp.where(mask, jnp.concatenate(pieces, axis=1), 0.0).astype(BF16)
        halves.append(dot(spread, units))
    return jnp.concatenate(halves, axis=1)


def flatten_first(net, transposed, out, mask, units):
    for half in range(2):
        block = transposed[:, half * LANES : (half + 1) * LANES]
        parts = jnp.concatenate(three_parts(block), axis=0).astype(BF16)
        spread = dot_nt(parts, units)
        spread = spread[:IN_ROWS] + (spread[IN_ROWS : 2 * IN_ROWS] + spread[2 * IN_ROWS :])
        line = jnp.sum(jnp.where(mask, spread, 0.0), axis=0, keepdims=True)
        for row in range(net.in_size):
            target = half * net.in_size + row
            out[target : target + 1, :] = line[:, row * LANES : (row + 1) * LANES]


def as_column(row):
    return jnp.transpose(jnp.broadcast_to(row, (LANES, HID)))


def flat_row(flat, start):
    return jnp.concatenate([flat[start : start + 1, :], flat[start + 1 : start + 2, :]], axis=1)


class Weights:
    shapes = (
        ((HID, IN_ROWS), BF16),
        ((HID, HID), BF16),
        ((HID, LANES), F32),
        ((16, HID), BF16),
    )
    back_shapes = (
        ((HID, HID), BF16),
        ((HID, LANES), F32),
        ((16, HID), BF16),
        ((HID, 16), BF16),
    )


def scratch_of(shapes):
    return [pltpu.VMEM(shape, dtype) for shape, dtype in shapes]


def unpack_net(net, flat, mask, units, refs, back=None):
    first, second, bias2, third = refs
    first_t = 0.5 * unpack_first(net, flat, mask, units)
    bias1 = three_parts(0.5 * flat_row(flat, net.bias1))
    row = iota((IN_ROWS, HID), 0)
    for part in range(3):
        first_t = jnp.where(row == ONES_ROW + part, bias1[part], first_t)
    first[...] = jnp.transpose(first_t).astype(BF16)
    left = flat[pl.ds(net.weight2, HID, stride=2), :]
    right = flat[pl.ds(net.weight2 + 1, HID, stride=2), :]
    second_value = 0.5 * jnp.concatenate([left, right], axis=1)
    second[...] = second_value.astype(BF16)
    bias2[...] = as_column(0.5 * flat_row(flat, net.bias2))
    left = flat[pl.ds(net.weight3, 8, stride=2), :]
    right = flat[pl.ds(net.weight3 + 1, 8, stride=2), :]
    third_value = jnp.concatenate([left, right], axis=1)
    third_value = jnp.where(iota((8, HID), 0) < net.out_size, third_value, 0.0)
    third_value = jnp.concatenate([third_value, jnp.zeros((8, HID), F32)], axis=0)
    third[...] = third_value.astype(BF16)
    if back is not None:
        second_t, third_column, action_rows, third_t = back
        second_t[...] = jnp.transpose(second_value).astype(BF16)
        third_low = 0.5 * third_value.astype(BF16).astype(F32)
        third_column[...] = as_column(third_low[0:1])
        action_rows[...] = first_t[16:32].astype(BF16)
        third_t[...] = jnp.transpose(third_low).astype(BF16)


def load_flat(net, flat, value):
    flat[0 : net.rows, :] = value.reshape(net.rows, LANES)
    flat[net.rows : FLAT_ROWS, :] = jnp.zeros((FLAT_ROWS - net.rows, LANES), F32)


def body_of(net, ref):
    return ref[pl.ds(0, net.rows * LANES)]


def tail_of(net, ref):
    return ref[pl.ds(net.rows * LANES, net.out_size)].reshape(1, net.out_size)


def tail_column(tail):
    size = tail.shape[1]
    eye = iota((8, size), 0) == iota((8, size), 1)
    return jnp.sum(jnp.where(eye, jnp.broadcast_to(tail, (8, size)), 0.0), axis=1, keepdims=True)


def start_inputs(inputs):
    inputs[...] = jnp.zeros_like(inputs)
    row = iota((8, inputs.shape[1]), 0) + 16
    inputs[16:24, :] = jnp.where((row >= ONES_ROW) & (row < ONES_ROW + 3), 1.0, 0.0)


def silu_low(half_pre):
    wave = jnp.tanh(half_pre)
    return (half_pre * wave + half_pre).astype(BF16)


def silu_and_slope(half_pre):
    wave = jnp.tanh(half_pre)
    above = 1.0 + wave
    return (half_pre * above).astype(BF16), above + half_pre * (1.0 - wave * wave)


def forward(refs, inputs):
    first, second, bias2, third = refs
    width = inputs.shape[1]
    hidden = silu_low(dot(first[...], inputs))
    hidden = silu_low(dot(second[...], hidden) + wide(bias2[...], width))
    return dot(third[...], hidden)[0:8]


def forward_kept(refs, inputs, hidden1):
    first, second, bias2, third = refs
    width = inputs.shape[1]
    low1, slope1 = silu_and_slope(dot(first[...], inputs))
    hidden1[0:HID, :] = low1
    low2, slope2 = silu_and_slope(dot(second[...], low1) + wide(bias2[...], width))
    return dot(third[...], low2)[0:8], slope1, low2, slope2


def write_gradient(net, sums, last_row, flat, mask, units):
    sum1, sum2, sum3 = sums
    flatten_first(net, sum1[...], flat, mask, units)
    bias1 = sum1[ONES_ROW : ONES_ROW + 1, :]
    bias2 = sum2[HID : HID + 1, :]
    weight2 = jnp.transpose(sum2[0:HID, :])
    for side in range(2):
        lanes = slice(side * LANES, (side + 1) * LANES)
        flat[net.bias1 + side : net.bias1 + side + 1, :] = bias1[:, lanes]
        flat[pl.ds(net.weight2 + side, HID, stride=2), :] = weight2[:, lanes]
        flat[net.bias2 + side : net.bias2 + side + 1, :] = bias2[:, lanes]
        for unit in range(net.out_size):
            row = net.weight3 + 2 * unit + side
            flat[row : row + 1, :] = sum3[unit : unit + 1, lanes]
    flat[net.rows : net.rows + 1, :] = last_row
    rest = FLAT_ROWS - net.rows - 1
    flat[net.rows + 1 : FLAT_ROWS, :] = jnp.zeros((rest, LANES), F32)


def split_halves(flat, core, keep, send):
    low = flat[0:HALF_ROWS, :]
    high = flat[HALF_ROWS:FLAT_ROWS, :]
    keep[...] = jnp.where(core == 0, low, high)
    send[...] = jnp.where(core == 0, high, low)


def join_halves(core, mine, other, flat):
    flat[0:HALF_ROWS, :] = jnp.where(core == 0, mine[...], other[...])
    flat[HALF_ROWS:FLAT_ROWS, :] = jnp.where(core == 0, other[...], mine[...])


def adamw_step(weight, gradient, moment_one, moment_two):
    moment_one = BETA_ONE * moment_one + (1.0 - BETA_ONE) * gradient
    moment_two = BETA_TWO * moment_two + (1.0 - BETA_TWO) * gradient * gradient
    corrected_one = moment_one / (1.0 - BETA_ONE**STEP)
    corrected_two = moment_two / (1.0 - BETA_TWO**STEP)
    weight = weight - LEARN_RATE * (
        corrected_one / (jnp.sqrt(corrected_two) + EPSILON) + WEIGHT_DECAY * weight
    )
    return (weight, moment_one, moment_two)


def polyak_mix(lagged, fresh):
    return POLYAK_RATE * fresh + (1.0 - POLYAK_RATE) * lagged


def clear(refs):
    for ref in refs:
        ref[...] = jnp.zeros_like(ref)


SUM_SHAPES = (((IN_ROWS, HID), F32), ((HID + 16, HID), F32), ((16, HID), F32))


def critic_tile(refs, back, bias3, inputs, target, scale, hidden1, sums, tail_sums):
    second_t, third_column = back[0], back[1]
    width = inputs.shape[1]
    out, slope1, low2, slope2 = forward_kept(refs, inputs, hidden1)
    error = out[0:1] + bias3 - target
    grad3_low = (scale * error).astype(BF16)
    grad3 = grad3_low.astype(F32)
    tail_sums[0:1, :] += grad3
    tail_sums[1:2, :] += error * error
    sums[2][...] += dot_nt(jnp.broadcast_to(grad3, (16, width)).astype(BF16), low2)
    grad2 = (wide(third_column[...], width) * grad3 * slope2).astype(BF16)
    sums[1][...] += dot_nt(hidden1[...], grad2)
    grad1 = (dot(second_t[...], grad2) * slope1).astype(BF16)
    sums[0][...] += dot_nt(inputs, grad1)


def critic_last_row(tail_sums):
    totals = jnp.sum(tail_sums[...], axis=1, keepdims=True)
    lane = iota((1, LANES), 1)
    return jnp.where(lane == 0, totals[0:1], jnp.where(lane == 1, totals[1:2], 0.0))


def target_kernel(
    row_total,
    core_ref,
    states,
    actions,
    rewards,
    next_states,
    done_flags,
    smoothing,
    target_actor,
    own_lagged,
    far_lagged,
    own_critic,
    far_critic,
    target_out,
    keep,
    send,
    inputs,
    hidden1,
    tail_sums,
    flat,
    units_actor,
    units_critic,
    *rest,
):
    actor, lag_one, lag_two, critic = rest[0:4], rest[4:8], rest[8:12], rest[12:16]
    back = rest[16:20]
    sums = rest[20:23]
    tails = rest[23]
    core = core_ref[0]
    step = pl.program_id(0)

    @pl.when(step == 0)
    def _():
        start_inputs(inputs)
        hidden1[HID : HID + 16, :] = jnp.ones((16, TILE), BF16)
        clear(sums)
        clear([tail_sums])
        units_actor[...] = place_units(ACTOR)
        units_critic[...] = place_units(CRITIC)
        mask = place_mask(ACTOR)
        load_flat(ACTOR, flat, body_of(ACTOR, target_actor))
        unpack_net(ACTOR, flat, mask, units_actor[...], actor)
        mask = place_mask(CRITIC)
        load_flat(CRITIC, flat, body_of(CRITIC, own_lagged))
        unpack_net(CRITIC, flat, mask, units_critic[...], lag_one)
        load_flat(CRITIC, flat, body_of(CRITIC, far_lagged))
        unpack_net(CRITIC, flat, mask, units_critic[...], lag_two)
        chosen = jnp.where(core == 0, body_of(CRITIC, own_critic), body_of(CRITIC, far_critic))
        load_flat(CRITIC, flat, chosen)
        unpack_net(CRITIC, flat, mask, units_critic[...], critic, back)
        tail = jnp.where(core == 0, tail_of(CRITIC, own_critic), tail_of(CRITIC, far_critic))
        tails[0:8, 0:1] = tail_column(tail_of(ACTOR, target_actor))
        tails[8:16, 0:1] = tail_column(tail_of(CRITIC, own_lagged))
        tails[16:24, 0:1] = tail_column(tail_of(CRITIC, far_lagged))
        tails[24:32, 0:1] = tail_column(tail)

    inputs[0:SDIM, :] = next_states[...]
    lagged_action = jnp.tanh(forward(actor, inputs[...].astype(BF16)) + tails[0:8, 0:1])
    jitter = jnp.clip(NOISE_SCALE * smoothing[...], -NOISE_CLIP, NOISE_CLIP)
    next_action = jnp.clip(lagged_action[0:ADIM] + jitter, -1.0, 1.0)
    inputs[ACTION_ROW : ACTION_ROW + ADIM, :] = next_action
    joined = inputs[...].astype(BF16)
    value_one = forward(lag_one, joined)[0:1] + tails[8:9, 0:1]
    value_two = forward(lag_two, joined)[0:1] + tails[16:17, 0:1]
    keep_going = 1.0 - done_flags[...].astype(F32)
    target = rewards[...] + DISCOUNT * keep_going * jnp.minimum(value_one, value_two)
    target_out[...] = target

    inputs[0:SDIM, :] = states[...]
    inputs[ACTION_ROW : ACTION_ROW + ADIM, :] = actions[...]
    joined = inputs[...].astype(BF16)
    critic_tile(
        critic, back, tails[24:25, 0:1], joined, target, 2.0 / row_total, hidden1, sums, tail_sums
    )

    @pl.when(step == pl.num_programs(0) - 1)
    def _():
        last = critic_last_row(tail_sums)
        write_gradient(CRITIC, sums, last, flat, place_mask(CRITIC), units_critic[...])
        split_halves(flat, core, keep, send)


def critic_kernel(
    row_total,
    core_ref,
    states,
    actions,
    target,
    own_critic,
    far_critic,
    keep,
    send,
    inputs,
    hidden1,
    tail_sums,
    flat,
    units_critic,
    *rest,
):
    critic, back, sums, tails = rest[0:4], rest[4:8], rest[8:11], rest[11]
    core = core_ref[0]
    step = pl.program_id(0)

    @pl.when(step == 0)
    def _():
        start_inputs(inputs)
        hidden1[HID : HID + 16, :] = jnp.ones((16, TILE), BF16)
        clear(sums)
        clear([tail_sums])
        units_critic[...] = place_units(CRITIC)
        chosen = jnp.where(core == 1, body_of(CRITIC, own_critic), body_of(CRITIC, far_critic))
        load_flat(CRITIC, flat, chosen)
        unpack_net(CRITIC, flat, place_mask(CRITIC), units_critic[...], critic, back)
        tail = jnp.where(core == 1, tail_of(CRITIC, own_critic), tail_of(CRITIC, far_critic))
        tails[0:8, 0:1] = tail_column(tail)

    inputs[0:SDIM, :] = states[...]
    inputs[ACTION_ROW : ACTION_ROW + ADIM, :] = actions[...]
    joined = inputs[...].astype(BF16)
    critic_tile(
        critic, back, tails[0:1, 0:1], joined, target[...], 2.0 / row_total, hidden1, sums, tail_sums
    )

    @pl.when(step == pl.num_programs(0) - 1)
    def _():
        last = critic_last_row(tail_sums)
        write_gradient(CRITIC, sums, last, flat, place_mask(CRITIC), units_critic[...])
        split_halves(flat, core, keep, send)


def actor_kernel(
    row_total,
    core_ref,
    states,
    actor_weights,
    mine,
    other,
    own_critic,
    far_critic,
    own_first,
    far_first,
    own_second,
    far_second,
    keep,
    send,
    inputs,
    hidden1,
    tail_sums,
    flat,
    gradient,
    units_actor,
    units_critic,
    *rest,
):
    actor, actor_back = rest[0:4], rest[4:8]
    judge, judge_back = rest[8:12], rest[12:16]
    sums, tails = rest[16:19], rest[19]
    core = core_ref[0]
    step = pl.program_id(0)

    @pl.when(step == 0)
    def _():
        start_inputs(inputs)
        hidden1[HID : HID + 16, :] = jnp.ones((16, TILE), BF16)
        clear(sums)
        clear([tail_sums])
        units_actor[...] = place_units(ACTOR)
        units_critic[...] = place_units(CRITIC)
        load_flat(ACTOR, flat, body_of(ACTOR, actor_weights))
        unpack_net(ACTOR, flat, place_mask(ACTOR), units_actor[...], actor, actor_back)
        tails[0:8, 0:1] = tail_column(tail_of(ACTOR, actor_weights))
        join_halves(core, mine, other, gradient)

        def chosen(part, own, far):
            return jnp.where(core == 0, part(CRITIC, own), part(CRITIC, far))

        def fresh(part, grad):
            return adamw_step(
                chosen(part, own_critic, far_critic),
                grad,
                chosen(part, own_first, far_first),
                chosen(part, own_second, far_second),
            )[0]

        body = gradient[0 : CRITIC.rows, :].reshape(CRITIC.rows * LANES)
        load_flat(CRITIC, flat, fresh(body_of, body))
        unpack_net(CRITIC, flat, place_mask(CRITIC), units_critic[...], judge, judge_back)
        tail = fresh(tail_of, gradient[CRITIC.rows : CRITIC.rows + 1, 0:1])
        tails[8:16, 0:1] = tail_column(tail)

    inputs[0:SDIM, :] = states[...]
    state_low = inputs[...].astype(BF16)
    out, slope1, low2, slope2 = forward_kept(actor, state_low, hidden1)
    action = jnp.tanh(out + tails[0:8, 0:1])
    inputs[ACTION_ROW:IN_ROWS, :] = action
    joined = inputs[...].astype(BF16)
    first, second, bias2, third = judge
    judge_low, judge_slope1 = silu_and_slope(dot(first[...], joined))
    judge_low, judge_slope2 = silu_and_slope(dot(second[...], judge_low) + wide(bias2[...], TILE))
    value = dot(third[...], judge_low)[0:1] + tails[8:9, 0:1]
    tail_sums[8:9, :] += value
    start = jnp.full((HID, LANES), -1.0 / row_total, F32).astype(BF16).astype(F32)
    judge_second_t, judge_column, judge_rows, unused = judge_back
    grad2 = (wide(judge_column[...] * start, TILE) * judge_slope2).astype(BF16)
    grad1 = (dot(judge_second_t[...], grad2) * judge_slope1).astype(BF16)
    grad_action = 2.0 * dot(judge_rows[...], grad1)[8:16]
    grad3 = (grad_action * (1.0 - action * action)).astype(BF16).astype(F32)
    tail_sums[0:8, :] += grad3
    grad3_low = jnp.concatenate([grad3, jnp.zeros_like(grad3)], axis=0).astype(BF16)
    actor_second_t, unused, unused, actor_third_t = actor_back
    sums[2][...] += dot_nt(grad3_low, low2)
    grad2 = (dot(actor_third_t[...], grad3_low) * slope2).astype(BF16)
    sums[1][...] += dot_nt(hidden1[...], grad2)
    grad1 = (dot(actor_second_t[...], grad2) * slope1).astype(BF16)
    sums[0][...] += dot_nt(state_low, grad1)

    @pl.when(step == pl.num_programs(0) - 1)
    def _():
        totals = jnp.sum(tail_sums[...], axis=1, keepdims=True)
        lane = iota((8, LANES), 1)
        biases = jnp.where(lane == iota((8, LANES), 0), totals[0:8], 0.0)
        last = jnp.sum(biases, axis=0, keepdims=True)
        last = jnp.where(iota((1, LANES), 1) == 8, -totals[8:9], last)
        write_gradient(ACTOR, sums, last, flat, place_mask(ACTOR), units_actor[...])
        split_halves(flat, core, keep, send)


def step_kernel(
    core_ref,
    actor_mine,
    actor_other,
    one_mine,
    one_other,
    two_mine,
    two_other,
    actor_weights,
    actor_first,
    actor_second,
    target_actor,
    critic_weights,
    critic_first,
    critic_second,
    target_critic,
    new_actor,
    new_actor_first,
    new_actor_second,
    new_target_actor,
    new_critic,
    new_critic_first,
    new_critic_second,
    new_target_critic,
    losses,
    gradient,
    second_gradient,
):
    core = core_ref[0]

    def update(net, grad_ref, sources, outs):
        for part, where, grad in (
            (body_of, pl.ds(0, net.rows * LANES), grad_ref[0 : net.rows, :]),
            (
                tail_of,
                pl.ds(net.rows * LANES, net.out_size),
                grad_ref[net.rows : net.rows + 1, 0 : net.out_size],
            ),
        ):
            weight, first, second, lagged = [part(net, source) for source in sources]
            grad = grad.reshape(weight.shape)
            fresh, first, second = adamw_step(weight, grad, first, second)
            results = (fresh, first, second, polyak_mix(lagged, fresh))
            for out, result in zip(outs, results):
                out[where] = result.reshape(result.size)

    join_halves(core, actor_mine, actor_other, gradient)
    update(
        ACTOR,
        gradient,
        (actor_weights, actor_first, actor_second, target_actor),
        (new_actor, new_actor_first, new_actor_second, new_target_actor),
    )
    lane = iota((1, LANES), 1)
    actor_row = jnp.where(lane == 8, gradient[ACTOR.rows : ACTOR.rows + 1, :], 0.0)
    actor_loss = jnp.sum(actor_row, axis=1, keepdims=True)
    join_halves(core, one_mine, one_other, gradient)
    join_halves(core, two_mine, two_other, second_gradient)
    gradient[...] = jnp.where(core == 0, gradient[...], second_gradient[...])
    update(
        CRITIC,
        gradient,
        (critic_weights, critic_first, critic_second, target_critic),
        (new_critic, new_critic_first, new_critic_second, new_target_critic),
    )
    critic_row = jnp.where(lane == 1, gradient[CRITIC.rows : CRITIC.rows + 1, :], 0.0)
    critic_loss = jnp.sum(critic_row, axis=1, keepdims=True)
    losses[...] = jnp.where(lane == 0, critic_loss, jnp.where(lane == 1, actor_loss, 0.0))


def twin_swap(value):
    return lax.ppermute(value, "twin", [(0, 1), (1, 0)])


def sum_over_chips(value):
    size = lax.axis_size("dp")
    mask = 1
    while mask < size:
        pairs = [(source, source ^ mask) for source in range(size)]
        value = value + lax.ppermute(value, "dp", pairs)
        mask *= 2
    return value


def sum_halves(keep, send):
    mine = sum_over_chips(keep + twin_swap(send))
    return mine, twin_swap(mine)


def whole(shape):
    return pl.BlockSpec(shape, lambda *unused: (0,) * len(shape))


def on_device(
    states,
    actions,
    rewards,
    next_states,
    done_flags,
    smoothing,
    actor_weights,
    actor_first,
    actor_second,
    critic_weights,
    critic_first,
    critic_second,
    target_actor,
    target_critic,
):
    core = lax.axis_index("twin").astype(jnp.int32).reshape(1)
    local_rows = states.shape[1]
    tiles = local_rows // 2 // TILE
    row_total = local_rows * lax.axis_size("dp")
    rewards = rewards.reshape(1, local_rows)
    done_flags = done_flags.reshape(1, local_rows)
    critic_weights = critic_weights.reshape(-1)
    critic_first = critic_first.reshape(-1)
    critic_second = critic_second.reshape(-1)
    target_critic = target_critic.reshape(-1)
    far_weights = twin_swap(critic_weights)
    far_lagged = twin_swap(target_critic)
    far_first = twin_swap(critic_first)
    far_second = twin_swap(critic_second)

    def mine(rows):
        return pl.BlockSpec((rows, TILE), lambda i, core_ref: (0, core_ref[0] * tiles + i))

    def local(rows):
        return pl.BlockSpec((rows, TILE), lambda i, core_ref: (0, i))

    actor_flat = whole((ACTOR.size,))
    critic_flat = whole((CRITIC.size,))
    half = whole((HALF_ROWS, LANES))
    half_shape = jax.ShapeDtypeStruct((HALF_ROWS, LANES), F32)
    common = [
        pltpu.VMEM((IN_ROWS, TILE), F32),
        pltpu.VMEM((HID + 16, TILE), BF16),
        pltpu.VMEM((16, TILE), F32),
        pltpu.VMEM((FLAT_ROWS + 8, LANES), F32),
    ]
    units_actor = pltpu.VMEM((LANES * ACTOR.in_size, LANES), BF16)
    units_critic = pltpu.VMEM((LANES * CRITIC.in_size, LANES), BF16)
    net = scratch_of(Weights.shapes)
    back = scratch_of(Weights.back_shapes)
    sums = scratch_of(SUM_SHAPES)
    tails = pltpu.VMEM((32, LANES), F32)
    params = pltpu.CompilerParams(vmem_limit_bytes=VMEM_BYTES)

    def call(kernel, in_specs, out_specs, out_shape, scratch, name):
        return pl.pallas_call(
            kernel,
            grid_spec=pltpu.PrefetchScalarGridSpec(
                num_scalar_prefetch=1,
                grid=(tiles,),
                in_specs=in_specs,
                out_specs=out_specs,
                scratch_shapes=scratch,
            ),
            out_shape=out_shape,
            compiler_params=params,
            name=name,
        )

    target, keep_one, send_one = call(
        lambda *refs: target_kernel(row_total, *refs),
        [mine(SDIM), mine(ADIM), mine(1), mine(SDIM), mine(1), mine(ADIM), actor_flat]
        + [critic_flat] * 4,
        [local(1), half, half],
        [jax.ShapeDtypeStruct((1, local_rows // 2), F32), half_shape, half_shape],
        common + [units_actor, units_critic] + net * 4 + back + sums + [tails],
        "target_and_first_critic",
    )(
        core,
        states,
        actions,
        rewards,
        next_states,
        done_flags,
        smoothing,
        target_actor,
        target_critic,
        far_lagged,
        critic_weights,
        far_weights,
    )
    keep_two, send_two = call(
        lambda *refs: critic_kernel(row_total, *refs),
        [mine(SDIM), mine(ADIM), local(1), critic_flat, critic_flat],
        [half, half],
        [half_shape, half_shape],
        common + [units_critic] + net + back + sums + [tails],
        "second_critic",
    )(core, states, actions, target, critic_weights, far_weights)
    one_mine, one_other = sum_halves(keep_one, send_one)
    keep_actor, send_actor = call(
        lambda *refs: actor_kernel(row_total, *refs),
        [mine(SDIM), actor_flat, half, half] + [critic_flat] * 6,
        [half, half],
        [half_shape, half_shape],
        common
        + [pltpu.VMEM((FLAT_ROWS, LANES), F32), units_actor, units_critic]
        + (net + back) * 2
        + sums
        + [tails],
        "actor",
    )(
        core,
        states,
        actor_weights,
        one_mine,
        one_other,
        critic_weights,
        far_weights,
        critic_first,
        far_first,
        critic_second,
        far_second,
    )
    both_mine, both_other = sum_halves(
        jnp.stack([keep_actor, keep_two]), jnp.stack([send_actor, send_two])
    )
    actor_mine, two_mine = both_mine[0], both_mine[1]
    actor_other, two_other = both_other[0], both_other[1]
    vector = pl.BlockSpec(memory_space=pltpu.VMEM)
    scalar = pl.BlockSpec(memory_space=pltpu.SMEM)
    actor_out = jax.ShapeDtypeStruct((ACTOR.size,), F32)
    critic_out = jax.ShapeDtypeStruct((CRITIC.size,), F32)
    results = pl.pallas_call(
        step_kernel,
        in_specs=[scalar] + [vector] * 14,
        out_specs=[vector] * 9,
        out_shape=[actor_out] * 4
        + [critic_out] * 4
        + [jax.ShapeDtypeStruct((1, LANES), F32)],
        scratch_shapes=[pltpu.VMEM((FLAT_ROWS, LANES), F32)] * 2,
        compiler_params=params,
        name="step",
    )(
        core,
        actor_mine,
        actor_other,
        one_mine,
        one_other,
        two_mine,
        two_other,
        actor_weights,
        actor_first,
        actor_second,
        target_actor,
        critic_weights,
        critic_first,
        critic_second,
        target_critic,
    )
    new_actor, new_actor_first, new_actor_second, new_target_actor = results[0:4]
    new_critic, new_critic_first, new_critic_second, new_target_critic = [
        result.reshape(1, -1) for result in results[4:8]
    ]
    losses = results[8]
    return (
        new_actor,
        new_actor_first,
        new_actor_second,
        new_critic,
        new_critic_first,
        new_critic_second,
        new_target_actor,
        new_target_critic,
        losses[0, 0:1],
        losses[0, 1],
    )


def solution(mesh):
    columns = P(None, "dp")
    critic = P("twin", None)
    return jax.shard_map(
        on_device,
        mesh=mesh,
        in_specs=(
            columns,
            columns,
            P("dp"),
            columns,
            P("dp"),
            columns,
            P(),
            P(),
            P(),
            critic,
            critic,
            critic,
            P(),
            critic,
        ),
        out_specs=(P(), P(), P(), critic, critic, critic, P(), critic, P("twin"), P()),
        check_vma=False,
    )
```

time: 588 us -> 157 us (0.27); the launches traced: 576 us -> 157 us
  matrix products: 188 us -> 0 us
  waiting for transfers between devices: 197 us -> 52.5 us
  local copies, waits for them, and re-layouts: 79.7 us -> 11.5 us
  Pallas kernels: 0 us -> 66.7 us
  other arithmetic: 49.3 us -> 7.81 us
  blocking collectives: 40.5 us -> 0 us
  between operations: 20.4 us -> 0.87 us
  starting transfers between devices: 1.15 us -> 17.1 us
    psum x3 -> x0, waiting for transfers between devices: 197 us -> none  [the longest x1 106 us: on_device(): critic_grad = lax.psum(critic_grad, 'dp')]
    dot_general x92 -> x0, matrix products: 188 us -> none  [the longest x52 102 us: forward(): jnp.dot(weight, moved_low, preferred_element_type=jnp.float32) + bias_term]
    pallas_call x0 -> x4, Pallas kernels: none -> 66.7 us  [the longest x1 25.9 us: on_device(): call(lambda *refs: target_kernel(row_total, *refs), [mine(SDIM), mine(ADI...]
    ppermute x4 -> x16, waiting for transfers between devices: 0.01 us -> 52.5 us  [the longest x8 47.4 us: sum_over_chips(): value = value + lax.ppermute(value, 'dp', pairs)]
    unnamed x352 -> x32, local copies, waits for them, and re-layouts: 45.9 us -> 2.18 us
    psum x1 -> x0, blocking collectives: 40.5 us -> none  [on_device(): loss_pair, actor_loss = lax.psum((critic_vec, -actor_sum), ('dp', 'twin'))]
    reduce_sum x10 -> x0, other arithmetic: 22.7 us -> none  [the longest x4 12.6 us: backward(): jnp.sum(grad_low.astype(jnp.float32), axis=1)]
    ppermute x4 -> x16, starting transfers between devices: 1.02 us -> 17.1 us  [the longest x8 15.1 us: sum_over_chips(): value = value + lax.ppermute(value, 'dp', pairs)]
  transfers between devices with their start and end apart: 7 -> 16, of which waited for: 3 -> 12; matrix products, arithmetic and copies ran while one was open for 19% -> 2% of each run, Pallas kernels for 0% -> 9%
where the time goes in v1:
time: 157 us
  Pallas kernels  66.7 us (42%)
  waiting for transfers between devices  52.5 us (33%)
  starting transfers between devices  17.1 us (11%)
  local copies, waits for them, and re-layouts  11.5 us (7%)
  other arithmetic  7.81 us (5%)
    ppermute x8, waiting for transfers between devices, sum_over_chips(): value = value + lax.ppermute(value, 'dp', pairs)  47.4 us
    pallas_call x1, Pallas kernels, on_device(): call(lambda *refs: target_kernel(row_total, *refs), [mine(SDIM), mine(ADI...  25.9 us
    pallas_call x1, Pallas kernels, on_device(): call(lambda *refs: actor_kernel(row_total, *refs), [mine(SDIM), actor_fla...  22.3 us
    ppermute x8, starting transfers between devices, sum_over_chips(): value = value + lax.ppermute(value, 'dp', pairs)  15.1 us
    pallas_call x1, Pallas kernels, on_device(): call(lambda *refs: critic_kernel(row_total, *refs), [mine(SDIM), mine(ADI...  14.6 us
    reshape x4, local copies, waits for them, and re-layouts, on_device(): result.reshape(1, -1)  6.52 us
    ppermute x8, waiting for transfers between devices, twin_swap(): return lax.ppermute(value, 'twin', [(0, 1), (1, 0)])  5.1 us
    unnamed x4, other arithmetic  4.71 us
  transfers between devices with their start and end apart: 16, of which 12 were waited for; matrix products, arithmetic and copies ran while one was open for 2% of the time, Pallas kernels for 9%

profile of v1, /device:TPU:0, one launch (start us, length us, event | category | flops | bytes accessed | tf_op | source)
XLA Modules:
  0.0 156.5 jit_solution(12030501589518029395)
XLA Ops:
  0.6 1.7 %reduce.refs_8_.target_critic = f32[72193]{0:T(1024)S(1)} reduce(f32[1,72193]{1,0:T(1,128)} %param.27, f32[]{:T(128)} %constant.8), dimensions={0}, to_apply=%param.27.reduce_sub_computation | reduce | bytes 577548 | tf_op args[13]
  2.3 0.5 collective-permute-start
  2.8 1.6 %reduce.1.refs_10_.refs_5_.refs_4_.critic_weights = f32[72193]{0:T(1024)S(1)} reduce(f32[1,72193]{1,0:T(1,128)} %param.23, f32[]{:T(128)} %constant.8), dimensions={0}, to_apply=%param.23.reduce_sub_computation | reduce | bytes 577548 | tf_op args[9]
  4.5 0.1 collective-permute-start.1
  4.6 1.5 collective-permute-done.1.refs_11_.refs_6_.refs_5_
  6.2 0.7 copy-done.3
  6.9 25.9 %target_and_first_critic.1 = (f32[1,8192]{1,0:T(1,128)}, f32[288,128]{1,0:T(8,128)}, f32[288,128]{1,0:T(8,128)}) custom-call(s32[1]{0:T(128)} %bitcast.refs_0_.core_ref, f32[17,16384]{1,0:T(8,128)} %refs_1_.5, f32[6,16384]{1,0:T(8,128)} %refs_2_.5, f32[1,16384]{1,0:T(1,128)} %bitcast.23, f32[17,16384]{1,0:T(8,128)} %refs_4_.1, s32[1,16384]{1,0:T(1,128)} %bitcast.24, ...), custom_call_target="tpu_custom_call" | custom-call | tf_op jit(solution)/shard_map/target_and_first_critic/pallas_call | solution.py:697
  32.8 0.2 collective-permute-start.2
  33.0 1.4 collective-permute-done.2
  34.4 0.9 add.30
  35.4 2.7 %collective-permute-start.3 = (f32[288,128]{1,0:T(8,128)S(1)}, f32[288,128]{1,0:T(8,128)S(1)}, u32[]{:S(2)}, u32[]{:S(2)}) collective-permute-start(f32[288,128]{1,0:T(8,128)S(1)} %add.30), channel_id=1, source_target_pairs={{0,2},{2,0},{4,6},{6,4},{8,10},{10,8},{12,14},{14,12},{16,18},{18,... | collective-permute-start | bytes 442376 | tf_op jit(solution)/shard_map/ppermute | solution.py:613
  38.1 4.4 %collective-permute-done.3 = f32[288,128]{1,0:T(8,128)S(1)} collective-permute-done((f32[288,128]{1,0:T(8,128)S(1)}, f32[288,128]{1,0:T(8,128)S(1)}, u32[]{:S(2)}, u32[]{:S(2)}) %collective-permute-start.3) | collective-permute-done | bytes 147488 | tf_op jit(solution)/shard_map/ppermute | solution.py:613
  42.5 1.8 %collective-permute-start.4 = (f32[288,128]{1,0:T(8,128)S(1)}, f32[288,128]{1,0:T(8,128)S(1)}, u32[]{:S(2)}, u32[]{:S(2)}) collective-permute-start(f32[288,128]{1,0:T(8,128)S(1)} %add.31), channel_id=1, source_target_pairs={{0,4},{2,6},{4,0},{6,2},{8,12},{10,14},{12,8},{14,10},{16,20},{18,... | collective-permute-start | bytes 442376 | tf_op jit(solution)/shard_map/ppermute | solution.py:613
  44.3 3.8 %collective-permute-done.4 = f32[288,128]{1,0:T(8,128)S(1)} collective-permute-done((f32[288,128]{1,0:T(8,128)S(1)}, f32[288,128]{1,0:T(8,128)S(1)}, u32[]{:S(2)}, u32[]{:S(2)}) %collective-permute-start.4) | collective-permute-done | bytes 147488 | tf_op jit(solution)/shard_map/ppermute | solution.py:613
  48.1 1.6 %collective-permute-start.5 = (f32[288,128]{1,0:T(8,128)S(1)}, f32[288,128]{1,0:T(8,128)S(1)}, u32[]{:S(2)}, u32[]{:S(2)}) collective-permute-start(f32[288,128]{1,0:T(8,128)S(1)} %add.32), channel_id=1, source_target_pairs={{0,8},{2,10},{4,12},{6,14},{8,0},{10,2},{12,4},{14,6},{16,24},{18,... | collective-permute-start | bytes 442376 | tf_op jit(solution)/shard_map/ppermute | solution.py:613
  49.7 3.6 %collective-permute-done.5 = f32[288,128]{1,0:T(8,128)S(1)} collective-permute-done((f32[288,128]{1,0:T(8,128)S(1)}, f32[288,128]{1,0:T(8,128)S(1)}, u32[]{:S(2)}, u32[]{:S(2)}) %collective-permute-start.5) | collective-permute-done | bytes 147488 | tf_op jit(solution)/shard_map/ppermute | solution.py:613
  53.3 2.7 %collective-permute-start.6 = (f32[288,128]{1,0:T(8,128)S(1)}, f32[288,128]{1,0:T(8,128)S(1)}, u32[]{:S(2)}, u32[]{:S(2)}) collective-permute-start(f32[288,128]{1,0:T(8,128)S(1)} %add.33), channel_id=1, source_target_pairs={{0,16},{2,18},{4,20},{6,22},{8,24},{10,26},{12,28},{14,30},{16,0},... | collective-permute-start | bytes 442376 | tf_op jit(solution)/shard_map/ppermute | solution.py:613
  56.0 0.7 reduce.3.refs_9_.critic_second
  56.7 0.1 collective-permute-start.9
  56.8 0.7 reduce.2.refs_7_.critic_first
  57.5 0.6 collective-permute-start.8
  58.1 3.0 %collective-permute-done.6 = f32[288,128]{1,0:T(8,128)S(1)} collective-permute-done((f32[288,128]{1,0:T(8,128)S(1)}, f32[288,128]{1,0:T(8,128)S(1)}, u32[]{:S(2)}, u32[]{:S(2)}) %collective-permute-start.6) | collective-permute-done | bytes 147488 | tf_op jit(solution)/shard_map/ppermute | solution.py:613
  61.1 14.6 %second_critic.1 = (f32[288,128]{1,0:T(8,128)}, f32[288,128]{1,0:T(8,128)}) custom-call(s32[1]{0:T(128)} %bitcast.refs_0_.core_ref, f32[17,16384]{1,0:T(8,128)} %refs_1_.5, f32[6,16384]{1,0:T(8,128)} %refs_2_.5, f32[1,8192]{1,0:T(1,128)} %get-tuple-element.29.refs_3_, f32[72193]{0:T(1024)} %copy-done, f32[72193]{0:T(1024)} %copy-done.3), custom_call_target="tpu_custom_call" | custom-call | tf_op jit(solution)/shard_map/second_critic/pallas_call | solution.py:719
  75.8 0.7 copy-done.9
  76.5 0.1 copy-done.10
  76.6 0.7 copy-done.8
  77.2 22.3 %actor.1 = (f32[288,128]{1,0:T(8,128)}, f32[288,128]{1,0:T(8,128)}) custom-call(s32[1]{0:T(128)} %bitcast.refs_0_.core_ref, f32[17,16384]{1,0:T(8,128)} %refs_1_.5, f32[71942]{0:T(1024)} %actor_weights.1, f32[288,128]{1,0:T(8,128)} %copy-done.5, f32[288,128]{1,0:T(8,128)} %copy-done.8, f32[72193]{0:T(1024)} %copy-done, f32[72193]{0:T(1024)} %copy-done.3, ...), custom_call_target="tpu_custom_call" | custom-call | tf_op jit(solution)/shard_map/actor/pallas_call | solution.py:728
  99.6 1.0 pad_maximum_fusion
  100.6 0.3 collective-permute-start.10
  100.9 1.3 collective-permute-done.10
  102.2 1.0 maximum_add_fusion
  103.2 1.6 collective-permute-start.11
  104.7 7.7 %collective-permute-done.11 = f32[2,288,128]{2,1,0:T(8,128)S(1)} collective-permute-done((f32[2,288,128]{2,1,0:T(8,128)S(1)}, f32[2,288,128]{2,1,0:T(8,128)S(1)}, u32[]{:S(2)}, u32[]{:S(2)}) %collective-permute-start.11) | collective-permute-done | bytes 294944 | tf_op jit(solution)/shard_map/ppermute | solution.py:613
  112.5 1.6 %collective-permute-start.12 = (f32[2,288,128]{2,1,0:T(8,128)S(1)}, f32[2,288,128]{2,1,0:T(8,128)S(1)}, u32[]{:S(2)}, u32[]{:S(2)}) collective-permute-start(f32[2,288,128]{2,1,0:T(8,128)S(1)} %fusion.1), channel_id=1, source_target_pairs={{0,4},{2,6},{4,0},{6,2},{8,12},{10,14},{12,8},{14,10},{16,20},{18,... | collective-permute-start | bytes 884744 | tf_op jit(solution)/shard_map/ppermute | solution.py:613
  114.1 6.9 %collective-permute-done.12 = f32[2,288,128]{2,1,0:T(8,128)S(1)} collective-permute-done((f32[2,288,128]{2,1,0:T(8,128)S(1)}, f32[2,288,128]{2,1,0:T(8,128)S(1)}, u32[]{:S(2)}, u32[]{:S(2)}) %collective-permute-start.12) | collective-permute-done | bytes 294944 | tf_op jit(solution)/shard_map/ppermute | solution.py:613
  121.0 0.8 collective-permute-start.13
  121.7 6.8 %collective-permute-done.13 = f32[2,288,128]{2,1,0:T(8,128)S(1)} collective-permute-done((f32[2,288,128]{2,1,0:T(8,128)S(1)}, f32[2,288,128]{2,1,0:T(8,128)S(1)}, u32[]{:S(2)}, u32[]{:S(2)}) %collective-permute-start.13) | collective-permute-done | bytes 294944 | tf_op jit(solution)/shard_map/ppermute | solution.py:613
  128.5 2.4 %collective-permute-start.14 = (f32[2,288,128]{2,1,0:T(8,128)S(1)}, f32[2,288,128]{2,1,0:T(8,128)S(1)}, u32[]{:S(2)}, u32[]{:S(2)}) collective-permute-start(f32[2,288,128]{2,1,0:T(8,128)S(1)} %add.38), channel_id=1, source_target_pairs={{0,16},{2,18},{4,20},{6,22},{8,24},{10,26},{12,28},{14,30},{16,0},... | collective-permute-start | bytes 884744 | tf_op jit(solution)/shard_map/ppermute | solution.py:613
  130.9 11.4 %collective-permute-done.14 = f32[2,288,128]{2,1,0:T(8,128)S(1)} collective-permute-done((f32[2,288,128]{2,1,0:T(8,128)S(1)}, f32[2,288,128]{2,1,0:T(8,128)S(1)}, u32[]{:S(2)}, u32[]{:S(2)}) %collective-permute-start.14) | collective-permute-done | bytes 294944 | tf_op jit(solution)/shard_map/ppermute | solution.py:613
  142.5 0.7 slice_bitcast_fusion.1
  143.2 0.8 collective-permute-done.15
  144.0 0.7 slice_bitcast_fusion
  144.8 3.9 %step.1 = (f32[71942]{0:T(1024)}, f32[71942]{0:T(1024)}, f32[71942]{0:T(1024)}, f32[71942]{0:T(1024)}, f32[72193]{0:T(1024)}, /*index=5*/f32[72193]{0:T(1024)}, ...) custom-call(s32[1]{0:T(128)} %bitcast.refs_0_.core_ref, f32[288,128]{1,0:T(8,128)} %get-tuple-element.45.actor_mine, ...), custom_call_target="tpu_custom_call" | custom-call | tf_op jit(solution)/shard_map/step/pallas_call | solution.py:761
  148.6 1.3 fusion
  150.0 1.9 %reshape.60 = f32[1,72193]{1,0:T(1,128)} reshape(f32[72193]{0:T(1024)} %get-tuple-element.36) | data formatting | bytes 577544 | tf_op jit(solution)/shard_map/reshape | solution.py:790
  151.9 1.9 %reshape.61 = f32[1,72193]{1,0:T(1,128)} reshape(f32[72193]{0:T(1024)} %get-tuple-element.37) | data formatting | bytes 577544 | tf_op jit(solution)/shard_map/reshape | solution.py:790
  153.7 1.9 %reshape.62 = f32[1,72193]{1,0:T(1,128)} reshape(f32[72193]{0:T(1024)} %get-tuple-element.38) | data formatting | bytes 577544 | tf_op jit(solution)/shard_map/reshape | solution.py:790
  155.6 0.9 reshape.63
  (42 shorter events, 0.5 us)
Async XLA Ops:
  2.3 3.8 %copy-start.4 = (f32[72193]{0:T(1024)}, f32[72193]{0:T(1024)S(1)}, u32[]{:S(2)}) copy-start(f32[72193]{0:T(1024)S(1)} %reduce.refs_8_.target_critic) | copy-start | bytes 866320
  2.3 2.3 %collective-permute-start = (f32[72193]{0:T(1024)S(1)}, f32[72193]{0:T(1024)S(1)}, u32[]{:S(2)}, u32[]{:S(2)}) collective-permute-start(f32[72193]{0:T(1024)S(1)} %reduce.refs_8_.target_critic), channel_id=1, source_target_pairs={{0,1},{1,0},{2,3},{3,2},{4,5},{5,4},{6,7},{7,6},{8,9},{9,8},{10,11... | collective-permute-start | bytes 866324 | tf_op jit(solution)/shard_map/ppermute | solution.py:605
  4.5 1.7 %copy-start = (f32[72193]{0:T(1024)}, f32[72193]{0:T(1024)S(1)}, u32[]{:S(2)}) copy-start(f32[72193]{0:T(1024)S(1)} %reduce.1.refs_10_.refs_5_.refs_4_.critic_weights) | copy-start | bytes 866320
  4.5 1.6 %collective-permute-start.1 = (f32[72193]{0:T(1024)S(1)}, f32[72193]{0:T(1024)S(1)}, u32[]{:S(2)}, u32[]{:S(2)}) collective-permute-start(f32[72193]{0:T(1024)S(1)} %reduce.1.refs_10_.refs_5_.refs_4_.critic_weights), channel_id=1, source_target_pairs={{0,1},{1,0},{2,3},{3,2},{4,5},{5,4},{6,7},{7,6},{8,9},{9,8},{10,11... | collective-permute-start | bytes 866324 | tf_op jit(solution)/shard_map/ppermute | solution.py:605
  4.6 1.5 copy-start.12
  6.1 0.7 copy-start.3
  32.8 23.2 %copy-start.13 = (f32[1,72193]{1,0:T(1,128)S(1)}, f32[1,72193]{1,0:T(1,128)}, u32[]{:S(2)}) copy-start(f32[1,72193]{1,0:T(1,128)} %param.25) | copy-start | bytes 866320
  32.8 24.0 %copy-start.14 = (f32[1,72193]{1,0:T(1,128)S(1)}, f32[1,72193]{1,0:T(1,128)}, u32[]{:S(2)}) copy-start(f32[1,72193]{1,0:T(1,128)} %param.24) | copy-start | bytes 866320
  32.8 1.6 %collective-permute-start.2 = (f32[288,128]{1,0:T(8,128)}, f32[288,128]{1,0:T(8,128)S(1)}, u32[]{:S(2)}, u32[]{:S(2)}) collective-permute-start(f32[288,128]{1,0:T(8,128)} %get-tuple-element.27), channel_id=1, source_target_pairs={{0,1},{1,0},{2,3},{3,2},{4,5},{5,4},{6,7},{7,6},{8,9},{9,8},{10,11... | collective-permute-start | bytes 442376 | tf_op jit(solution)/shard_map/ppermute | solution.py:605
  35.4 7.1 %collective-permute-start.3 = (f32[288,128]{1,0:T(8,128)S(1)}, f32[288,128]{1,0:T(8,128)S(1)}, u32[]{:S(2)}, u32[]{:S(2)}) collective-permute-start(f32[288,128]{1,0:T(8,128)S(1)} %add.30), channel_id=1, source_target_pairs={{0,2},{2,0},{4,6},{6,4},{8,10},{10,8},{12,14},{14,12},{16,18},{18,... | collective-permute-start | bytes 442376 | tf_op jit(solution)/shard_map/ppermute | solution.py:613
  42.5 5.6 %collective-permute-start.4 = (f32[288,128]{1,0:T(8,128)S(1)}, f32[288,128]{1,0:T(8,128)S(1)}, u32[]{:S(2)}, u32[]{:S(2)}) collective-permute-start(f32[288,128]{1,0:T(8,128)S(1)} %add.31), channel_id=1, source_target_pairs={{0,4},{2,6},{4,0},{6,2},{8,12},{10,14},{12,8},{14,10},{16,20},{18,... | collective-permute-start | bytes 442376 | tf_op jit(solution)/shard_map/ppermute | solution.py:613
  48.1 5.2 %collective-permute-start.5 = (f32[288,128]{1,0:T(8,128)S(1)}, f32[288,128]{1,0:T(8,128)S(1)}, u32[]{:S(2)}, u32[]{:S(2)}) collective-permute-start(f32[288,128]{1,0:T(8,128)S(1)} %add.32), channel_id=1, source_target_pairs={{0,8},{2,10},{4,12},{6,14},{8,0},{10,2},{12,4},{14,6},{16,24},{18,... | collective-permute-start | bytes 442376 | tf_op jit(solution)/shard_map/ppermute | solution.py:613
  53.3 7.7 %collective-permute-start.6 = (f32[288,128]{1,0:T(8,128)S(1)}, f32[288,128]{1,0:T(8,128)S(1)}, u32[]{:S(2)}, u32[]{:S(2)}) collective-permute-start(f32[288,128]{1,0:T(8,128)S(1)} %add.33), channel_id=1, source_target_pairs={{0,16},{2,18},{4,20},{6,22},{8,24},{10,26},{12,28},{14,30},{16,0},... | collective-permute-start | bytes 442376 | tf_op jit(solution)/shard_map/ppermute | solution.py:613
  56.7 19.1 %copy-start.1 = (f32[72193]{0:T(1024)}, f32[72193]{0:T(1024)S(1)}, u32[]{:S(2)}) copy-start(f32[72193]{0:T(1024)S(1)} %reduce.3.refs_9_.critic_second) | copy-start | bytes 866320
  56.7 19.1 %collective-permute-start.9 = (f32[72193]{0:T(1024)S(1)}, f32[72193]{0:T(1024)S(1)}, u32[]{:S(2)}, u32[]{:S(2)}) collective-permute-start(f32[72193]{0:T(1024)S(1)} %reduce.3.refs_9_.critic_second), channel_id=1, source_target_pairs={{0,1},{1,0},{2,3},{3,2},{4,5},{5,4},{6,7},{7,6},{8,9},{9,8},{10,11... | collective-permute-start | bytes 866324 | tf_op jit(solution)/shard_map/ppermute | solution.py:605
  57.5 18.2 %copy-start.2 = (f32[72193]{0:T(1024)}, f32[72193]{0:T(1024)S(1)}, u32[]{:S(2)}) copy-start(f32[72193]{0:T(1024)S(1)} %reduce.2.refs_7_.critic_first) | copy-start | bytes 866320
  57.5 18.3 %collective-permute-start.8 = (f32[72193]{0:T(1024)S(1)}, f32[72193]{0:T(1024)S(1)}, u32[]{:S(2)}, u32[]{:S(2)}) collective-permute-start(f32[72193]{0:T(1024)S(1)} %reduce.2.refs_7_.critic_first), channel_id=1, source_target_pairs={{0,1},{1,0},{2,3},{3,2},{4,5},{5,4},{6,7},{7,6},{8,9},{9,8},{10,11... | collective-permute-start | bytes 866324 | tf_op jit(solution)/shard_map/ppermute | solution.py:605
  61.0 14.8 %copy-start.5 = (f32[288,128]{1,0:T(8,128)}, f32[288,128]{1,0:T(8,128)S(1)}, u32[]{:S(2)}) copy-start(f32[288,128]{1,0:T(8,128)S(1)} %add.34.refs_3_.one_mine) | copy-start | bytes 442372
  61.0 14.8 %collective-permute-start.7 = (f32[288,128]{1,0:T(8,128)S(1)}, f32[288,128]{1,0:T(8,128)S(1)}, u32[]{:S(2)}, u32[]{:S(2)}) collective-permute-start(f32[288,128]{1,0:T(8,128)S(1)} %add.34.refs_3_.one_mine), channel_id=1, source_target_pairs={{0,1},{1,0},{2,3},{3,2},{4,5},{5,4},{6,7},{7,6},{8,9},{9,8},{10,11... | collective-permute-start | bytes 442376 | tf_op jit(solution)/shard_map/ppermute | solution.py:605
  75.7 23.8 %copy-start.15 = (f32[288,128]{1,0:T(8,128)S(1)}, f32[288,128]{1,0:T(8,128)}, u32[]{:S(2)}) copy-start(f32[288,128]{1,0:T(8,128)} %get-tuple-element.32) | copy-start | bytes 442372
  75.7 26.5 %copy-start.6 = (f32[288,128]{1,0:T(8,128)S(1)}, f32[288,128]{1,0:T(8,128)}, u32[]{:S(2)}) copy-start(f32[288,128]{1,0:T(8,128)} %get-tuple-element.30) | copy-start | bytes 442372
  75.8 0.7 copy-start.9
  75.8 0.8 copy-start.10
  76.6 0.7 copy-start.8
  99.6 12.9 %copy-start.7 = (f32[288,128]{1,0:T(8,128)S(1)}, f32[288,128]{1,0:T(8,128)}, u32[]{:S(2)}) copy-start(f32[288,128]{1,0:T(8,128)} %get-tuple-element.28) | copy-start | bytes 442372
  100.6 1.6 %collective-permute-start.10 = (f32[2,288,128]{2,1,0:T(8,128)S(1)}, f32[2,288,128]{2,1,0:T(8,128)S(1)}, u32[]{:S(2)}, u32[]{:S(2)}) collective-permute-start(f32[2,288,128]{2,1,0:T(8,128)S(1)} %pad_maximum_fusion), channel_id=1, source_target_pairs={{0,1},{1,0},{2,3},{3,2},{4,5},{5,4},{6,7},{7,6},{8,9},{9,8},{10,11... | collective-permute-start | bytes 884744 | tf_op jit(solution)/shard_map/ppermute | solution.py:605
  103.2 9.3 %collective-permute-start.11 = (f32[2,288,128]{2,1,0:T(8,128)S(1)}, f32[2,288,128]{2,1,0:T(8,128)S(1)}, u32[]{:S(2)}, u32[]{:S(2)}) collective-permute-start(f32[2,288,128]{2,1,0:T(8,128)S(1)} %maximum_add_fusion), channel_id=1, source_target_pairs={{0,2},{2,0},{4,6},{6,4},{8,10},{10,8},{12,14},{14,12},{16,18},{18,... | collective-permute-start | bytes 884744 | tf_op jit(solution)/shard_map/ppermute | solution.py:613
  112.5 8.4 %collective-permute-start.12 = (f32[2,288,128]{2,1,0:T(8,128)S(1)}, f32[2,288,128]{2,1,0:T(8,128)S(1)}, u32[]{:S(2)}, u32[]{:S(2)}) collective-permute-start(f32[2,288,128]{2,1,0:T(8,128)S(1)} %fusion.1), channel_id=1, source_target_pairs={{0,4},{2,6},{4,0},{6,2},{8,12},{10,14},{12,8},{14,10},{16,20},{18,... | collective-permute-start | bytes 884744 | tf_op jit(solution)/shard_map/ppermute | solution.py:613
  121.0 7.5 %collective-permute-start.13 = (f32[2,288,128]{2,1,0:T(8,128)S(1)}, f32[2,288,128]{2,1,0:T(8,128)S(1)}, u32[]{:S(2)}, u32[]{:S(2)}) collective-permute-start(f32[2,288,128]{2,1,0:T(8,128)S(1)} %add.37), channel_id=1, source_target_pairs={{0,8},{2,10},{4,12},{6,14},{8,0},{10,2},{12,4},{14,6},{16,24},{18,... | collective-permute-start | bytes 884744 | tf_op jit(solution)/shard_map/ppermute | solution.py:613
  128.5 13.8 %collective-permute-start.14 = (f32[2,288,128]{2,1,0:T(8,128)S(1)}, f32[2,288,128]{2,1,0:T(8,128)S(1)}, u32[]{:S(2)}, u32[]{:S(2)}) collective-permute-start(f32[2,288,128]{2,1,0:T(8,128)S(1)} %add.38), channel_id=1, source_target_pairs={{0,16},{2,18},{4,20},{6,22},{8,24},{10,26},{12,28},{14,30},{16,0},... | collective-permute-start | bytes 884744 | tf_op jit(solution)/shard_map/ppermute | solution.py:613
  142.4 1.6 %collective-permute-start.15 = (f32[2,288,128]{2,1,0:T(8,128)S(1)}, f32[2,288,128]{2,1,0:T(8,128)S(1)}, u32[]{:S(2)}, u32[]{:S(2)}) collective-permute-start(f32[2,288,128]{2,1,0:T(8,128)S(1)} %add.39), channel_id=1, source_target_pairs={{0,1},{1,0},{2,3},{3,2},{4,5},{5,4},{6,7},{7,6},{8,9},{9,8},{10,11... | collective-permute-start | bytes 884744 | tf_op jit(solution)/shard_map/ppermute | solution.py:605
  148.6 7.0 %copy-start.11 = (f32[72193]{0:T(1024)S(1)}, f32[72193]{0:T(1024)}, u32[]{:S(2)}) copy-start(f32[72193]{0:T(1024)} %get-tuple-element.40) | copy-start | bytes 866320

commit v2 on v1

--- a/solution.py
+++ b/solution.py
@@ -27,7 +27,7 @@
 IN_ROWS = 32
 FLAT_ROWS = 576
 HALF_ROWS = FLAT_ROWS // 2
-VMEM_BYTES = 56 * 2**20
+VMEM_BYTES = 24 * 2**20
 
 F32 = jnp.float32
 BF16 = jnp.bfloat16
@@ -169,22 +169,30 @@
         second_t, third_column, action_rows, third_t = back
         second_t[...] = jnp.transpose(second_value).astype(BF16)
         third_low = 0.5 * third_value.astype(BF16).astype(F32)
-        third_column[...] = as_column(third_low[0:1])
-        action_rows[...] = first_t[16:32].astype(BF16)
-        third_t[...] = jnp.transpose(third_low).astype(BF16)
+        if third_column is not None:
+            third_column[...] = as_column(third_low[0:1])
+        if action_rows is not None:
+            action_rows[...] = first_t[16:32].astype(BF16)
+        if third_t is not None:
+            third_t[...] = jnp.transpose(third_low).astype(BF16)
 
 
 def load_flat(net, flat, value):
-    flat[0 : net.rows, :] = value.reshape(net.rows, LANES)
+    flat[0 : net.rows, :] = value
     flat[net.rows : FLAT_ROWS, :] = jnp.zeros((FLAT_ROWS - net.rows, LANES), F32)
 
 
+def span_of(net, ref, tail):
+    where = pl.ds(net.rows * LANES, net.out_size) if tail else pl.ds(0, net.rows * LANES)
+    return (where,) if len(ref.shape) == 1 else (slice(0, 1), where)
+
+
 def body_of(net, ref):
-    return ref[pl.ds(0, net.rows * LANES)]
+    return ref[span_of(net, ref, False)].reshape(net.rows, LANES)
 
 
 def tail_of(net, ref):
-    return ref[pl.ds(net.rows * LANES, net.out_size)].reshape(1, net.out_size)
+    return ref[span_of(net, ref, True)].reshape(1, net.out_size)
 
 
 def tail_column(tail):
@@ -320,18 +328,14 @@
     target_out,
     keep,
     send,
-    inputs,
-    hidden1,
-    tail_sums,
-    flat,
-    units_actor,
-    units_critic,
     *rest,
 ):
-    actor, lag_one, lag_two, critic = rest[0:4], rest[4:8], rest[8:12], rest[12:16]
-    back = rest[16:20]
-    sums = rest[20:23]
-    tails = rest[23]
+    next_critic, next_second_t, next_column, next_tail = rest[0:4], rest[4], rest[5], rest[6]
+    inputs, hidden1, tail_sums, flat, units_actor, units_critic = rest[7:13]
+    actor, lag_one, lag_two, critic = rest[13:17], rest[17:21], rest[21:25], rest[25:29]
+    back = (rest[29], rest[30], None, None)
+    sums = rest[31:34]
+    tails = rest[34]
     core = core_ref[0]
     step = pl.program_id(0)
 
@@ -359,6 +363,12 @@
         tails[8:16, 0:1] = tail_column(tail_of(CRITIC, own_lagged))
         tails[16:24, 0:1] = tail_column(tail_of(CRITIC, far_lagged))
         tails[24:32, 0:1] = tail_column(tail)
+        chosen = jnp.where(core == 1, body_of(CRITIC, own_critic), body_of(CRITIC, far_critic))
+        load_flat(CRITIC, flat, chosen)
+        next_back = (next_second_t, next_column, None, None)
+        unpack_net(CRITIC, flat, mask, units_critic[...], next_critic, next_back)
+        tail = jnp.where(core == 1, tail_of(CRITIC, own_critic), tail_of(CRITIC, far_critic))
+        next_tail[...] = jnp.broadcast_to(tail_column(tail), (8, LANES))
 
     inputs[0:SDIM, :] = next_states[...]
     lagged_action = jnp.tanh(forward(actor, inputs[...].astype(BF16)) + tails[0:8, 0:1])
@@ -386,52 +396,42 @@
         split_halves(flat, core, keep, send)
 
 
-def critic_kernel(
-    row_total,
-    core_ref,
-    states,
-    actions,
-    target,
-    own_critic,
-    far_critic,
-    keep,
-    send,
-    inputs,
-    hidden1,
-    tail_sums,
-    flat,
-    units_critic,
-    *rest,
-):
-    critic, back, sums, tails = rest[0:4], rest[4:8], rest[8:11], rest[11]
-    core = core_ref[0]
-    step = pl.program_id(0)
-
-    @pl.when(step == 0)
-    def _():
-        start_inputs(inputs)
-        hidden1[HID : HID + 16, :] = jnp.ones((16, TILE), BF16)
-        clear(sums)
-        clear([tail_sums])
-        units_critic[...] = place_units(CRITIC)
-        chosen = jnp.where(core == 1, body_of(CRITIC, own_critic), body_of(CRITIC, far_critic))
-        load_flat(CRITIC, flat, chosen)
-        unpack_net(CRITIC, flat, place_mask(CRITIC), units_critic[...], critic, back)
-        tail = jnp.where(core == 1, tail_of(CRITIC, own_critic), tail_of(CRITIC, far_critic))
-        tails[0:8, 0:1] = tail_column(tail)
-
+def critic_kernel(row_total, is_first, is_last, core_ref, *refs):
+    states, actions, target = refs[0:3]
+    critic, second_t, third_column, tail = refs[3:7], refs[7], refs[8], refs[9]
+    refs = refs[10:]
+    before = () if is_first else refs[0:4]
+    refs = refs[len(before) :]
+    if is_last:
+        keep, send, inputs, hidden1 = refs[0:4]
+        sums, tail_sums, flat, units = refs[4:7], refs[7], refs[8], refs[9]
+    else:
+        sums, tail_sums, inputs, hidden1 = refs[0:3], refs[3], refs[4], refs[5]
+    start_inputs(inputs)
+    hidden1[HID : HID + 16, :] = jnp.ones((16, TILE), BF16)
+    if is_first:
+        clear([*sums, tail_sums])
+    for after, value in zip([*sums, tail_sums], before):
+        after[...] = value[...]
     inputs[0:SDIM, :] = states[...]
     inputs[ACTION_ROW : ACTION_ROW + ADIM, :] = actions[...]
     joined = inputs[...].astype(BF16)
     critic_tile(
-        critic, back, tails[0:1, 0:1], joined, target[...], 2.0 / row_total, hidden1, sums, tail_sums
-    )
-
-    @pl.when(step == pl.num_programs(0) - 1)
-    def _():
+        critic,
+        (second_t, third_column),
+        tail[0:1, 0:1],
+        joined,
+        target[...],
+        2.0 / row_total,
+        hidden1,
+        sums,
+        tail_sums,
+    )
+    if is_last:
+        units[...] = place_units(CRITIC)
         last = critic_last_row(tail_sums)
-        write_gradient(CRITIC, sums, last, flat, place_mask(CRITIC), units_critic[...])
-        split_halves(flat, core, keep, send)
+        write_gradient(CRITIC, sums, last, flat, place_mask(CRITIC), units[...])
+        split_halves(flat, core_ref[0], keep, send)
 
 
 def actor_kernel(
@@ -488,8 +488,7 @@
                 chosen(part, own_second, far_second),
             )[0]
 
-        body = gradient[0 : CRITIC.rows, :].reshape(CRITIC.rows * LANES)
-        load_flat(CRITIC, flat, fresh(body_of, body))
+        load_flat(CRITIC, flat, fresh(body_of, gradient[0 : CRITIC.rows, :]))
         unpack_net(CRITIC, flat, place_mask(CRITIC), units_critic[...], judge, judge_back)
         tail = fresh(tail_of, gradient[CRITIC.rows : CRITIC.rows + 1, 0:1])
         tails[8:16, 0:1] = tail_column(tail)
@@ -555,27 +554,24 @@
     new_critic_first,
     new_critic_second,
     new_target_critic,
-    losses,
+    critic_loss,
+    actor_loss,
     gradient,
     second_gradient,
 ):
     core = core_ref[0]
 
     def update(net, grad_ref, sources, outs):
-        for part, where, grad in (
-            (body_of, pl.ds(0, net.rows * LANES), grad_ref[0 : net.rows, :]),
-            (
-                tail_of,
-                pl.ds(net.rows * LANES, net.out_size),
-                grad_ref[net.rows : net.rows + 1, 0 : net.out_size],
-            ),
+        for part, tail, grad in (
+            (body_of, False, grad_ref[0 : net.rows, :]),
+            (tail_of, True, grad_ref[net.rows : net.rows + 1, 0 : net.out_size]),
         ):
             weight, first, second, lagged = [part(net, source) for source in sources]
-            grad = grad.reshape(weight.shape)
             fresh, first, second = adamw_step(weight, grad, first, second)
             results = (fresh, first, second, polyak_mix(lagged, fresh))
             for out, result in zip(outs, results):
-                out[where] = result.reshape(result.size)
+                shape = (1, result.size) if len(out.shape) == 2 else (result.size,)
+                out[span_of(net, out, tail)] = result.reshape(shape)
 
     join_halves(core, actor_mine, actor_other, gradient)
     update(
@@ -586,7 +582,7 @@
     )
     lane = iota((1, LANES), 1)
     actor_row = jnp.where(lane == 8, gradient[ACTOR.rows : ACTOR.rows + 1, :], 0.0)
-    actor_loss = jnp.sum(actor_row, axis=1, keepdims=True)
+    actor_loss[0] = jnp.sum(actor_row)
     join_halves(core, one_mine, one_other, gradient)
     join_halves(core, two_mine, two_other, second_gradient)
     gradient[...] = jnp.where(core == 0, gradient[...], second_gradient[...])
@@ -597,27 +593,28 @@
         (new_critic, new_critic_first, new_critic_second, new_target_critic),
     )
     critic_row = jnp.where(lane == 1, gradient[CRITIC.rows : CRITIC.rows + 1, :], 0.0)
-    critic_loss = jnp.sum(critic_row, axis=1, keepdims=True)
-    losses[...] = jnp.where(lane == 0, critic_loss, jnp.where(lane == 1, actor_loss, 0.0))
+    critic_loss[0] = jnp.sum(critic_row)
 
 
 def twin_swap(value):
     return lax.ppermute(value, "twin", [(0, 1), (1, 0)])
 
 
-def sum_over_chips(value):
-    size = lax.axis_size("dp")
-    mask = 1
-    while mask < size:
-        pairs = [(source, source ^ mask) for source in range(size)]
-        value = value + lax.ppermute(value, "dp", pairs)
-        mask *= 2
-    return value
-
-
-def sum_halves(keep, send):
-    mine = sum_over_chips(keep + twin_swap(send))
-    return mine, twin_swap(mine)
+def to_second(value):
+    return lax.ppermute(value, "twin", [(0, 1)])
+
+
+def chip_masks():
+    return [1 << bit for bit in range((lax.axis_size("dp") - 1).bit_length())]
+
+
+def partner(value, mask):
+    pairs = [(source, source ^ mask) for source in range(lax.axis_size("dp"))]
+    return lax.ppermute(value, "dp", pairs)
+
+
+def in_hbm(value):
+    return pltpu.with_memory_space_constraint(value, pltpu.HBM)
 
 
 def whole(shape):
@@ -646,31 +643,31 @@
     row_total = local_rows * lax.axis_size("dp")
     rewards = rewards.reshape(1, local_rows)
     done_flags = done_flags.reshape(1, local_rows)
-    critic_weights = critic_weights.reshape(-1)
-    critic_first = critic_first.reshape(-1)
-    critic_second = critic_second.reshape(-1)
-    target_critic = target_critic.reshape(-1)
+    far_lagged = twin_swap(target_critic)
     far_weights = twin_swap(critic_weights)
-    far_lagged = twin_swap(target_critic)
     far_first = twin_swap(critic_first)
     far_second = twin_swap(critic_second)
-
-    def mine(rows):
-        return pl.BlockSpec((rows, TILE), lambda i, core_ref: (0, core_ref[0] * tiles + i))
-
-    def local(rows):
-        return pl.BlockSpec((rows, TILE), lambda i, core_ref: (0, i))
+    far_lagged, far_weights, far_first, far_second = lax.optimization_barrier(
+        (far_lagged, far_weights, far_first, far_second)
+    )
+
+    def mine(rows, tile=None):
+        if tile is None:
+            return pl.BlockSpec((rows, TILE), lambda i, core_ref: (0, core_ref[0] * tiles + i))
+        return pl.BlockSpec((rows, TILE), lambda i, core_ref: (0, core_ref[0] * tiles + tile))
+
+    def local(rows, tile=None):
+        return pl.BlockSpec((rows, TILE), lambda i, core_ref: (0, i if tile is None else tile))
 
     actor_flat = whole((ACTOR.size,))
-    critic_flat = whole((CRITIC.size,))
+    critic_flat = whole((1, CRITIC.size))
     half = whole((HALF_ROWS, LANES))
     half_shape = jax.ShapeDtypeStruct((HALF_ROWS, LANES), F32)
-    common = [
-        pltpu.VMEM((IN_ROWS, TILE), F32),
-        pltpu.VMEM((HID + 16, TILE), BF16),
-        pltpu.VMEM((16, TILE), F32),
-        pltpu.VMEM((FLAT_ROWS + 8, LANES), F32),
-    ]
+    inputs = pltpu.VMEM((IN_ROWS, TILE), F32)
+    hidden1 = pltpu.VMEM((HID + 16, TILE), BF16)
+    tail_shapes = (((16, TILE), F32),)
+    flat = pltpu.VMEM((FLAT_ROWS + 8, LANES), F32)
+    common = [inputs, hidden1] + scratch_of(tail_shapes) + [flat]
     units_actor = pltpu.VMEM((LANES * ACTOR.in_size, LANES), BF16)
     units_critic = pltpu.VMEM((LANES * CRITIC.in_size, LANES), BF16)
     net = scratch_of(Weights.shapes)
@@ -679,54 +676,105 @@
     tails = pltpu.VMEM((32, LANES), F32)
     params = pltpu.CompilerParams(vmem_limit_bytes=VMEM_BYTES)
 
-    def call(kernel, in_specs, out_specs, out_shape, scratch, name):
+    def call(
+        kernel, steps, in_specs, out_specs, out_shape, scratch, name, flops, aliases=(), vmem=VMEM_BYTES
+    ):
         return pl.pallas_call(
             kernel,
             grid_spec=pltpu.PrefetchScalarGridSpec(
                 num_scalar_prefetch=1,
-                grid=(tiles,),
+                grid=(steps,),
                 in_specs=in_specs,
                 out_specs=out_specs,
                 scratch_shapes=scratch,
             ),
             out_shape=out_shape,
-            compiler_params=params,
+            input_output_aliases=dict(aliases),
+            compiler_params=pltpu.CompilerParams(vmem_limit_bytes=vmem),
+            cost_estimate=pl.CostEstimate(flops=flops, bytes_accessed=10**6, transcendentals=0),
             name=name,
         )
 
-    target, keep_one, send_one = call(
+    unit_flops = 2 * HID * HID * TILE
+    passed = Weights.shapes + Weights.back_shapes[0:2] + (((8, LANES), F32),)
+    passed_specs = [whole(shape) for shape, dtype in passed]
+    passed_shapes = [jax.ShapeDtypeStruct(shape, dtype) for shape, dtype in passed]
+    target, keep_one, send_one, *critic_two = call(
         lambda *refs: target_kernel(row_total, *refs),
+        tiles,
         [mine(SDIM), mine(ADIM), mine(1), mine(SDIM), mine(1), mine(ADIM), actor_flat]
         + [critic_flat] * 4,
-        [local(1), half, half],
-        [jax.ShapeDtypeStruct((1, local_rows // 2), F32), half_shape, half_shape],
-        common + [units_actor, units_critic] + net * 4 + back + sums + [tails],
+        [local(1), half, half] + passed_specs,
+        [jax.ShapeDtypeStruct((1, local_rows // 2), F32), half_shape, half_shape] + passed_shapes,
+        common + [units_actor, units_critic] + net * 4 + back[0:2] + sums + [tails],
         "target_and_first_critic",
+        16 * tiles * unit_flops,
     )(
         core,
-        states,
-        actions,
-        rewards,
-        next_states,
-        done_flags,
-        smoothing,
+        in_hbm(states),
+        in_hbm(actions),
+        in_hbm(rewards),
+        in_hbm(next_states),
+        in_hbm(done_flags),
+        in_hbm(smoothing),
         target_actor,
         target_critic,
         far_lagged,
         critic_weights,
         far_weights,
     )
-    keep_two, send_two = call(
-        lambda *refs: critic_kernel(row_total, *refs),
-        [mine(SDIM), mine(ADIM), local(1), critic_flat, critic_flat],
-        [half, half],
-        [half_shape, half_shape],
-        common + [units_critic] + net + back + sums + [tails],
-        "second_critic",
-    )(core, states, actions, target, critic_weights, far_weights)
-    one_mine, one_other = sum_halves(keep_one, send_one)
+
+    carried = SUM_SHAPES + tail_shapes
+    carried_specs = [whole(shape) for shape, dtype in carried]
+    carried_shapes = [jax.ShapeDtypeStruct(shape, dtype) for shape, dtype in carried]
+
+    def second_critic(tile, tied_target, state):
+        is_first, is_last = tile == 0, tile == tiles - 1
+        in_specs = [mine(SDIM, tile), mine(ADIM, tile), local(1, tile)] + passed_specs
+        scratch = [inputs, hidden1]
+        out_specs, out_shape = carried_specs, carried_shapes
+        aliases = []
+        if not is_first:
+            aliases = [(1 + len(in_specs) + i, i) for i in range(len(carried))]
+            in_specs = in_specs + carried_specs
+        if is_last:
+            out_specs, out_shape, aliases = [half, half], [half_shape, half_shape], []
+            scratch = scratch + sums + scratch_of(tail_shapes) + [flat, units_critic]
+        return call(
+            lambda *refs: critic_kernel(row_total, is_first, is_last, *refs),
+            1,
+            in_specs,
+            out_specs,
+            out_shape,
+            scratch,
+            "second_critic",
+            8 * unit_flops,
+            aliases,
+        )(core, states, actions, tied_target, *critic_two, *state)
+
+    masks = chip_masks()
+    state = ()
+    one = keep_one + twin_swap(send_one)
+    tile = 0
+    for mask in masks:
+        moved = partner(one, mask)
+        if tile < tiles:
+            one, tied_target = lax.optimization_barrier((one, target))
+            state = second_critic(tile, tied_target, state)
+            tile += 1
+        one = one + moved
+        one, state = lax.optimization_barrier((one, state))
+    while tile < tiles:
+        state = second_critic(tile, target, state)
+        tile += 1
+    keep_two, send_two = state
+    one_other = twin_swap(one)
+    two = keep_two + twin_swap(send_two)
+    two_moved = partner(two, masks[-1])
+    two, one, one_other = lax.optimization_barrier((two, one, one_other))
     keep_actor, send_actor = call(
         lambda *refs: actor_kernel(row_total, *refs),
+        tiles,
         [mine(SDIM), actor_flat, half, half] + [critic_flat] * 6,
         [half, half],
         [half_shape, half_shape],
@@ -736,11 +784,12 @@
         + sums
         + [tails],
         "actor",
+        10 * tiles * unit_flops,
     )(
         core,
         states,
         actor_weights,
-        one_mine,
+        one,
         one_other,
         critic_weights,
         far_weights,
@@ -749,32 +798,48 @@
         critic_second,
         far_second,
     )
-    both_mine, both_other = sum_halves(
-        jnp.stack([keep_actor, keep_two]), jnp.stack([send_actor, send_two])
-    )
-    actor_mine, two_mine = both_mine[0], both_mine[1]
-    actor_other, two_other = both_other[0], both_other[1]
+    actor_moved = twin_swap(send_actor)
+    two = two + two_moved
+    two, keep_actor, actor_moved = lax.optimization_barrier((two, keep_actor, actor_moved))
+    actor = keep_actor + actor_moved
+    for mask, other_mask in zip(masks, masks[-2:-1] + masks[:-2] + [None]):
+        moved = partner(actor, mask)
+        if other_mask is not None:
+            two = two + partner(two, other_mask)
+        actor = actor + moved
+    actor_other = twin_swap(actor)
+    two_other = to_second(two)
     vector = pl.BlockSpec(memory_space=pltpu.VMEM)
     scalar = pl.BlockSpec(memory_space=pltpu.SMEM)
     actor_out = jax.ShapeDtypeStruct((ACTOR.size,), F32)
-    critic_out = jax.ShapeDtypeStruct((CRITIC.size,), F32)
-    results = pl.pallas_call(
+    critic_out = jax.ShapeDtypeStruct((1, CRITIC.size), F32)
+    loss_out = jax.ShapeDtypeStruct((1,), F32)
+    (
+        new_actor,
+        new_actor_first,
+        new_actor_second,
+        new_target_actor,
+        new_critic,
+        new_critic_first,
+        new_critic_second,
+        new_target_critic,
+        critic_loss,
+        actor_loss,
+    ) = pl.pallas_call(
         step_kernel,
         in_specs=[scalar] + [vector] * 14,
-        out_specs=[vector] * 9,
-        out_shape=[actor_out] * 4
-        + [critic_out] * 4
-        + [jax.ShapeDtypeStruct((1, LANES), F32)],
+        out_specs=[vector] * 8 + [scalar] * 2,
+        out_shape=[actor_out] * 4 + [critic_out] * 4 + [loss_out] * 2,
         scratch_shapes=[pltpu.VMEM((FLAT_ROWS, LANES), F32)] * 2,
         compiler_params=params,
         name="step",
     )(
         core,
-        actor_mine,
+        actor,
         actor_other,
-        one_mine,
+        one,
         one_other,
-        two_mine,
+        two,
         two_other,
         actor_weights,
         actor_first,
@@ -785,11 +850,6 @@
         critic_second,
         target_critic,
     )
-    new_actor, new_actor_first, new_actor_second, new_target_actor = results[0:4]
-    new_critic, new_critic_first, new_critic_second, new_target_critic = [
-        result.reshape(1, -1) for result in results[4:8]
-    ]
-    losses = results[8]
     return (
         new_actor,
         new_actor_first,
@@ -799,8 +859,8 @@
         new_critic_second,
         new_target_actor,
         new_target_critic,
-        losses[0, 0:1],
-        losses[0, 1],
+        critic_loss,
+        actor_loss.reshape(()),
     )
 
 

time: 157 us -> 112 us (0.71)
  waiting for transfers between devices: 52.5 us -> 22.1 us
  starting transfers between devices: 17.1 us -> 25.8 us
  local copies, waits for them, and re-layouts: 11.5 us -> 2.94 us
  other arithmetic: 7.81 us -> 0.27 us
  Pallas kernels: 66.7 us -> 59.2 us
    ppermute x8 -> x13, waiting for transfers between devices: 47.4 us -> 15.5 us  [the longest x12 15.5 us: partner(): return lax.ppermute(value, 'dp', pairs)]
    ppermute x8 -> x13, starting transfers between devices: 15.1 us -> 23.5 us  [the longest x12 22.2 us: partner(): return lax.ppermute(value, 'dp', pairs)]
    reshape x4 -> x0, local copies, waits for them, and re-layouts: 6.52 us -> none  [on_device(): result.reshape(1, -1)]
    pallas_call x3 -> x6, Pallas kernels: 62.8 us -> 57.1 us  [the longest x1 25 us: on_device(): call(lambda *refs: target_kernel(row_total, *refs), tiles, [mine(SDIM), m...]
    unnamed x4 -> x0, other arithmetic: 4.71 us -> none
    add x10 -> x15, other arithmetic: 2.13 us -> 0.27 us  [the longest x4 0.07 us: on_device(): actor = actor + moved]
    pallas_call x1, Pallas kernels: 3.86 us -> 2.14 us  [on_device(): pl.pallas_call(step_kernel, in_specs=[scalar] + [vector] * 14, out_specs=...]
    ppermute x8 -> x9, waiting for transfers between devices: 5.1 us -> 6.6 us  [twin_swap(): return lax.ppermute(value, 'twin', [(0, 1), (1, 0)])]
  transfers between devices with their start and end apart: 16 -> 22, of which waited for: 12 -> 18; matrix products, arithmetic and copies ran while one was open for 2% -> 0% of each run, Pallas kernels for 9% -> 29%
where the time goes in v2:
time: 112 us; the launch traced here: 111 us
  Pallas kernels  59.2 us (53%)
  starting transfers between devices  25.8 us (23%)
  waiting for transfers between devices  22.1 us (20%)
  local copies, waits for them, and re-layouts  2.94 us (3%)
  between operations  1.12 us (1%)
    pallas_call x1, Pallas kernels, on_device(): call(lambda *refs: target_kernel(row_total, *refs), tiles, [mine(SDIM), m...  25 us
    ppermute x12, starting transfers between devices, partner(): return lax.ppermute(value, 'dp', pairs)  22.2 us
    pallas_call x1, Pallas kernels, on_device(): call(lambda *refs: actor_kernel(row_total, *refs), tiles, [mine(SDIM), ac...  20.3 us
    ppermute x12, waiting for transfers between devices, partner(): return lax.ppermute(value, 'dp', pairs)  15.5 us
    pallas_call x4, Pallas kernels, second_critic(): call(lambda *refs: critic_kernel(row_total, is_first, is_last, *refs), 1,...  11.8 us
    ppermute x9, waiting for transfers between devices, twin_swap(): return lax.ppermute(value, 'twin', [(0, 1), (1, 0)])  6.6 us
    unnamed x26, local copies, waits for them, and re-layouts  2.94 us
    ppermute x9, starting transfers between devices, twin_swap(): return lax.ppermute(value, 'twin', [(0, 1), (1, 0)])  2.26 us
  transfers between devices with their start and end apart: 22, of which 18 were waited for; matrix products, arithmetic and copies ran while one was open for 0% of the time, Pallas kernels for 29%

profile of v2, /device:TPU:0, one launch (start us, length us, event | category | flops | bytes accessed | tf_op | source)
XLA Modules:
  0.0 111.4 jit_solution(262477832305372625)
XLA Ops:
  0.6 0.5 collective-permute-start.2
  1.2 0.1 collective-permute-start.3
  1.2 0.4 collective-permute-start
  1.7 0.1 collective-permute-start.1
  1.8 0.8 collective-permute-done.2.refs_8_
  2.6 0.4 collective-permute-done.3.refs_10_
  3.0 0.4 collective-permute-done.refs_9_
  3.4 0.4 collective-permute-done.1.refs_11_.refs_6_
  3.8 1.0 copy-done.1
  4.8 1.0 copy-done.5
  5.7 1.0 copy-done.7
  6.7 25.0 %target_and_first_critic.1 = (f32[1,8192]{1,0:T(1,128)S(1)}, f32[288,128]{1,0:T(8,128)S(1)}, f32[288,128]{1,0:T(8,128)S(1)}, bf16[256,32]{1,0:T(8,128)(2,1)S(1)}...) custom-call(s32[1]{0:T(128)} %bitcast.refs_0_.core_ref, ...), custom_call_target="tpu_custom_call" | custom-call | flops 17179869184 | bytes 1000000 | tf_op jit(solution)/shard_map/target_and_first_critic/pallas_call | solution.py:702
  31.7 0.4 collective-permute-start.4
  32.1 1.0 collective-permute-done.4
  33.2 2.9 %collective-permute-start.5 = (f32[288,128]{1,0:T(8,128)S(1)}, f32[288,128]{1,0:T(8,128)S(1)}, u32[]{:S(2)}, u32[]{:S(2)}) collective-permute-start(f32[288,128]{1,0:T(8,128)S(1)} %add.45), channel_id=1, source_target_pairs={{0,2},{2,0},{4,6},{6,4},{8,10},{10,8},{12,14},{14,12},{16,18},{18,... | collective-permute-start | bytes 442376 | tf_op jit(solution)/shard_map/ppermute | solution.py:613
  36.1 2.7 %second_critic.4 = (f32[32,256]{1,0:T(8,128)S(1)}, f32[272,256]{1,0:T(8,128)S(1)}, f32[16,256]{1,0:T(8,128)S(1)}, f32[16,2048]{1,0:T(8,128)S(1)}) custom-call(s32[1]{0:T(128)} %bitcast.refs_0_.core_ref, f32[17,16384]{1,0:T(8,128)S(1)} %copy-done.11, f32[6,16384]{1,0:T(8,128)S(1)} %copy-done.12, f32[1,8192]{1,0:T(1,128)S(1)} %get-tuple-element.124.refs_3_, ...), custom_call_target="tpu_custom_call" | custom-call | flops 2147483648 | bytes 1000000 | tf_op jit(solution)/shard_map/second_critic/pallas_call | solution.py:743
  38.8 1.5 %collective-permute-done.5 = f32[288,128]{1,0:T(8,128)S(1)} collective-permute-done((f32[288,128]{1,0:T(8,128)S(1)}, f32[288,128]{1,0:T(8,128)S(1)}, u32[]{:S(2)}, u32[]{:S(2)}) %collective-permute-start.5) | collective-permute-done | bytes 147488 | tf_op jit(solution)/shard_map/ppermute | solution.py:613
  40.3 1.8 %collective-permute-start.6 = (f32[288,128]{1,0:T(8,128)S(1)}, f32[288,128]{1,0:T(8,128)S(1)}, u32[]{:S(2)}, u32[]{:S(2)}) collective-permute-start(f32[288,128]{1,0:T(8,128)S(1)} %add.46), channel_id=1, source_target_pairs={{0,4},{2,6},{4,0},{6,2},{8,12},{10,14},{12,8},{14,10},{16,20},{18,... | collective-permute-start | bytes 442376 | tf_op jit(solution)/shard_map/ppermute | solution.py:613
  42.1 2.7 %second_critic.5 = (f32[32,256]{1,0:T(8,128)S(1)}, f32[272,256]{1,0:T(8,128)S(1)}, f32[16,256]{1,0:T(8,128)S(1)}, f32[16,2048]{1,0:T(8,128)S(1)}) custom-call(s32[1]{0:T(128)} %bitcast.refs_0_.core_ref, f32[17,16384]{1,0:T(8,128)S(1)} %copy-done.11, ...), custom_call_target="tpu_custom_call", output_to_operand_aliasing={{0}: (11, {}), {1}: (12, {}), {2}: (13, {}), {3}: (14, {})} | custom-call | flops 2147483648 | bytes 1000000 | tf_op jit(solution)/shard_map/second_critic/pallas_call | solution.py:743
  44.8 0.9 collective-permute-done.6
  45.7 1.7 %collective-permute-start.7 = (f32[288,128]{1,0:T(8,128)S(1)}, f32[288,128]{1,0:T(8,128)S(1)}, u32[]{:S(2)}, u32[]{:S(2)}) collective-permute-start(f32[288,128]{1,0:T(8,128)S(1)} %add.47), channel_id=1, source_target_pairs={{0,8},{2,10},{4,12},{6,14},{8,0},{10,2},{12,4},{14,6},{16,24},{18,... | collective-permute-start | bytes 442376 | tf_op jit(solution)/shard_map/ppermute | solution.py:613
  47.4 2.7 %second_critic.6 = (f32[32,256]{1,0:T(8,128)S(1)}, f32[272,256]{1,0:T(8,128)S(1)}, f32[16,256]{1,0:T(8,128)S(1)}, f32[16,2048]{1,0:T(8,128)S(1)}) custom-call(s32[1]{0:T(128)} %bitcast.refs_0_.core_ref, f32[17,16384]{1,0:T(8,128)S(1)} %copy-done.11, ...), custom_call_target="tpu_custom_call", output_to_operand_aliasing={{0}: (11, {}), {1}: (12, {}), {2}: (13, {}), {3}: (14, {})} | custom-call | flops 2147483648 | bytes 1000000 | tf_op jit(solution)/shard_map/second_critic/pallas_call | solution.py:743
  50.1 0.8 collective-permute-done.7
  51.0 3.0 %collective-permute-start.8 = (f32[288,128]{1,0:T(8,128)S(1)}, f32[288,128]{1,0:T(8,128)S(1)}, u32[]{:S(2)}, u32[]{:S(2)}) collective-permute-start(f32[288,128]{1,0:T(8,128)S(1)} %add.48), channel_id=1, source_target_pairs={{0,16},{2,18},{4,20},{6,22},{8,24},{10,26},{12,28},{14,30},{16,0},... | collective-permute-start | bytes 442376 | tf_op jit(solution)/shard_map/ppermute | solution.py:613
  54.0 3.7 %second_critic.7 = (f32[288,128]{1,0:T(8,128)S(1)}, f32[288,128]{1,0:T(8,128)S(1)}) custom-call(s32[1]{0:T(128)} %bitcast.refs_0_.core_ref, f32[17,16384]{1,0:T(8,128)S(1)} %copy-done.11, f32[6,16384]{1,0:T(8,128)S(1)} %copy-done.12, f32[1,8192]{1,0:T(1,128)S(1)} %get-tuple-element.124.refs_3_, bf16[256,32]{1,0:T(8,128)(2,1)S(1)} %get-tuple-element.89.refs_4_, ...), custom_call_target="tpu_custom_call" | custom-call | flops 2147483648 | bytes 1000000 | tf_op jit(solution)/shard_map/second_critic/pallas_call | solution.py:743
  57.7 1.0 collective-permute-done.8
  58.7 0.1 collective-permute-start.9
  58.8 0.5 collective-permute-start.10
  59.3 0.9 collective-permute-done.9
  60.2 1.5 %collective-permute-start.11 = (f32[288,128]{1,0:T(8,128)S(1)}, f32[288,128]{1,0:T(8,128)S(1)}, u32[]{:S(2)}, u32[]{:S(2)}) collective-permute-start(f32[288,128]{1,0:T(8,128)S(1)} %add.50), channel_id=1, source_target_pairs={{0,16},{2,18},{4,20},{6,22},{8,24},{10,26},{12,28},{14,30},{16,0},... | collective-permute-start | bytes 442376 | tf_op jit(solution)/shard_map/ppermute | solution.py:613
  61.7 20.3 %actor.1 = (f32[288,128]{1,0:T(8,128)S(1)}, f32[288,128]{1,0:T(8,128)S(1)}) custom-call(s32[1]{0:T(128)} %bitcast.refs_0_.core_ref, f32[17,16384]{1,0:T(8,128)S(1)} %copy-done.11, f32[71942]{0:T(1024)S(1)} %copy-done, f32[288,128]{1,0:T(8,128)S(1)} %add.49.refs_3_.one_mine, f32[288,128]{1,0:T(8,128)S(1)} %collective-permute-done.10.refs_4_.one_other, ...), custom_call_target="tpu_custom_call" | custom-call | flops 10737418240 | bytes 1000000 | tf_op jit(solution)/shard_map/actor/pallas_call | solution.py:775
  82.0 0.1 collective-permute-start.12
  82.2 1.3 %collective-permute-done.12 = f32[288,128]{1,0:T(8,128)S(1)} collective-permute-done((f32[288,128]{1,0:T(8,128)S(1)}, f32[288,128]{1,0:T(8,128)S(1)}, u32[]{:S(2)}, u32[]{:S(2)}) %collective-permute-start.12) | collective-permute-done | bytes 147488 | tf_op jit(solution)/shard_map/ppermute | solution.py:600
  83.5 1.6 %collective-permute-start.13 = (f32[288,128]{1,0:T(8,128)S(1)}, f32[288,128]{1,0:T(8,128)S(1)}, u32[]{:S(2)}, u32[]{:S(2)}) collective-permute-start(f32[288,128]{1,0:T(8,128)S(1)} %add.52), channel_id=1, source_target_pairs={{0,2},{2,0},{4,6},{6,4},{8,10},{10,8},{12,14},{14,12},{16,18},{18,... | collective-permute-start | bytes 442376 | tf_op jit(solution)/shard_map/ppermute | solution.py:613
  85.1 2.7 %collective-permute-start.18 = (f32[288,128]{1,0:T(8,128)S(1)}, f32[288,128]{1,0:T(8,128)S(1)}, u32[]{:S(2)}, u32[]{:S(2)}) collective-permute-start(f32[288,128]{1,0:T(8,128)S(1)} %add.51), channel_id=1, source_target_pairs={{0,8},{2,10},{4,12},{6,14},{8,0},{10,2},{12,4},{14,6},{16,24},{18,... | collective-permute-start | bytes 442376 | tf_op jit(solution)/shard_map/ppermute | solution.py:613
  87.8 1.7 %collective-permute-done.13 = f32[288,128]{1,0:T(8,128)S(1)} collective-permute-done((f32[288,128]{1,0:T(8,128)S(1)}, f32[288,128]{1,0:T(8,128)S(1)}, u32[]{:S(2)}, u32[]{:S(2)}) %collective-permute-start.13) | collective-permute-done | bytes 147488 | tf_op jit(solution)/shard_map/ppermute | solution.py:613
  89.5 1.6 %collective-permute-start.14 = (f32[288,128]{1,0:T(8,128)S(1)}, f32[288,128]{1,0:T(8,128)S(1)}, u32[]{:S(2)}, u32[]{:S(2)}) collective-permute-start(f32[288,128]{1,0:T(8,128)S(1)} %add.53), channel_id=1, source_target_pairs={{0,4},{2,6},{4,0},{6,2},{8,12},{10,14},{12,8},{14,10},{16,20},{18,... | collective-permute-start | bytes 442376 | tf_op jit(solution)/shard_map/ppermute | solution.py:613
  91.1 0.6 collective-permute-done.18
  91.7 1.0 collective-permute-start.19
  92.7 2.0 %collective-permute-done.14 = f32[288,128]{1,0:T(8,128)S(1)} collective-permute-done((f32[288,128]{1,0:T(8,128)S(1)}, f32[288,128]{1,0:T(8,128)S(1)}, u32[]{:S(2)}, u32[]{:S(2)}) %collective-permute-start.14) | collective-permute-done | bytes 147488 | tf_op jit(solution)/shard_map/ppermute | solution.py:613
  94.8 2.8 %collective-permute-start.15 = (f32[288,128]{1,0:T(8,128)S(1)}, f32[288,128]{1,0:T(8,128)S(1)}, u32[]{:S(2)}, u32[]{:S(2)}) collective-permute-start(f32[288,128]{1,0:T(8,128)S(1)} %add.54), channel_id=1, source_target_pairs={{0,8},{2,10},{4,12},{6,14},{8,0},{10,2},{12,4},{14,6},{16,24},{18,... | collective-permute-start | bytes 442376 | tf_op jit(solution)/shard_map/ppermute | solution.py:613
  97.6 1.6 %collective-permute-start.20 = (f32[288,128]{1,0:T(8,128)S(1)}, f32[288,128]{1,0:T(8,128)S(1)}, u32[]{:S(2)}, u32[]{:S(2)}) collective-permute-start(f32[288,128]{1,0:T(8,128)S(1)} %add.58), channel_id=1, source_target_pairs={{0,4},{2,6},{4,0},{6,2},{8,12},{10,14},{12,8},{14,10},{16,20},{18,... | collective-permute-start | bytes 442376 | tf_op jit(solution)/shard_map/ppermute | solution.py:613
  99.1 2.3 %collective-permute-done.15 = f32[288,128]{1,0:T(8,128)S(1)} collective-permute-done((f32[288,128]{1,0:T(8,128)S(1)}, f32[288,128]{1,0:T(8,128)S(1)}, u32[]{:S(2)}, u32[]{:S(2)}) %collective-permute-start.15) | collective-permute-done | bytes 147488 | tf_op jit(solution)/shard_map/ppermute | solution.py:613
  101.6 1.2 %collective-permute-done.20 = f32[288,128]{1,0:T(8,128)S(1)} collective-permute-done((f32[288,128]{1,0:T(8,128)S(1)}, f32[288,128]{1,0:T(8,128)S(1)}, u32[]{:S(2)}, u32[]{:S(2)}) %collective-permute-start.20) | collective-permute-done | bytes 147488 | tf_op jit(solution)/shard_map/ppermute | solution.py:613
  102.8 1.3 %collective-permute-start.21 = (f32[288,128]{1,0:T(8,128)S(1)}, f32[288,128]{1,0:T(8,128)S(1)}, u32[]{:S(2)}, u32[]{:S(2)}) collective-permute-start(f32[288,128]{1,0:T(8,128)S(1)} %add.59.two_mine), channel_id=1, source_target_pairs={{0,1},{2,3},{4,5},{6,7},{8,9},{10,11},{12,13},{14,15},{16,17},{18,... | collective-permute-start | bytes 442376 | tf_op jit(solution)/shard_map/ppermute | solution.py:604
  104.1 3.5 %collective-permute-done.16 = f32[288,128]{1,0:T(8,128)S(1)} collective-permute-done((f32[288,128]{1,0:T(8,128)S(1)}, f32[288,128]{1,0:T(8,128)S(1)}, u32[]{:S(2)}, u32[]{:S(2)}) %collective-permute-start.16) | collective-permute-done | bytes 147488 | tf_op jit(solution)/shard_map/ppermute | solution.py:613
  107.7 1.3 %collective-permute-done.17.actor_other = f32[288,128]{1,0:T(8,128)S(1)} collective-permute-done((f32[288,128]{1,0:T(8,128)S(1)}, f32[288,128]{1,0:T(8,128)S(1)}, u32[]{:S(2)}, u32[]{:S(2)}) %collective-permute-start.17) | collective-permute-done | bytes 147488 | tf_op jit(solution)/shard_map/ppermute | solution.py:600
  109.1 2.1 %step.1 = (f32[71942]{0:T(1024)}, f32[71942]{0:T(1024)}, f32[71942]{0:T(1024)}, f32[71942]{0:T(1024)}, f32[1,72193]{1,0:T(1,128)}, /*index=5*/f32[1,72193]{1,0:T...) custom-call(s32[1]{0:T(128)} %bitcast.refs_0_.core_ref, f32[288,128]{1,0:T(8,128)S(1)} %add.56.actor_mine, ...), custom_call_target="tpu_custom_call" | custom-call | tf_op jit(solution)/shard_map/step/pallas_call | solution.py:828
  (44 shorter events, 0.5 us)
Async XLA Ops:
  0.6 1.9 %collective-permute-start.2 = (f32[1,72193]{1,0:T(1,128)}, f32[1,72193]{1,0:T(1,128)S(1)}, u32[]{:S(2)}, u32[]{:S(2)}) collective-permute-start(f32[1,72193]{1,0:T(1,128)} %critic_first.1), channel_id=1, source_target_pairs={{0,1},{1,0},{2,3},{3,2},{4,5},{5,4},{6,7},{7,6},{8,9},{9,8},{10,11... | collective-permute-start | bytes 866324 | tf_op jit(solution)/shard_map/ppermute | solution.py:600
  1.2 1.8 %collective-permute-start.3 = (f32[1,72193]{1,0:T(1,128)}, f32[1,72193]{1,0:T(1,128)S(1)}, u32[]{:S(2)}, u32[]{:S(2)}) collective-permute-start(f32[1,72193]{1,0:T(1,128)} %critic_second.1), channel_id=1, source_target_pairs={{0,1},{1,0},{2,3},{3,2},{4,5},{5,4},{6,7},{7,6},{8,9},{9,8},{10,11... | collective-permute-start | bytes 866324 | tf_op jit(solution)/shard_map/ppermute | solution.py:600
  1.2 2.2 %collective-permute-start = (f32[1,72193]{1,0:T(1,128)}, f32[1,72193]{1,0:T(1,128)S(1)}, u32[]{:S(2)}, u32[]{:S(2)}) collective-permute-start(f32[1,72193]{1,0:T(1,128)} %target_critic.1), channel_id=1, source_target_pairs={{0,1},{1,0},{2,3},{3,2},{4,5},{5,4},{6,7},{7,6},{8,9},{9,8},{10,11... | collective-permute-start | bytes 866324 | tf_op jit(solution)/shard_map/ppermute | solution.py:600
  1.7 2.1 %collective-permute-start.1 = (f32[1,72193]{1,0:T(1,128)}, f32[1,72193]{1,0:T(1,128)S(1)}, u32[]{:S(2)}, u32[]{:S(2)}) collective-permute-start(f32[1,72193]{1,0:T(1,128)} %critic_weights.1), channel_id=1, source_target_pairs={{0,1},{1,0},{2,3},{3,2},{4,5},{5,4},{6,7},{7,6},{8,9},{9,8},{10,11... | collective-permute-start | bytes 866324 | tf_op jit(solution)/shard_map/ppermute | solution.py:600
  3.8 1.0 copy-start.1
  4.8 1.0 copy-start.5
  5.7 1.0 copy-start.7
  6.7 29.4 %copy-start.11 = (f32[17,16384]{1,0:T(8,128)S(1)}, f32[17,16384]{1,0:T(8,128)}, u32[]{:S(2)}) copy-start(f32[17,16384]{1,0:T(8,128)} %refs_1_.11) | copy-start | bytes 3342340
  6.7 29.4 %copy-start.12 = (f32[6,16384]{1,0:T(8,128)S(1)}, f32[6,16384]{1,0:T(8,128)}, u32[]{:S(2)}) copy-start(f32[6,16384]{1,0:T(8,128)} %refs_2_.10) | copy-start | bytes 1179652
  31.7 1.4 %collective-permute-start.4 = (f32[288,128]{1,0:T(8,128)S(1)}, f32[288,128]{1,0:T(8,128)S(1)}, u32[]{:S(2)}, u32[]{:S(2)}) collective-permute-start(f32[288,128]{1,0:T(8,128)S(1)} %get-tuple-element.85), channel_id=1, source_target_pairs={{0,1},{1,0},{2,3},{3,2},{4,5},{5,4},{6,7},{7,6},{8,9},{9,8},{10,11... | collective-permute-start | bytes 442376 | tf_op jit(solution)/shard_map/ppermute | solution.py:600
  33.2 7.1 %collective-permute-start.5 = (f32[288,128]{1,0:T(8,128)S(1)}, f32[288,128]{1,0:T(8,128)S(1)}, u32[]{:S(2)}, u32[]{:S(2)}) collective-permute-start(f32[288,128]{1,0:T(8,128)S(1)} %add.45), channel_id=1, source_target_pairs={{0,2},{2,0},{4,6},{6,4},{8,10},{10,8},{12,14},{14,12},{16,18},{18,... | collective-permute-start | bytes 442376 | tf_op jit(solution)/shard_map/ppermute | solution.py:613
  40.3 5.5 %collective-permute-start.6 = (f32[288,128]{1,0:T(8,128)S(1)}, f32[288,128]{1,0:T(8,128)S(1)}, u32[]{:S(2)}, u32[]{:S(2)}) collective-permute-start(f32[288,128]{1,0:T(8,128)S(1)} %add.46), channel_id=1, source_target_pairs={{0,4},{2,6},{4,0},{6,2},{8,12},{10,14},{12,8},{14,10},{16,20},{18,... | collective-permute-start | bytes 442376 | tf_op jit(solution)/shard_map/ppermute | solution.py:613
  45.7 5.2 %collective-permute-start.7 = (f32[288,128]{1,0:T(8,128)S(1)}, f32[288,128]{1,0:T(8,128)S(1)}, u32[]{:S(2)}, u32[]{:S(2)}) collective-permute-start(f32[288,128]{1,0:T(8,128)S(1)} %add.47), channel_id=1, source_target_pairs={{0,8},{2,10},{4,12},{6,14},{8,0},{10,2},{12,4},{14,6},{16,24},{18,... | collective-permute-start | bytes 442376 | tf_op jit(solution)/shard_map/ppermute | solution.py:613
  51.0 10.7 %copy-start = (f32[71942]{0:T(1024)S(1)}, f32[71942]{0:T(1024)}, u32[]{:S(2)}) copy-start(f32[71942]{0:T(1024)} %actor_weights.1) | copy-start | bytes 863308
  51.0 10.7 %copy-start.8 = (f32[1,72193]{1,0:T(1,128)S(1)}, f32[1,72193]{1,0:T(1,128)}, u32[]{:S(2)}) copy-start(f32[1,72193]{1,0:T(1,128)} %critic_weights.1) | copy-start | bytes 866320
  51.0 10.7 %copy-start.9 = (f32[1,72193]{1,0:T(1,128)S(1)}, f32[1,72193]{1,0:T(1,128)}, u32[]{:S(2)}) copy-start(f32[1,72193]{1,0:T(1,128)} %critic_first.1) | copy-start | bytes 866320
  51.0 10.7 %copy-start.10 = (f32[1,72193]{1,0:T(1,128)S(1)}, f32[1,72193]{1,0:T(1,128)}, u32[]{:S(2)}) copy-start(f32[1,72193]{1,0:T(1,128)} %critic_second.1) | copy-start | bytes 866320
  51.0 7.7 %collective-permute-start.8 = (f32[288,128]{1,0:T(8,128)S(1)}, f32[288,128]{1,0:T(8,128)S(1)}, u32[]{:S(2)}, u32[]{:S(2)}) collective-permute-start(f32[288,128]{1,0:T(8,128)S(1)} %add.48), channel_id=1, source_target_pairs={{0,16},{2,18},{4,20},{6,22},{8,24},{10,26},{12,28},{14,30},{16,0},... | collective-permute-start | bytes 442376 | tf_op jit(solution)/shard_map/ppermute | solution.py:613
  58.7 1.4 %collective-permute-start.9 = (f32[288,128]{1,0:T(8,128)S(1)}, f32[288,128]{1,0:T(8,128)S(1)}, u32[]{:S(2)}, u32[]{:S(2)}) collective-permute-start(f32[288,128]{1,0:T(8,128)S(1)} %get-tuple-element.132), channel_id=1, source_target_pairs={{0,1},{1,0},{2,3},{3,2},{4,5},{5,4},{6,7},{7,6},{8,9},{9,8},{10,11... | collective-permute-start | bytes 442376 | tf_op jit(solution)/shard_map/ppermute | solution.py:600
  58.8 2.9 %collective-permute-start.10 = (f32[288,128]{1,0:T(8,128)S(1)}, f32[288,128]{1,0:T(8,128)S(1)}, u32[]{:S(2)}, u32[]{:S(2)}) collective-permute-start(f32[288,128]{1,0:T(8,128)S(1)} %add.49.refs_3_.one_mine), channel_id=1, source_target_pairs={{0,1},{1,0},{2,3},{3,2},{4,5},{5,4},{6,7},{7,6},{8,9},{9,8},{10,11... | collective-permute-start | bytes 442376 | tf_op jit(solution)/shard_map/ppermute | solution.py:600
  60.2 21.9 %collective-permute-start.11 = (f32[288,128]{1,0:T(8,128)S(1)}, f32[288,128]{1,0:T(8,128)S(1)}, u32[]{:S(2)}, u32[]{:S(2)}) collective-permute-start(f32[288,128]{1,0:T(8,128)S(1)} %add.50), channel_id=1, source_target_pairs={{0,16},{2,18},{4,20},{6,22},{8,24},{10,26},{12,28},{14,30},{16,0},... | collective-permute-start | bytes 442376 | tf_op jit(solution)/shard_map/ppermute | solution.py:613
  82.0 1.4 %collective-permute-start.12 = (f32[288,128]{1,0:T(8,128)S(1)}, f32[288,128]{1,0:T(8,128)S(1)}, u32[]{:S(2)}, u32[]{:S(2)}) collective-permute-start(f32[288,128]{1,0:T(8,128)S(1)} %get-tuple-element.140), channel_id=1, source_target_pairs={{0,1},{1,0},{2,3},{3,2},{4,5},{5,4},{6,7},{7,6},{8,9},{9,8},{10,11... | collective-permute-start | bytes 442376 | tf_op jit(solution)/shard_map/ppermute | solution.py:600
  83.5 25.6 %copy-start.2 = (f32[71942]{0:T(1024)S(1)}, f32[71942]{0:T(1024)}, u32[]{:S(2)}) copy-start(f32[71942]{0:T(1024)} %target_actor.1) | copy-start | bytes 863308
  83.5 25.5 %copy-start.3 = (f32[71942]{0:T(1024)S(1)}, f32[71942]{0:T(1024)}, u32[]{:S(2)}) copy-start(f32[71942]{0:T(1024)} %actor_first.1) | copy-start | bytes 863308
  83.5 25.5 %copy-start.4 = (f32[71942]{0:T(1024)S(1)}, f32[71942]{0:T(1024)}, u32[]{:S(2)}) copy-start(f32[71942]{0:T(1024)} %actor_second.1) | copy-start | bytes 863308
  83.5 25.5 %copy-start.6 = (f32[1,72193]{1,0:T(1,128)S(1)}, f32[1,72193]{1,0:T(1,128)}, u32[]{:S(2)}) copy-start(f32[1,72193]{1,0:T(1,128)} %target_critic.1) | copy-start | bytes 866320
  83.5 6.0 %collective-permute-start.13 = (f32[288,128]{1,0:T(8,128)S(1)}, f32[288,128]{1,0:T(8,128)S(1)}, u32[]{:S(2)}, u32[]{:S(2)}) collective-permute-start(f32[288,128]{1,0:T(8,128)S(1)} %add.52), channel_id=1, source_target_pairs={{0,2},{2,0},{4,6},{6,4},{8,10},{10,8},{12,14},{14,12},{16,18},{18,... | collective-permute-start | bytes 442376 | tf_op jit(solution)/shard_map/ppermute | solution.py:613
  85.1 6.6 %collective-permute-start.18 = (f32[288,128]{1,0:T(8,128)S(1)}, f32[288,128]{1,0:T(8,128)S(1)}, u32[]{:S(2)}, u32[]{:S(2)}) collective-permute-start(f32[288,128]{1,0:T(8,128)S(1)} %add.51), channel_id=1, source_target_pairs={{0,8},{2,10},{4,12},{6,14},{8,0},{10,2},{12,4},{14,6},{16,24},{18,... | collective-permute-start | bytes 442376 | tf_op jit(solution)/shard_map/ppermute | solution.py:613
  89.5 5.2 %collective-permute-start.14 = (f32[288,128]{1,0:T(8,128)S(1)}, f32[288,128]{1,0:T(8,128)S(1)}, u32[]{:S(2)}, u32[]{:S(2)}) collective-permute-start(f32[288,128]{1,0:T(8,128)S(1)} %add.53), channel_id=1, source_target_pairs={{0,4},{2,6},{4,0},{6,2},{8,12},{10,14},{12,8},{14,10},{16,20},{18,... | collective-permute-start | bytes 442376 | tf_op jit(solution)/shard_map/ppermute | solution.py:613
  91.7 5.8 %collective-permute-start.19 = (f32[288,128]{1,0:T(8,128)S(1)}, f32[288,128]{1,0:T(8,128)S(1)}, u32[]{:S(2)}, u32[]{:S(2)}) collective-permute-start(f32[288,128]{1,0:T(8,128)S(1)} %add.57), channel_id=1, source_target_pairs={{0,2},{2,0},{4,6},{6,4},{8,10},{10,8},{12,14},{14,12},{16,18},{18,... | collective-permute-start | bytes 442376 | tf_op jit(solution)/shard_map/ppermute | solution.py:613
  94.8 6.7 %collective-permute-start.15 = (f32[288,128]{1,0:T(8,128)S(1)}, f32[288,128]{1,0:T(8,128)S(1)}, u32[]{:S(2)}, u32[]{:S(2)}) collective-permute-start(f32[288,128]{1,0:T(8,128)S(1)} %add.54), channel_id=1, source_target_pairs={{0,8},{2,10},{4,12},{6,14},{8,0},{10,2},{12,4},{14,6},{16,24},{18,... | collective-permute-start | bytes 442376 | tf_op jit(solution)/shard_map/ppermute | solution.py:613
  97.6 5.2 %collective-permute-start.20 = (f32[288,128]{1,0:T(8,128)S(1)}, f32[288,128]{1,0:T(8,128)S(1)}, u32[]{:S(2)}, u32[]{:S(2)}) collective-permute-start(f32[288,128]{1,0:T(8,128)S(1)} %add.58), channel_id=1, source_target_pairs={{0,4},{2,6},{4,0},{6,2},{8,12},{10,14},{12,8},{14,10},{16,20},{18,... | collective-permute-start | bytes 442376 | tf_op jit(solution)/shard_map/ppermute | solution.py:613
  101.5 6.1 %collective-permute-start.16 = (f32[288,128]{1,0:T(8,128)S(1)}, f32[288,128]{1,0:T(8,128)S(1)}, u32[]{:S(2)}, u32[]{:S(2)}) collective-permute-start(f32[288,128]{1,0:T(8,128)S(1)} %add.55), channel_id=1, source_target_pairs={{0,16},{2,18},{4,20},{6,22},{8,24},{10,26},{12,28},{14,30},{16,0},... | collective-permute-start | bytes 442376 | tf_op jit(solution)/shard_map/ppermute | solution.py:613
  102.8 4.9 %collective-permute-start.21 = (f32[288,128]{1,0:T(8,128)S(1)}, f32[288,128]{1,0:T(8,128)S(1)}, u32[]{:S(2)}, u32[]{:S(2)}) collective-permute-start(f32[288,128]{1,0:T(8,128)S(1)} %add.59.two_mine), channel_id=1, source_target_pairs={{0,1},{2,3},{4,5},{6,7},{8,9},{10,11},{12,13},{14,15},{16,17},{18,... | collective-permute-start | bytes 442376 | tf_op jit(solution)/shard_map/ppermute | solution.py:604
  107.6 1.4 %collective-permute-start.17 = (f32[288,128]{1,0:T(8,128)S(1)}, f32[288,128]{1,0:T(8,128)S(1)}, u32[]{:S(2)}, u32[]{:S(2)}) collective-permute-start(f32[288,128]{1,0:T(8,128)S(1)} %add.56.actor_mine), channel_id=1, source_target_pairs={{0,1},{1,0},{2,3},{3,2},{4,5},{5,4},{6,7},{7,6},{8,9},{9,8},{10,11... | collective-permute-start | bytes 442376 | tf_op jit(solution)/shard_map/ppermute | solution.py:600

commit v3 on v2

v3 whole, which is shorter than its diff:
```python
import jax
import jax.numpy as jnp
from jax import lax
from jax.experimental import pallas as pl
from jax.experimental.pallas import tpu as pltpu
from jax.sharding import PartitionSpec as P

SDIM = 17
ADIM = 6
HID = 256
STEP = 10

DISCOUNT = 0.99
POLYAK_RATE = 0.005
LEARN_RATE = 0.05
BETA_ONE = 0.9
BETA_TWO = 0.999
EPSILON = 1e-08
WEIGHT_DECAY = 0.01
NOISE_SCALE = 0.2
NOISE_CLIP = 0.5

LANES = 128
TILE = 2048
ACTION_PART = 2048
LAG = 1
TARGET_TILE = 2048
TARGET_PART = 2048
TARGET_LAG = 1
CRITIC_PART = 1024
CRITIC_LAG = 3
ACTOR_TILE = 2048
ACTOR_PART = 1024
ACTOR_LAG = 3
ONES_ROW = 17
ACTION_ROW = 24
IN_ROWS = 32
FLAT_ROWS = 576
HALF_ROWS = FLAT_ROWS // 2
VMEM_BYTES = 24 * 2**20

F32 = jnp.float32
BF16 = jnp.bfloat16


class Net:
    def __init__(self, in_size, out_size):
        self.in_size = in_size
        self.out_size = out_size
        self.bias1 = 2 * in_size
        self.weight2 = self.bias1 + 2
        self.bias2 = self.weight2 + 2 * HID
        self.weight3 = self.bias2 + 2
        self.rows = self.weight3 + 2 * out_size
        self.size = self.rows * LANES + out_size


ACTOR = Net(SDIM, ADIM)
CRITIC = Net(SDIM + ADIM, 1)


def dot(a, b):
    return jnp.dot(a, b, preferred_element_type=F32)


def dot_nt(a, b):
    return lax.dot_general(a, b, (((1,), (1,)), ((), ())), preferred_element_type=F32)


def wide(column, width):
    return jnp.concatenate([column] * (width // LANES), axis=1)


def iota(shape, axis):
    return lax.broadcasted_iota(jnp.int32, shape, axis)


def rows_to_lanes(block):
    return jnp.concatenate([block[row : row + 1] for row in range(block.shape[0])], axis=1)


def place_mask(net):
    width = LANES * net.in_size
    position = iota((8, width), 1).astype(F32)
    phase = position - net.in_size * jnp.floor((position + 0.5) * (1.0 / net.in_size))
    blocks = []
    for start in range(0, IN_ROWS, 8):
        row = iota((8, width), 0) + start
        source = jnp.where(row < SDIM, row, jnp.where(row >= ACTION_ROW, row - ACTION_ROW + SDIM, -1))
        source = jnp.where(source < net.in_size, source, -1).astype(F32)
        blocks.append(jnp.where(phase == source, 1.0, 0.0))
    return jnp.concatenate(blocks, axis=0)


def place_units(net):
    shape = (LANES * net.in_size, LANES)
    gap = iota(shape, 0) - net.in_size * iota(shape, 1)
    return jnp.where(gap.astype(jnp.uint32) < net.in_size, 1.0, 0.0).astype(BF16)


def three_parts(value):
    high = value.astype(BF16).astype(F32)
    rest = value - high
    middle = rest.astype(BF16).astype(F32)
    return high, middle, rest - middle


def spread_first(net, flat, mask, spread, slot):
    for half in range(2):
        pieces = [
            jnp.broadcast_to(
                flat[half * net.in_size + row : half * net.in_size + row + 1, :],
                (IN_ROWS, LANES),
            )
            for row in range(net.in_size)
        ]
        start = (2 * slot + half) * IN_ROWS
        spread[start : start + IN_ROWS, :] = (
            jnp.concatenate(pieces, axis=1) * mask[...]
        ).astype(BF16)


def gather_first(spread, units, nets):
    gathered = dot(spread[0 : 2 * IN_ROWS * nets, :], units[...])
    halves = [gathered[i * IN_ROWS : (i + 1) * IN_ROWS] for i in range(2 * nets)]
    return [jnp.concatenate(halves[2 * i : 2 * i + 2], axis=1) for i in range(nets)]


def flatten_first(net, transposed, out, mask, units):
    blocks = [transposed[:, 0:LANES], transposed[:, LANES:HID]]
    parts = [part for block in blocks for part in three_parts(block)]
    spread = dot_nt(jnp.concatenate(parts, axis=0).astype(BF16), units[...])
    for half in range(2):
        high, middle, low = [
            spread[(3 * half + part) * IN_ROWS : (3 * half + part + 1) * IN_ROWS]
            for part in range(3)
        ]
        total = (high + (middle + low)) * mask[...]
        line = jnp.sum(total, axis=0, keepdims=True)
        for row in range(net.in_size):
            target = half * net.in_size + row
            out[target : target + 1, :] = line[:, row * LANES : (row + 1) * LANES]


def as_column(row):
    return jnp.transpose(jnp.broadcast_to(row, (LANES, HID)))


def flat_row(flat, start):
    return jnp.concatenate([flat[start : start + 1, :], flat[start + 1 : start + 2, :]], axis=1)


class Weights:
    shapes = (
        ((HID, IN_ROWS), BF16),
        ((HID, HID), BF16),
        ((HID, LANES), F32),
        ((16, HID), BF16),
    )
    back_shapes = (
        ((HID, HID), BF16),
        ((HID, LANES), F32),
        ((16, HID), BF16),
        ((HID, 16), BF16),
    )


def scratch_of(shapes):
    return [pltpu.VMEM(shape, dtype) for shape, dtype in shapes]


def unpack_first(net, first_t, bias1, refs, back=None):
    first_t = 0.5 * first_t
    row = iota((IN_ROWS, HID), 0)
    for part, value in enumerate(three_parts(0.5 * bias1)):
        first_t = jnp.where(row == ONES_ROW + part, value, first_t)
    refs[0][...] = jnp.transpose(first_t).astype(BF16)
    if back is not None and back[2] is not None:
        back[2][...] = first_t[16:32].astype(BF16)


def unpack_rest(net, flat, refs, back=None):
    first, second, bias2, third = refs
    left = flat[pl.ds(net.weight2, HID, stride=2), :]
    right = flat[pl.ds(net.weight2 + 1, HID, stride=2), :]
    second_value = 0.5 * jnp.concatenate([left, right], axis=1)
    second[...] = second_value.astype(BF16)
    bias2[...] = as_column(0.5 * flat_row(flat, net.bias2))
    left = flat[pl.ds(net.weight3, 8, stride=2), :]
    right = flat[pl.ds(net.weight3 + 1, 8, stride=2), :]
    third_value = jnp.concatenate([left, right], axis=1)
    third_value = jnp.where(iota((8, HID), 0) < net.out_size, third_value, 0.0)
    third_value = jnp.concatenate([third_value, jnp.zeros((8, HID), F32)], axis=0)
    third[...] = third_value.astype(BF16)
    if back is not None:
        second_t, third_column, unused, third_t = back
        second_t[...] = jnp.transpose(second_value).astype(BF16)
        third_low = 0.5 * third_value.astype(BF16).astype(F32)
        if third_column is not None:
            third_column[...] = as_column(third_low[0:1])
        if third_t is not None:
            third_t[...] = jnp.transpose(third_low).astype(BF16)


def unpack_nets(net, values, flat, mask, units, spread, refs, backs):
    biases = []
    for slot, (value, net_refs, back) in enumerate(zip(values, refs, backs)):
        load_flat(net, flat, value())
        spread_first(net, flat, mask, spread, slot)
        biases.append(flat_row(flat, net.bias1))
        unpack_rest(net, flat, net_refs, back)
    firsts = gather_first(spread, units, len(values))
    for first_t, bias1, net_refs, back in zip(firsts, biases, refs, backs):
        unpack_first(net, first_t, bias1, net_refs, back)


def load_flat(net, flat, value):
    flat[0 : net.rows, :] = value
    flat[net.rows : FLAT_ROWS, :] = jnp.zeros((FLAT_ROWS - net.rows, LANES), F32)


def span_of(net, ref, tail):
    where = pl.ds(net.rows * LANES, net.out_size) if tail else pl.ds(0, net.rows * LANES)
    return (where,) if len(ref.shape) == 1 else (slice(0, 1), where)


def body_of(net, ref):
    return ref[span_of(net, ref, False)].reshape(net.rows, LANES)


def tail_of(net, ref):
    return ref[span_of(net, ref, True)].reshape(1, net.out_size)


def tail_column(tail):
    size = tail.shape[1]
    eye = iota((8, size), 0) == iota((8, size), 1)
    return jnp.sum(jnp.where(eye, jnp.broadcast_to(tail, (8, size)), 0.0), axis=1, keepdims=True)


def start_inputs(inputs):
    inputs[...] = jnp.zeros_like(inputs)
    row = iota((8, inputs.shape[1]), 0) + 16
    inputs[16:24, :] = jnp.where((row >= ONES_ROW) & (row < ONES_ROW + 3), 1.0, 0.0)


def staggered(parts, lag):
    parts = list(parts)
    step = 0
    while any(part is not None for part in parts):
        for index, part in enumerate(parts):
            if part is not None and step >= index * lag:
                try:
                    next(part)
                except StopIteration:
                    parts[index] = None
        step += 1


def column_parts(width, size):
    return [slice(start, start + size) for start in range(0, width, size)]


def silu_low(half_pre):
    wave = jnp.tanh(half_pre)
    return (half_pre * wave + half_pre).astype(BF16)


def silu_and_slope(half_pre):
    wave = jnp.tanh(half_pre)
    above = 1.0 + wave
    hidden = half_pre * above
    return hidden.astype(BF16), above + hidden * (1.0 - wave)


def forward(refs, inputs):
    first, second, bias2, third = refs
    width = inputs.shape[1]
    pre = dot(first[...], inputs)
    yield
    hidden = silu_low(pre)
    yield
    pre = dot(second[...], hidden)
    yield
    hidden = silu_low(pre + wide(bias2[...], width))
    yield
    return dot(third[...], hidden)[0:8]


def forward_kept(refs, inputs, hidden1=None):
    first, second, bias2, third = refs
    width = inputs.shape[1]
    pre = dot(first[...], inputs)
    yield
    low1, slope1 = silu_and_slope(pre)
    if hidden1 is not None:
        hidden1[0:HID, :] = low1
    yield
    pre = dot(second[...], low1)
    yield
    low2, slope2 = silu_and_slope(pre + wide(bias2[...], width))
    yield
    return dot(third[...], low2)[0:8], slope1, low2, slope2


def write_gradient(net, sums, last_row, flat, mask, units):
    sum1, sum2, sum3 = sums
    flatten_first(net, sum1[...], flat, mask, units)
    bias1 = sum1[ONES_ROW : ONES_ROW + 1, :]
    bias2 = sum2[HID : HID + 1, :]
    weight2 = jnp.transpose(sum2[0:HID, :])
    for side in range(2):
        lanes = slice(side * LANES, (side + 1) * LANES)
        flat[net.bias1 + side : net.bias1 + side + 1, :] = bias1[:, lanes]
        flat[pl.ds(net.weight2 + side, HID, stride=2), :] = weight2[:, lanes]
        flat[net.bias2 + side : net.bias2 + side + 1, :] = bias2[:, lanes]
        for unit in range(net.out_size):
            row = net.weight3 + 2 * unit + side
            flat[row : row + 1, :] = sum3[unit : unit + 1, lanes]
    flat[net.rows : net.rows + 1, :] = last_row
    rest = FLAT_ROWS - net.rows - 1
    flat[net.rows + 1 : FLAT_ROWS, :] = jnp.zeros((rest, LANES), F32)


def split_halves(flat, core, keep, send):
    low = flat[0:HALF_ROWS, :]
    high = flat[HALF_ROWS:FLAT_ROWS, :]
    keep[...] = jnp.where(core == 0, low, high)
    send[...] = jnp.where(core == 0, high, low)


def join_halves(core, mine, other, flat):
    flat[0:HALF_ROWS, :] = jnp.where(core == 0, mine[...], other[...])
    flat[HALF_ROWS:FLAT_ROWS, :] = jnp.where(core == 0, other[...], mine[...])


def adamw_step(weight, gradient, moment_one, moment_two):
    moment_one = BETA_ONE * moment_one + (1.0 - BETA_ONE) * gradient
    moment_two = BETA_TWO * moment_two + (1.0 - BETA_TWO) * gradient * gradient
    corrected_one = moment_one / (1.0 - BETA_ONE**STEP)
    corrected_two = moment_two / (1.0 - BETA_TWO**STEP)
    weight = weight - LEARN_RATE * (
        corrected_one / (jnp.sqrt(corrected_two) + EPSILON) + WEIGHT_DECAY * weight
    )
    return (weight, moment_one, moment_two)


def polyak_mix(lagged, fresh):
    return POLYAK_RATE * fresh + (1.0 - POLYAK_RATE) * lagged


def clear(refs):
    for ref in refs:
        ref[...] = jnp.zeros_like(ref)


SUM_SHAPES = (((IN_ROWS, HID), F32), ((HID + 16, HID), F32), ((16, HID), F32))


def critic_part(refs, back, bias3, inputs, target, scale, hidden1, sums, tail_sums):
    second_t, third_column = back[0], back[1]
    width = inputs.shape[1]
    out, slope1, low2, slope2 = yield from forward_kept(refs, inputs, hidden1)
    error = out[0:1] + bias3 - target
    grad3 = (scale * error).astype(BF16).astype(F32)
    tail_sums[0:1, :] += grad3
    tail_sums[1:2, :] += error * error
    yield
    grad2 = (wide(third_column[...], width) * grad3 * slope2).astype(BF16)
    sums[2][...] += dot_nt(jnp.broadcast_to(grad3, (16, width)).astype(BF16), low2)
    yield
    grad_low1 = dot(second_t[...], grad2)
    yield
    grad1 = (grad_low1 * slope1).astype(BF16)
    sums[1][...] += dot_nt(hidden1[...], grad2)
    yield
    sums[0][...] += dot_nt(inputs, grad1)


def critic_last_row(tail_sums):
    totals = jnp.sum(tail_sums[...], axis=1, keepdims=True)
    lane = iota((1, LANES), 1)
    return jnp.where(lane == 0, totals[0:1], jnp.where(lane == 1, totals[1:2], 0.0))


def action_kernel(
    core_ref,
    next_states,
    smoothing,
    target_actor,
    next_action,
    mask_actor,
    units_actor,
    inputs,
    flat,
    spread,
    tails,
    *actor,
):
    step = pl.program_id(0)

    @pl.when(step == 0)
    def _():
        start_inputs(inputs)
        units_actor[...] = place_units(ACTOR)
        mask_actor[...] = place_mask(ACTOR)
        unpack_nets(
            ACTOR,
            [lambda: body_of(ACTOR, target_actor)],
            flat,
            mask_actor,
            units_actor,
            spread,
            [actor],
            [None],
        )
        tails[0:8, 0:1] = tail_column(tail_of(ACTOR, target_actor))

    inputs[0:SDIM, :] = next_states[...]

    def part(columns):
        out = yield from forward(actor, inputs[:, columns].astype(BF16))
        lagged_action = jnp.tanh(out + tails[0:8, 0:1])
        jitter = jnp.clip(NOISE_SCALE * smoothing[:, columns], -NOISE_CLIP, NOISE_CLIP)
        next_action[:, columns] = jnp.clip(lagged_action[0:ADIM] + jitter, -1.0, 1.0)

    staggered([part(columns) for columns in column_parts(TILE, ACTION_PART)], LAG)


def target_kernel(
    row_total,
    core_ref,
    states,
    actions,
    rewards,
    next_states,
    done_flags,
    next_action,
    own_lagged,
    far_lagged,
    own_critic,
    far_critic,
    target_out,
    keep,
    send,
    mask_critic,
    units_critic,
    *rest,
):
    next_critic, next_second_t, next_column, next_tail = rest[0:4], rest[4], rest[5], rest[6]
    inputs, hidden1, tail_sums, flat, spread, tails, next_inputs = rest[7:14]
    lag_one, lag_two, critic = rest[14:18], rest[18:22], rest[22:26]
    back = (rest[26], rest[27], None, None)
    sums = rest[28:31]
    core = core_ref[0]
    step = pl.program_id(0)
    width = inputs.shape[1]

    @pl.when(step == 0)
    def _():
        start_inputs(inputs)
        start_inputs(next_inputs)
        hidden1[HID : HID + 16, :] = jnp.ones((16, width), BF16)
        clear(sums)
        clear([tail_sums])
        units_critic[...] = place_units(CRITIC)
        mask_critic[...] = place_mask(CRITIC)

        def chosen(part, holder):
            return jnp.where(core == holder, part(CRITIC, own_critic), part(CRITIC, far_critic))

        unpack_nets(
            CRITIC,
            [
                lambda: body_of(CRITIC, own_lagged),
                lambda: body_of(CRITIC, far_lagged),
                lambda: chosen(body_of, 0),
                lambda: chosen(body_of, 1),
            ],
            flat,
            mask_critic,
            units_critic,
            spread,
            [lag_one, lag_two, critic, next_critic],
            [None, None, back, (next_second_t, next_column, None, None)],
        )
        tails[8:16, 0:1] = tail_column(tail_of(CRITIC, own_lagged))
        tails[16:24, 0:1] = tail_column(tail_of(CRITIC, far_lagged))
        tails[24:32, 0:1] = tail_column(chosen(tail_of, 0))
        next_tail[...] = jnp.broadcast_to(tail_column(chosen(tail_of, 1)), (8, LANES))

    next_inputs[0:SDIM, :] = next_states[...]
    next_inputs[ACTION_ROW : ACTION_ROW + ADIM, :] = next_action[...]
    inputs[0:SDIM, :] = states[...]
    inputs[ACTION_ROW : ACTION_ROW + ADIM, :] = actions[...]

    def part(columns):
        joined = next_inputs[:, columns].astype(BF16)
        out_one = yield from forward(lag_one, joined)
        yield
        out_two = yield from forward(lag_two, joined)
        value_one = out_one[0:1] + tails[8:9, 0:1]
        value_two = out_two[0:1] + tails[16:17, 0:1]
        keep_going = 1.0 - done_flags[:, columns].astype(F32)
        lagged = jnp.minimum(value_one, value_two)
        target = rewards[:, columns] + DISCOUNT * keep_going * lagged
        target_out[:, columns] = target

    def next_part(columns):
        return critic_part(
            critic,
            back,
            tails[24:25, 0:1],
            inputs[:, columns].astype(BF16),
            target_out[:, columns],
            2.0 / row_total,
            hidden1.at[:, columns],
            sums,
            tail_sums.at[:, columns],
        )

    staggered([part(columns) for columns in column_parts(width, TARGET_PART)], TARGET_LAG)
    staggered([next_part(columns) for columns in column_parts(width, CRITIC_PART)], CRITIC_LAG)

    @pl.when(step == pl.num_programs(0) - 1)
    def _():
        last = critic_last_row(tail_sums)
        write_gradient(CRITIC, sums, last, flat, mask_critic, units_critic)
        split_halves(flat, core, keep, send)


def critic_kernel(row_total, is_first, is_last, core_ref, *refs):
    states, actions, target = refs[0:3]
    critic, second_t, third_column, tail = refs[3:7], refs[7], refs[8], refs[9]
    refs = refs[10:]
    if is_last:
        mask, units = refs[0:2]
        refs = refs[2:]
    before = () if is_first else refs[0:4]
    refs = refs[len(before) :]
    if is_last:
        keep, send, inputs, hidden1 = refs[0:4]
        sums, tail_sums, flat = refs[4:7], refs[7], refs[8]
    else:
        sums, tail_sums, inputs, hidden1 = refs[0:3], refs[3], refs[4], refs[5]
    start_inputs(inputs)
    hidden1[HID : HID + 16, :] = jnp.ones((16, TILE), BF16)
    if is_first:
        clear([*sums, tail_sums])
    for after, value in zip([*sums, tail_sums], before):
        after[...] = value[...]
    inputs[0:SDIM, :] = states[...]
    inputs[ACTION_ROW : ACTION_ROW + ADIM, :] = actions[...]

    def part(columns):
        return critic_part(
            critic,
            (second_t, third_column),
            tail[0:1, 0:1],
            inputs[:, columns].astype(BF16),
            target[:, columns],
            2.0 / row_total,
            hidden1.at[:, columns],
            sums,
            tail_sums.at[:, columns],
        )

    staggered([part(columns) for columns in column_parts(TILE, CRITIC_PART)], CRITIC_LAG)
    if is_last:
        last = critic_last_row(tail_sums)
        write_gradient(CRITIC, sums, last, flat, mask, units)
        split_halves(flat, core_ref[0], keep, send)


def actor_kernel(
    row_total,
    core_ref,
    states,
    actor_weights,
    mine,
    other,
    own_critic,
    far_critic,
    own_first,
    far_first,
    own_second,
    far_second,
    mask_actor,
    units_actor,
    mask_critic,
    units_critic,
    keep,
    send,
    inputs,
    hidden1,
    tail_sums,
    flat,
    gradient,
    spread_actor,
    spread_critic,
    tails,
    *rest,
):
    actor, actor_back = rest[0:4], (rest[4], None, None, rest[5])
    judge, judge_back = rest[6:10], (rest[10], rest[11], rest[12], None)
    sums = rest[13:16]
    core = core_ref[0]
    step = pl.program_id(0)
    width = inputs.shape[1]

    @pl.when(step == 0)
    def _():
        start_inputs(inputs)
        hidden1[HID : HID + 16, :] = jnp.ones((16, width), BF16)
        clear(sums)
        clear([tail_sums])
        unpack_nets(
            ACTOR,
            [lambda: body_of(ACTOR, actor_weights)],
            flat,
            mask_actor,
            units_actor,
            spread_actor,
            [actor],
            [actor_back],
        )
        tails[0:8, 0:1] = tail_column(tail_of(ACTOR, actor_weights))
        join_halves(core, mine, other, gradient)

        def chosen(part, own, far):
            return jnp.where(core == 0, part(CRITIC, own), part(CRITIC, far))

        def fresh(part, grad):
            return adamw_step(
                chosen(part, own_critic, far_critic),
                grad,
                chosen(part, own_first, far_first),
                chosen(part, own_second, far_second),
            )[0]

        unpack_nets(
            CRITIC,
            [lambda: fresh(body_of, gradient[0 : CRITIC.rows, :])],
            flat,
            mask_critic,
            units_critic,
            spread_critic,
            [judge],
            [judge_back],
        )
        tail = fresh(tail_of, gradient[CRITIC.rows : CRITIC.rows + 1, 0:1])
        tails[8:16, 0:1] = tail_column(tail)

    inputs[0:SDIM, :] = states[...]
    judge_second_t, judge_column, judge_rows, unused = judge_back
    actor_second_t, unused, unused, actor_third_t = actor_back
    start = jnp.full((HID, LANES), -1.0 / row_total, F32).astype(BF16).astype(F32)
    start = judge_column[...] * start

    def part(columns):
        part_width = columns.stop - columns.start
        state_low = inputs[:, columns].astype(BF16)
        hidden = hidden1.at[:, columns]
        out, slope1, low2, slope2 = yield from forward_kept(actor, state_low, hidden)
        action = jnp.tanh(out + tails[0:8, 0:1])
        inputs[ACTION_ROW:IN_ROWS, columns] = action
        joined = inputs[:, columns].astype(BF16)
        yield
        out, judge_slope1, unused, judge_slope2 = yield from forward_kept(judge, joined)
        tail_sums[8:9, columns] += out[0:1] + tails[8:9, 0:1]
        grad2 = (wide(start, part_width) * judge_slope2).astype(BF16)
        yield
        grad_low1 = dot(judge_second_t[...], grad2)
        yield
        grad1 = (grad_low1 * judge_slope1).astype(BF16)
        yield
        grad_action = 2.0 * dot(judge_rows[...], grad1)[8:16]
        grad3 = (grad_action * (1.0 - action * action)).astype(BF16).astype(F32)
        tail_sums[0:8, columns] += grad3
        grad3_low = jnp.concatenate([grad3, jnp.zeros_like(grad3)], axis=0).astype(BF16)
        yield
        grad_low2 = dot(actor_third_t[...], grad3_low)
        yield
        grad2 = (grad_low2 * slope2).astype(BF16)
        sums[2][...] += dot_nt(grad3_low, low2)
        yield
        grad_low1 = dot(actor_second_t[...], grad2)
        yield
        grad1 = (grad_low1 * slope1).astype(BF16)
        sums[1][...] += dot_nt(hidden[...], grad2)
        yield
        sums[0][...] += dot_nt(state_low, grad1)

    staggered([part(columns) for columns in column_parts(width, ACTOR_PART)], ACTOR_LAG)

    @pl.when(step == pl.num_programs(0) - 1)
    def _():
        totals = jnp.sum(tail_sums[...], axis=1, keepdims=True)
        lane = iota((8, LANES), 1)
        biases = jnp.where(lane == iota((8, LANES), 0), totals[0:8], 0.0)
        last = jnp.sum(biases, axis=0, keepdims=True)
        last = jnp.where(iota((1, LANES), 1) == 8, -totals[8:9], last)
        write_gradient(ACTOR, sums, last, flat, mask_actor, units_actor)
        split_halves(flat, core, keep, send)


def step_kernel(net, loss_lane, core_ref, *refs):
    *halves, weights, first, second, lagged = refs[:-7]
    new_weights, new_first, new_second, new_lagged, loss, gradient, other_gradient = refs[-7:]
    core = core_ref[0]
    join_halves(core, halves[0], halves[1], gradient)
    if len(halves) > 2:
        join_halves(core, halves[2], halves[3], other_gradient)
        gradient[...] = jnp.where(core == 0, gradient[...], other_gradient[...])
    for part, tail, grad in (
        (body_of, False, gradient[0 : net.rows, :]),
        (tail_of, True, gradient[net.rows : net.rows + 1, 0 : net.out_size]),
    ):
        values = [part(net, source) for source in (weights, first, second)]
        fresh, moment_one, moment_two = adamw_step(values[0], grad, values[1], values[2])
        results = (fresh, moment_one, moment_two, polyak_mix(part(net, lagged), fresh))
        for out, result in zip((new_weights, new_first, new_second, new_lagged), results):
            shape = (1, result.size) if len(out.shape) == 2 else (result.size,)
            out[span_of(net, out, tail)] = result.reshape(shape)
    lane = iota((1, LANES), 1)
    row = gradient[net.rows : net.rows + 1, :]
    loss[0] = jnp.sum(jnp.where(lane == loss_lane, row, 0.0))


def twin_swap(value):
    return lax.ppermute(value, "twin", [(0, 1), (1, 0)])


def to_second(value):
    return lax.ppermute(value, "twin", [(0, 1)])


def chip_masks():
    return [1 << bit for bit in range((lax.axis_size("dp") - 1).bit_length())]


def partner(value, mask):
    pairs = [(source, source ^ mask) for source in range(lax.axis_size("dp"))]
    return lax.ppermute(value, "dp", pairs)


def in_hbm(value):
    return pltpu.with_memory_space_constraint(value, pltpu.HBM)


def whole(unused):
    return pl.BlockSpec(memory_space=pltpu.VMEM)


def on_device(
    states,
    actions,
    rewards,
    next_states,
    done_flags,
    smoothing,
    actor_weights,
    actor_first,
    actor_second,
    critic_weights,
    critic_first,
    critic_second,
    target_actor,
    target_critic,
):
    core = lax.axis_index("twin").astype(jnp.int32).reshape(1)
    local_rows = states.shape[1]
    tiles = local_rows // 2 // TILE
    row_total = local_rows * lax.axis_size("dp")
    rewards = rewards.reshape(1, local_rows)
    done_flags = done_flags.reshape(1, local_rows)
    far_lagged = twin_swap(target_critic)
    far_weights = twin_swap(critic_weights)
    far_first = twin_swap(critic_first)
    far_second = twin_swap(critic_second)
    far_lagged, far_weights, far_first, far_second = lax.optimization_barrier(
        (far_lagged, far_weights, far_first, far_second)
    )

    def mine(rows, tile=None, width=TILE):
        count = local_rows // 2 // width
        return pl.BlockSpec(
            (rows, width),
            lambda i, core_ref: (0, core_ref[0] * count + (i if tile is None else tile)),
        )

    def local(rows, tile=None, width=TILE):
        return pl.BlockSpec((rows, width), lambda i, core_ref: (0, i if tile is None else tile))

    def tile_scratch(width):
        return [
            pltpu.VMEM((IN_ROWS, width), F32),
            pltpu.VMEM((HID + 16, width), BF16),
            pltpu.VMEM((16, width), F32),
            flat,
        ]

    actor_flat = whole((ACTOR.size,))
    critic_flat = whole((1, CRITIC.size))
    half = whole((HALF_ROWS, LANES))
    half_shape = jax.ShapeDtypeStruct((HALF_ROWS, LANES), F32)
    tail_shapes = (((16, TILE), F32),)
    flat = pltpu.VMEM((FLAT_ROWS + 8, LANES), F32)

    def places(kind):
        width = LANES * kind.in_size
        mask = jax.ShapeDtypeStruct((IN_ROWS, width), F32)
        return [mask, jax.ShapeDtypeStruct((width, LANES), BF16)]

    def spread(kind, nets):
        return pltpu.VMEM((2 * IN_ROWS * nets, LANES * kind.in_size), BF16)

    place_specs = [whole(None)] * 2
    net = scratch_of(Weights.shapes)
    back = scratch_of(Weights.back_shapes)
    sums = scratch_of(SUM_SHAPES)
    tails = pltpu.VMEM((32, LANES), F32)
    params = pltpu.CompilerParams(vmem_limit_bytes=VMEM_BYTES)

    def call(
        kernel, steps, in_specs, out_specs, out_shape, scratch, name, flops, aliases=(), vmem=VMEM_BYTES
    ):
        return pl.pallas_call(
            kernel,
            grid_spec=pltpu.PrefetchScalarGridSpec(
                num_scalar_prefetch=1,
                grid=(steps,),
                in_specs=in_specs,
                out_specs=out_specs,
                scratch_shapes=scratch,
            ),
            out_shape=out_shape,
            input_output_aliases=dict(aliases),
            compiler_params=pltpu.CompilerParams(vmem_limit_bytes=vmem),
            cost_estimate=pl.CostEstimate(flops=flops, bytes_accessed=10**6, transcendentals=0),
            name=name,
        )

    unit_flops = 2 * HID * HID * TILE
    passed = Weights.shapes + Weights.back_shapes[0:2] + (((8, LANES), F32),)
    passed_specs = [whole(shape) for shape, dtype in passed]
    passed_shapes = [jax.ShapeDtypeStruct(shape, dtype) for shape, dtype in passed]
    next_action, *places_actor = call(
        action_kernel,
        tiles,
        [mine(SDIM), mine(ADIM), actor_flat],
        [local(ADIM)] + place_specs,
        [jax.ShapeDtypeStruct((ADIM, local_rows // 2), F32)] + places(ACTOR),
        [pltpu.VMEM((IN_ROWS, TILE), F32), flat, spread(ACTOR, 1), tails] + net,
        "next_action",
        2 * tiles * unit_flops,
    )(core, in_hbm(next_states), in_hbm(smoothing), target_actor)
    target, keep_one, send_one, *rest = call(
        lambda *refs: target_kernel(row_total, *refs),
        local_rows // 2 // TARGET_TILE,
        [mine(rows, None, TARGET_TILE) for rows in (SDIM, ADIM, 1, SDIM, 1)]
        + [local(ADIM, None, TARGET_TILE)]
        + [critic_flat] * 4,
        [local(1, None, TARGET_TILE), half, half] + place_specs + passed_specs,
        [jax.ShapeDtypeStruct((1, local_rows // 2), F32), half_shape, half_shape]
        + places(CRITIC)
        + passed_shapes,
        tile_scratch(TARGET_TILE)
        + [spread(CRITIC, 4), tails, pltpu.VMEM((IN_ROWS, TARGET_TILE), F32)]
        + net * 3
        + back[0:2]
        + sums,
        "target_and_first_critic",
        14 * tiles * unit_flops,
    )(
        core,
        in_hbm(states),
        in_hbm(actions),
        in_hbm(rewards),
        in_hbm(next_states),
        in_hbm(done_flags),
        next_action,
        target_critic,
        far_lagged,
        critic_weights,
        far_weights,
    )
    places_critic, critic_two = rest[0:2], rest[2:]

    carried = SUM_SHAPES + tail_shapes
    carried_specs = [whole(shape) for shape, dtype in carried]
    carried_shapes = [jax.ShapeDtypeStruct(shape, dtype) for shape, dtype in carried]

    def second_critic(tile, tied_target, state):
        is_first, is_last = tile == 0, tile == tiles - 1
        in_specs = [mine(SDIM, tile), mine(ADIM, tile), local(1, tile)] + passed_specs
        operands = [core, states, actions, tied_target, *critic_two]
        if is_last:
            in_specs = in_specs + place_specs
            operands = operands + places_critic
        scratch = tile_scratch(TILE)[0:2]
        out_specs, out_shape = carried_specs, carried_shapes
        aliases = []
        if not is_first:
            aliases = [(1 + len(in_specs) + i, i) for i in range(len(carried))]
            in_specs = in_specs + carried_specs
        if is_last:
            out_specs, out_shape, aliases = [half, half], [half_shape, half_shape], []
            scratch = scratch + sums + scratch_of(tail_shapes) + [flat]
        return call(
            lambda *refs: critic_kernel(row_total, is_first, is_last, *refs),
            1,
            in_specs,
            out_specs,
            out_shape,
            scratch,
            "second_critic",
            8 * unit_flops,
            aliases,
        )(*operands, *state)

    masks = chip_masks()
    state = ()
    one = keep_one + twin_swap(send_one)
    tile = 0
    for mask in masks:
        moved = partner(one, mask)
        if tile < tiles:
            one, tied_target = lax.optimization_barrier((one, target))
            state = second_critic(tile, tied_target, state)
            tile += 1
        one = one + moved
        one, state = lax.optimization_barrier((one, state))
    while tile < tiles:
        state = second_critic(tile, target, state)
        tile += 1
    keep_two, send_two = state
    one_other = twin_swap(one)
    two = keep_two + twin_swap(send_two)
    two_moved = partner(two, masks[-1])
    two, one, one_other = lax.optimization_barrier((two, one, one_other))
    keep_actor, send_actor = call(
        lambda *refs: actor_kernel(row_total, *refs),
        local_rows // 2 // ACTOR_TILE,
        [mine(SDIM, None, ACTOR_TILE), actor_flat, half, half] + [critic_flat] * 6 + place_specs * 2,
        [half, half],
        [half_shape, half_shape],
        tile_scratch(ACTOR_TILE)
        + [pltpu.VMEM((FLAT_ROWS, LANES), F32), spread(ACTOR, 1), spread(CRITIC, 1), tails]
        + net
        + [back[0], back[3]]
        + net
        + back[0:3]
        + sums,
        "actor",
        10 * tiles * unit_flops,
    )(
        core,
        states,
        actor_weights,
        one,
        one_other,
        critic_weights,
        far_weights,
        critic_first,
        far_first,
        critic_second,
        far_second,
        *places_actor,
        *places_critic,
    )
    actor_moved = twin_swap(send_actor)
    two = two + two_moved
    two, keep_actor, actor_moved = lax.optimization_barrier((two, keep_actor, actor_moved))
    actor = keep_actor + actor_moved
    for mask, other_mask in zip(masks, masks[-2:-1] + masks[:-2] + [None]):
        moved = partner(actor, mask)
        if other_mask is not None:
            two = two + partner(two, other_mask)
        actor = actor + moved
    actor_other = twin_swap(actor)
    two_other = to_second(two)

    def step(net, loss_lane, halves, sources, name):
        vector = pl.BlockSpec(memory_space=pltpu.VMEM)
        scalar = pl.BlockSpec(memory_space=pltpu.SMEM)
        return pl.pallas_call(
            lambda *refs: step_kernel(net, loss_lane, *refs),
            in_specs=[scalar] + [vector] * (len(halves) + len(sources)),
            out_specs=[vector] * len(sources) + [scalar],
            out_shape=[jax.ShapeDtypeStruct(source.shape, F32) for source in sources]
            + [jax.ShapeDtypeStruct((1,), F32)],
            scratch_shapes=[pltpu.VMEM((FLAT_ROWS, LANES), F32)] * 2,
            compiler_params=params,
            name=name,
        )(core, *halves, *sources)

    new_critic, new_critic_first, new_critic_second, new_target_critic, critic_loss = step(
        CRITIC,
        1,
        (one, one_other, two, two_other),
        (critic_weights, critic_first, critic_second, target_critic),
        "critic_step",
    )
    new_actor, new_actor_first, new_actor_second, new_target_actor, actor_loss = step(
        ACTOR,
        8,
        (actor, actor_other),
        (actor_weights, actor_first, actor_second, target_actor),
        "actor_step",
    )
    return (
        new_actor,
        new_actor_first,
        new_actor_second,
        new_critic,
        new_critic_first,
        new_critic_second,
        new_target_actor,
        new_target_critic,
        critic_loss,
        actor_loss.reshape(()),
    )


def solution(mesh):
    columns = P(None, "dp")
    critic = P("twin", None)
    return jax.shard_map(
        on_device,
        mesh=mesh,
        in_specs=(
            columns,
            columns,
            P("dp"),
            columns,
            P("dp"),
            columns,
            P(),
            P(),
            P(),
            critic,
            critic,
            critic,
            P(),
            critic,
        ),
        out_specs=(P(), P(), P(), critic, critic, critic, P(), critic, P("twin"), P()),
        check_vma=False,
    )
```

time: 112 us -> 105 us (0.938)
  Pallas kernels: 59.2 us -> 55.8 us
  local copies, waits for them, and re-layouts: 2.94 us -> 1.01 us
  waiting for transfers between devices: 22.1 us -> 20.2 us
    ppermute x9, waiting for transfers between devices: 6.6 us -> 3.2 us  [twin_swap(): return lax.ppermute(value, 'twin', [(0, 1), (1, 0)])]
    pallas_call x3 -> x5, Pallas kernels: 47.4 us -> 45.5 us  [the longest x1 18.7 us: on_device(): call(lambda *refs: target_kernel(row_total, *refs), local_rows // 2 // TA...]
    unnamed x26 -> x22, local copies, waits for them, and re-layouts: 2.94 us -> 1.01 us
    ppermute x12, waiting for transfers between devices: 15.5 us -> 17 us  [partner(): return lax.ppermute(value, 'dp', pairs)]
    pallas_call x4, Pallas kernels: 11.8 us -> 10.4 us  [second_critic(): call(lambda *refs: critic_kernel(row_total, is_first, is_last, *refs), 1,...]
  transfers between devices with their start and end apart: 22 -> 22, of which waited for: 18 -> 13; matrix products, arithmetic and copies ran while one was open for 0% -> 0% of each run, Pallas kernels for 29% -> 34%
where the time goes in v3:
time: 105 us; the launch traced here: 104 us
  Pallas kernels  55.8 us (53%)
  starting transfers between devices  25.8 us (25%)
  waiting for transfers between devices  20.2 us (19%)
  between operations  1.1 us (1%)
    ppermute x12, starting transfers between devices, partner(): return lax.ppermute(value, 'dp', pairs)  22.2 us
    pallas_call x1, Pallas kernels, on_device(): call(lambda *refs: target_kernel(row_total, *refs), local_rows // 2 // TA...  18.7 us
    pallas_call x1, Pallas kernels, on_device(): call(lambda *refs: actor_kernel(row_total, *refs), local_rows // 2 // ACT...  18.5 us
    ppermute x12, waiting for transfers between devices, partner(): return lax.ppermute(value, 'dp', pairs)  17 us
    pallas_call x4, Pallas kernels, second_critic(): call(lambda *refs: critic_kernel(row_total, is_first, is_last, *refs), 1,...  10.4 us
    pallas_call x1, Pallas kernels, on_device(): call(action_kernel, tiles, [mine(SDIM), mine(ADIM), actor_flat], [local(A...  5.21 us
    ppermute x9, waiting for transfers between devices, twin_swap(): return lax.ppermute(value, 'twin', [(0, 1), (1, 0)])  3.2 us
    pallas_call x2, Pallas kernels, step(): pl.pallas_call(lambda *refs: step_kernel(net, loss_lane, *refs), in_specs...  3.12 us
  transfers between devices with their start and end apart: 22, of which 13 were waited for; matrix products, arithmetic and copies ran while one was open for 0% of the time, Pallas kernels for 34%

profile of v3, /device:TPU:0, one launch (start us, length us, event | category | flops | bytes accessed | tf_op | source)
XLA Modules:
  0.0 104.2 jit_solution(17494098779085321995)
XLA Ops:
  0.6 0.5 collective-permute-start.2
  1.2 0.1 collective-permute-start.3
  1.2 0.4 collective-permute-start
  1.7 0.1 collective-permute-start.1
  1.8 1.0 copy-done.1
  2.7 5.2 %next_action.1 = (f32[6,8192]{1,0:T(8,128)S(1)}, f32[32,2176]{1,0:T(8,128)S(1)}, bf16[2176,128]{1,0:T(8,128)(2,1)S(1)}) custom-call(s32[1]{0:T(128)} %bitcast.core_ref.refs_0_, f32[17,16384]{1,0:T(8,128)} %refs_4_.2, f32[6,16384]{1,0:T(8,128)} %smoothing.1, f32[71942]{0:T(1024)S(1)} %copy-done.1), custom_call_target="tpu_custom_call" | custom-call | flops 2147483648 | bytes 1000000 | tf_op jit(solution)/shard_map/next_action/pallas_call | solution.py:848
  8.0 0.0 copy-start.9
  8.0 0.0 copy-start.10
  8.0 18.7 %target_and_first_critic.1 = (f32[1,8192]{1,0:T(1,128)S(1)}, f32[288,128]{1,0:T(8,128)S(1)}, f32[288,128]{1,0:T(8,128)S(1)}, f32[32,2944]{1,0:T(8,128)S(1)}, bf1...) custom-call(s32[1]{0:T(128)} %bitcast.core_ref.refs_0_, ...), custom_call_target="tpu_custom_call" | custom-call | flops 15032385536 | bytes 1000000 | tf_op jit(solution)/shard_map/target_and_first_critic/pallas_call | solution.py:858
  26.7 0.5 collective-permute-start.4
  27.2 1.0 collective-permute-done.4
  28.2 2.9 %collective-permute-start.5 = (f32[288,128]{1,0:T(8,128)S(1)}, f32[288,128]{1,0:T(8,128)S(1)}, u32[]{:S(2)}, u32[]{:S(2)}) collective-permute-start(f32[288,128]{1,0:T(8,128)S(1)} %add.45), channel_id=1, source_target_pairs={{0,2},{2,0},{4,6},{6,4},{8,10},{10,8},{12,14},{14,12},{16,18},{18,... | collective-permute-start | bytes 442376 | tf_op jit(solution)/shard_map/ppermute | solution.py:744
  31.1 2.5 %second_critic.4 = (f32[32,256]{1,0:T(8,128)S(1)}, f32[272,256]{1,0:T(8,128)S(1)}, f32[16,256]{1,0:T(8,128)S(1)}, f32[16,2048]{1,0:T(8,128)S(1)}) custom-call(s32[1]{0:T(128)} %bitcast.core_ref.refs_0_, f32[17,16384]{1,0:T(8,128)S(1)} %copy-done.9, f32[6,16384]{1,0:T(8,128)S(1)} %copy-done.10, f32[1,8192]{1,0:T(1,128)S(1)} %get-tuple-element.130.refs_3_, ...), custom_call_target="tpu_custom_call" | custom-call | flops 2147483648 | bytes 1000000 | tf_op jit(solution)/shard_map/second_critic/pallas_call | solution.py:910
  33.6 1.7 %collective-permute-done.5 = f32[288,128]{1,0:T(8,128)S(1)} collective-permute-done((f32[288,128]{1,0:T(8,128)S(1)}, f32[288,128]{1,0:T(8,128)S(1)}, u32[]{:S(2)}, u32[]{:S(2)}) %collective-permute-start.5) | collective-permute-done | bytes 147488 | tf_op jit(solution)/shard_map/ppermute | solution.py:744
  35.3 1.8 %collective-permute-start.6 = (f32[288,128]{1,0:T(8,128)S(1)}, f32[288,128]{1,0:T(8,128)S(1)}, u32[]{:S(2)}, u32[]{:S(2)}) collective-permute-start(f32[288,128]{1,0:T(8,128)S(1)} %add.46), channel_id=1, source_target_pairs={{0,4},{2,6},{4,0},{6,2},{8,12},{10,14},{12,8},{14,10},{16,20},{18,... | collective-permute-start | bytes 442376 | tf_op jit(solution)/shard_map/ppermute | solution.py:744
  37.1 2.5 %second_critic.5 = (f32[32,256]{1,0:T(8,128)S(1)}, f32[272,256]{1,0:T(8,128)S(1)}, f32[16,256]{1,0:T(8,128)S(1)}, f32[16,2048]{1,0:T(8,128)S(1)}) custom-call(s32[1]{0:T(128)} %bitcast.core_ref.refs_0_, f32[17,16384]{1,0:T(8,128)S(1)} %copy-done.9, ...), custom_call_target="tpu_custom_call", output_to_operand_aliasing={{0}: (11, {}), {1}: (12, {}), {2}: (13, {}), {3}: (14, {})} | custom-call | flops 2147483648 | bytes 1000000 | tf_op jit(solution)/shard_map/second_critic/pallas_call | solution.py:910
  39.6 1.2 %collective-permute-done.6 = f32[288,128]{1,0:T(8,128)S(1)} collective-permute-done((f32[288,128]{1,0:T(8,128)S(1)}, f32[288,128]{1,0:T(8,128)S(1)}, u32[]{:S(2)}, u32[]{:S(2)}) %collective-permute-start.6) | collective-permute-done | bytes 147488 | tf_op jit(solution)/shard_map/ppermute | solution.py:744
  40.8 1.6 %collective-permute-start.7 = (f32[288,128]{1,0:T(8,128)S(1)}, f32[288,128]{1,0:T(8,128)S(1)}, u32[]{:S(2)}, u32[]{:S(2)}) collective-permute-start(f32[288,128]{1,0:T(8,128)S(1)} %add.47), channel_id=1, source_target_pairs={{0,8},{2,10},{4,12},{6,14},{8,0},{10,2},{12,4},{14,6},{16,24},{18,... | collective-permute-start | bytes 442376 | tf_op jit(solution)/shard_map/ppermute | solution.py:744
  42.4 2.5 %second_critic.6 = (f32[32,256]{1,0:T(8,128)S(1)}, f32[272,256]{1,0:T(8,128)S(1)}, f32[16,256]{1,0:T(8,128)S(1)}, f32[16,2048]{1,0:T(8,128)S(1)}) custom-call(s32[1]{0:T(128)} %bitcast.core_ref.refs_0_, f32[17,16384]{1,0:T(8,128)S(1)} %copy-done.9, ...), custom_call_target="tpu_custom_call", output_to_operand_aliasing={{0}: (11, {}), {1}: (12, {}), {2}: (13, {}), {3}: (14, {})} | custom-call | flops 2147483648 | bytes 1000000 | tf_op jit(solution)/shard_map/second_critic/pallas_call | solution.py:910
  44.9 1.1 %collective-permute-done.7 = f32[288,128]{1,0:T(8,128)S(1)} collective-permute-done((f32[288,128]{1,0:T(8,128)S(1)}, f32[288,128]{1,0:T(8,128)S(1)}, u32[]{:S(2)}, u32[]{:S(2)}) %collective-permute-start.7) | collective-permute-done | bytes 147488 | tf_op jit(solution)/shard_map/ppermute | solution.py:744
  46.0 3.1 %collective-permute-start.8 = (f32[288,128]{1,0:T(8,128)S(1)}, f32[288,128]{1,0:T(8,128)S(1)}, u32[]{:S(2)}, u32[]{:S(2)}) collective-permute-start(f32[288,128]{1,0:T(8,128)S(1)} %add.48), channel_id=1, source_target_pairs={{0,16},{2,18},{4,20},{6,22},{8,24},{10,26},{12,28},{14,30},{16,0},... | collective-permute-start | bytes 442376 | tf_op jit(solution)/shard_map/ppermute | solution.py:744
  49.1 3.0 %second_critic.7 = (f32[288,128]{1,0:T(8,128)S(1)}, f32[288,128]{1,0:T(8,128)S(1)}) custom-call(s32[1]{0:T(128)} %bitcast.core_ref.refs_0_, f32[17,16384]{1,0:T(8,128)S(1)} %copy-done.9, f32[6,16384]{1,0:T(8,128)S(1)} %copy-done.10, f32[1,8192]{1,0:T(1,128)S(1)} %get-tuple-element.130.refs_3_, bf16[256,32]{1,0:T(8,128)(2,1)S(1)} %get-tuple-element.95.refs_4_, ...), custom_call_target="tpu_custom_call" | custom-call | flops 2147483648 | bytes 1000000 | tf_op jit(solution)/shard_map/second_critic/pallas_call | solution.py:910
  52.1 1.7 %collective-permute-done.8 = f32[288,128]{1,0:T(8,128)S(1)} collective-permute-done((f32[288,128]{1,0:T(8,128)S(1)}, f32[288,128]{1,0:T(8,128)S(1)}, u32[]{:S(2)}, u32[]{:S(2)}) %collective-permute-start.8) | collective-permute-done | bytes 147488 | tf_op jit(solution)/shard_map/ppermute | solution.py:744
  53.8 0.1 collective-permute-start.9
  53.9 0.5 collective-permute-start.10
  54.4 0.9 collective-permute-done.9
  55.3 1.5 %collective-permute-start.11 = (f32[288,128]{1,0:T(8,128)S(1)}, f32[288,128]{1,0:T(8,128)S(1)}, u32[]{:S(2)}, u32[]{:S(2)}) collective-permute-start(f32[288,128]{1,0:T(8,128)S(1)} %add.50), channel_id=1, source_target_pairs={{0,16},{2,18},{4,20},{6,22},{8,24},{10,26},{12,28},{14,30},{16,0},... | collective-permute-start | bytes 442376 | tf_op jit(solution)/shard_map/ppermute | solution.py:744
  56.8 18.5 %actor.1 = (f32[288,128]{1,0:T(8,128)S(1)}, f32[288,128]{1,0:T(8,128)S(1)}) custom-call(s32[1]{0:T(128)} %bitcast.core_ref.refs_0_, f32[17,16384]{1,0:T(8,128)S(1)} %copy-done.9, f32[71942]{0:T(1024)S(1)} %copy-done, f32[288,128]{1,0:T(8,128)S(1)} %add.49.refs_3_.refs_1_, f32[288,128]{1,0:T(8,128)S(1)} %collective-permute-done.10.refs_4_.refs_2_, ...), custom_call_target="tpu_custom_call" | custom-call | flops 10737418240 | bytes 1000000 | tf_op jit(solution)/shard_map/actor/pallas_call | solution.py:942
  75.3 0.1 collective-permute-start.12
  75.4 1.3 %collective-permute-done.12 = f32[288,128]{1,0:T(8,128)S(1)} collective-permute-done((f32[288,128]{1,0:T(8,128)S(1)}, f32[288,128]{1,0:T(8,128)S(1)}, u32[]{:S(2)}, u32[]{:S(2)}) %collective-permute-start.12) | collective-permute-done | bytes 147488 | tf_op jit(solution)/shard_map/ppermute | solution.py:731
  76.7 1.6 %collective-permute-start.13 = (f32[288,128]{1,0:T(8,128)S(1)}, f32[288,128]{1,0:T(8,128)S(1)}, u32[]{:S(2)}, u32[]{:S(2)}) collective-permute-start(f32[288,128]{1,0:T(8,128)S(1)} %add.52), channel_id=1, source_target_pairs={{0,2},{2,0},{4,6},{6,4},{8,10},{10,8},{12,14},{14,12},{16,18},{18,... | collective-permute-start | bytes 442376 | tf_op jit(solution)/shard_map/ppermute | solution.py:744
  78.3 2.6 %collective-permute-start.18 = (f32[288,128]{1,0:T(8,128)S(1)}, f32[288,128]{1,0:T(8,128)S(1)}, u32[]{:S(2)}, u32[]{:S(2)}) collective-permute-start(f32[288,128]{1,0:T(8,128)S(1)} %add.51), channel_id=1, source_target_pairs={{0,8},{2,10},{4,12},{6,14},{8,0},{10,2},{12,4},{14,6},{16,24},{18,... | collective-permute-start | bytes 442376 | tf_op jit(solution)/shard_map/ppermute | solution.py:744
  80.9 1.8 %collective-permute-done.13 = f32[288,128]{1,0:T(8,128)S(1)} collective-permute-done((f32[288,128]{1,0:T(8,128)S(1)}, f32[288,128]{1,0:T(8,128)S(1)}, u32[]{:S(2)}, u32[]{:S(2)}) %collective-permute-start.13) | collective-permute-done | bytes 147488 | tf_op jit(solution)/shard_map/ppermute | solution.py:744
  82.7 1.6 %collective-permute-start.14 = (f32[288,128]{1,0:T(8,128)S(1)}, f32[288,128]{1,0:T(8,128)S(1)}, u32[]{:S(2)}, u32[]{:S(2)}) collective-permute-start(f32[288,128]{1,0:T(8,128)S(1)} %add.53), channel_id=1, source_target_pairs={{0,4},{2,6},{4,0},{6,2},{8,12},{10,14},{12,8},{14,10},{16,20},{18,... | collective-permute-start | bytes 442376 | tf_op jit(solution)/shard_map/ppermute | solution.py:744
  84.3 0.5 collective-permute-done.18
  84.8 1.0 collective-permute-start.19
  85.8 2.1 %collective-permute-done.14 = f32[288,128]{1,0:T(8,128)S(1)} collective-permute-done((f32[288,128]{1,0:T(8,128)S(1)}, f32[288,128]{1,0:T(8,128)S(1)}, u32[]{:S(2)}, u32[]{:S(2)}) %collective-permute-start.14) | collective-permute-done | bytes 147488 | tf_op jit(solution)/shard_map/ppermute | solution.py:744
  87.9 2.7 %collective-permute-start.15 = (f32[288,128]{1,0:T(8,128)S(1)}, f32[288,128]{1,0:T(8,128)S(1)}, u32[]{:S(2)}, u32[]{:S(2)}) collective-permute-start(f32[288,128]{1,0:T(8,128)S(1)} %add.54), channel_id=1, source_target_pairs={{0,8},{2,10},{4,12},{6,14},{8,0},{10,2},{12,4},{14,6},{16,24},{18,... | collective-permute-start | bytes 442376 | tf_op jit(solution)/shard_map/ppermute | solution.py:744
  90.7 0.0 copy-start.2
  90.7 1.6 %collective-permute-start.20 = (f32[288,128]{1,0:T(8,128)S(1)}, f32[288,128]{1,0:T(8,128)S(1)}, u32[]{:S(2)}, u32[]{:S(2)}) collective-permute-start(f32[288,128]{1,0:T(8,128)S(1)} %add.58), channel_id=1, source_target_pairs={{0,4},{2,6},{4,0},{6,2},{8,12},{10,14},{12,8},{14,10},{16,20},{18,... | collective-permute-start | bytes 442376 | tf_op jit(solution)/shard_map/ppermute | solution.py:744
  92.3 2.3 %collective-permute-done.15 = f32[288,128]{1,0:T(8,128)S(1)} collective-permute-done((f32[288,128]{1,0:T(8,128)S(1)}, f32[288,128]{1,0:T(8,128)S(1)}, u32[]{:S(2)}, u32[]{:S(2)}) %collective-permute-start.15) | collective-permute-done | bytes 147488 | tf_op jit(solution)/shard_map/ppermute | solution.py:744
  94.6 0.1 collective-permute-start.16
  94.7 1.2 %collective-permute-done.20 = f32[288,128]{1,0:T(8,128)S(1)} collective-permute-done((f32[288,128]{1,0:T(8,128)S(1)}, f32[288,128]{1,0:T(8,128)S(1)}, u32[]{:S(2)}, u32[]{:S(2)}) %collective-permute-start.20) | collective-permute-done | bytes 147488 | tf_op jit(solution)/shard_map/ppermute | solution.py:744
  95.9 1.3 %collective-permute-start.21 = (f32[288,128]{1,0:T(8,128)S(1)}, f32[288,128]{1,0:T(8,128)S(1)}, u32[]{:S(2)}, u32[]{:S(2)}) collective-permute-start(f32[288,128]{1,0:T(8,128)S(1)} %add.59.refs_3_), channel_id=1, source_target_pairs={{0,1},{2,3},{4,5},{6,7},{8,9},{10,11},{12,13},{14,15},{16,17},{18,... | collective-permute-start | bytes 442376 | tf_op jit(solution)/shard_map/ppermute | solution.py:735
  97.2 3.5 %collective-permute-done.16 = f32[288,128]{1,0:T(8,128)S(1)} collective-permute-done((f32[288,128]{1,0:T(8,128)S(1)}, f32[288,128]{1,0:T(8,128)S(1)}, u32[]{:S(2)}, u32[]{:S(2)}) %collective-permute-start.16) | collective-permute-done | bytes 147488 | tf_op jit(solution)/shard_map/ppermute | solution.py:744
  100.7 0.1 collective-permute-start.17
  100.8 1.6 %critic_step.1 = (f32[1,72193]{1,0:T(1,128)}, f32[1,72193]{1,0:T(1,128)}, f32[1,72193]{1,0:T(1,128)}, f32[1,72193]{1,0:T(1,128)}, f32[1]{0:T(128)}) custom-call(s32[1]{0:T(128)} %bitcast.core_ref.refs_0_, f32[288,128]{1,0:T(8,128)S(1)} %add.49.refs_3_.refs_1_, f32[288,128]{1,0:T(8,128)S(1)} %collective-permute-done.10.refs_4_.refs_2_, ...), custom_call_target="tpu_custom_call" | custom-call | tf_op jit(solution)/shard_map/critic_step/pallas_call | solution.py:987
  102.4 1.5 %actor_step.1 = (f32[71942]{0:T(1024)}, f32[71942]{0:T(1024)}, f32[71942]{0:T(1024)}, f32[71942]{0:T(1024)}, f32[1]{0:T(128)}) custom-call(s32[1]{0:T(128)} %bitcast.core_ref.refs_0_, f32[288,128]{1,0:T(8,128)S(1)} %add.56.refs_1_, f32[288,128]{1,0:T(8,128)S(1)} %collective-permute-done.17.refs_2_, f32[71942]{0:T(1024)S(1)} %copy-done, f32[71942]{0:T(1024)S(1)} %copy-done.3, ...), custom_call_target="tpu_custom_call" | custom-call | tf_op jit(solution)/shard_map/actor_step/pallas_call | solution.py:987
  (42 shorter events, 0.3 us)
Async XLA Ops:
  0.6 7.3 %collective-permute-start.2 = (f32[1,72193]{1,0:T(1,128)}, f32[1,72193]{1,0:T(1,128)S(1)}, u32[]{:S(2)}, u32[]{:S(2)}) collective-permute-start(f32[1,72193]{1,0:T(1,128)} %refs_6_.3), channel_id=1, source_target_pairs={{0,1},{1,0},{2,3},{3,2},{4,5},{5,4},{6,7},{7,6},{8,9},{9,8},{10,11... | collective-permute-start | bytes 866324 | tf_op jit(solution)/shard_map/ppermute | solution.py:731
  1.2 6.8 %collective-permute-start.3 = (f32[1,72193]{1,0:T(1,128)}, f32[1,72193]{1,0:T(1,128)S(1)}, u32[]{:S(2)}, u32[]{:S(2)}) collective-permute-start(f32[1,72193]{1,0:T(1,128)} %refs_7_.5), channel_id=1, source_target_pairs={{0,1},{1,0},{2,3},{3,2},{4,5},{5,4},{6,7},{7,6},{8,9},{9,8},{10,11... | collective-permute-start | bytes 866324 | tf_op jit(solution)/shard_map/ppermute | solution.py:731
  1.2 6.7 %collective-permute-start = (f32[1,72193]{1,0:T(1,128)}, f32[1,72193]{1,0:T(1,128)S(1)}, u32[]{:S(2)}, u32[]{:S(2)}) collective-permute-start(f32[1,72193]{1,0:T(1,128)} %refs_8_.1), channel_id=1, source_target_pairs={{0,1},{1,0},{2,3},{3,2},{4,5},{5,4},{6,7},{7,6},{8,9},{9,8},{10,11... | collective-permute-start | bytes 866324 | tf_op jit(solution)/shard_map/ppermute | solution.py:731
  1.7 6.3 %collective-permute-start.1 = (f32[1,72193]{1,0:T(1,128)}, f32[1,72193]{1,0:T(1,128)S(1)}, u32[]{:S(2)}, u32[]{:S(2)}) collective-permute-start(f32[1,72193]{1,0:T(1,128)} %refs_5_.5), channel_id=1, source_target_pairs={{0,1},{1,0},{2,3},{3,2},{4,5},{5,4},{6,7},{7,6},{8,9},{9,8},{10,11... | collective-permute-start | bytes 866324 | tf_op jit(solution)/shard_map/ppermute | solution.py:731
  1.8 1.0 copy-start.1
  2.7 5.3 %copy-start.5 = (f32[1,72193]{1,0:T(1,128)S(1)}, f32[1,72193]{1,0:T(1,128)}, u32[]{:S(2)}) copy-start(f32[1,72193]{1,0:T(1,128)} %refs_8_.1) | copy-start | bytes 866320
  2.7 5.3 %copy-start.6 = (f32[1,72193]{1,0:T(1,128)S(1)}, f32[1,72193]{1,0:T(1,128)}, u32[]{:S(2)}) copy-start(f32[1,72193]{1,0:T(1,128)} %refs_5_.5) | copy-start | bytes 866320
  8.0 23.1 %copy-start.9 = (f32[17,16384]{1,0:T(8,128)S(1)}, f32[17,16384]{1,0:T(8,128)}, u32[]{:S(2)}) copy-start(f32[17,16384]{1,0:T(8,128)} %refs_1_.11) | copy-start | bytes 3342340
  8.0 23.1 %copy-start.10 = (f32[6,16384]{1,0:T(8,128)S(1)}, f32[6,16384]{1,0:T(8,128)}, u32[]{:S(2)}) copy-start(f32[6,16384]{1,0:T(8,128)} %refs_2_.10) | copy-start | bytes 1179652
  26.7 1.5 %collective-permute-start.4 = (f32[288,128]{1,0:T(8,128)S(1)}, f32[288,128]{1,0:T(8,128)S(1)}, u32[]{:S(2)}, u32[]{:S(2)}) collective-permute-start(f32[288,128]{1,0:T(8,128)S(1)} %get-tuple-element.91), channel_id=1, source_target_pairs={{0,1},{1,0},{2,3},{3,2},{4,5},{5,4},{6,7},{7,6},{8,9},{9,8},{10,11... | collective-permute-start | bytes 442376 | tf_op jit(solution)/shard_map/ppermute | solution.py:731
  28.2 7.1 %collective-permute-start.5 = (f32[288,128]{1,0:T(8,128)S(1)}, f32[288,128]{1,0:T(8,128)S(1)}, u32[]{:S(2)}, u32[]{:S(2)}) collective-permute-start(f32[288,128]{1,0:T(8,128)S(1)} %add.45), channel_id=1, source_target_pairs={{0,2},{2,0},{4,6},{6,4},{8,10},{10,8},{12,14},{14,12},{16,18},{18,... | collective-permute-start | bytes 442376 | tf_op jit(solution)/shard_map/ppermute | solution.py:744
  35.3 5.5 %collective-permute-start.6 = (f32[288,128]{1,0:T(8,128)S(1)}, f32[288,128]{1,0:T(8,128)S(1)}, u32[]{:S(2)}, u32[]{:S(2)}) collective-permute-start(f32[288,128]{1,0:T(8,128)S(1)} %add.46), channel_id=1, source_target_pairs={{0,4},{2,6},{4,0},{6,2},{8,12},{10,14},{12,8},{14,10},{16,20},{18,... | collective-permute-start | bytes 442376 | tf_op jit(solution)/shard_map/ppermute | solution.py:744
  40.8 5.2 %collective-permute-start.7 = (f32[288,128]{1,0:T(8,128)S(1)}, f32[288,128]{1,0:T(8,128)S(1)}, u32[]{:S(2)}, u32[]{:S(2)}) collective-permute-start(f32[288,128]{1,0:T(8,128)S(1)} %add.47), channel_id=1, source_target_pairs={{0,8},{2,10},{4,12},{6,14},{8,0},{10,2},{12,4},{14,6},{16,24},{18,... | collective-permute-start | bytes 442376 | tf_op jit(solution)/shard_map/ppermute | solution.py:744
  46.0 7.8 %collective-permute-start.8 = (f32[288,128]{1,0:T(8,128)S(1)}, f32[288,128]{1,0:T(8,128)S(1)}, u32[]{:S(2)}, u32[]{:S(2)}) collective-permute-start(f32[288,128]{1,0:T(8,128)S(1)} %add.48), channel_id=1, source_target_pairs={{0,16},{2,18},{4,20},{6,22},{8,24},{10,26},{12,28},{14,30},{16,0},... | collective-permute-start | bytes 442376 | tf_op jit(solution)/shard_map/ppermute | solution.py:744
  49.1 7.7 %copy-start = (f32[71942]{0:T(1024)S(1)}, f32[71942]{0:T(1024)}, u32[]{:S(2)}) copy-start(f32[71942]{0:T(1024)} %refs_3_.1) | copy-start | bytes 863308
  49.1 7.7 %copy-start.7 = (f32[1,72193]{1,0:T(1,128)S(1)}, f32[1,72193]{1,0:T(1,128)}, u32[]{:S(2)}) copy-start(f32[1,72193]{1,0:T(1,128)} %refs_6_.3) | copy-start | bytes 866320
  49.1 7.7 %copy-start.8 = (f32[1,72193]{1,0:T(1,128)S(1)}, f32[1,72193]{1,0:T(1,128)}, u32[]{:S(2)}) copy-start(f32[1,72193]{1,0:T(1,128)} %refs_7_.5) | copy-start | bytes 866320
  53.8 1.4 %collective-permute-start.9 = (f32[288,128]{1,0:T(8,128)S(1)}, f32[288,128]{1,0:T(8,128)S(1)}, u32[]{:S(2)}, u32[]{:S(2)}) collective-permute-start(f32[288,128]{1,0:T(8,128)S(1)} %get-tuple-element.140), channel_id=1, source_target_pairs={{0,1},{1,0},{2,3},{3,2},{4,5},{5,4},{6,7},{7,6},{8,9},{9,8},{10,11... | collective-permute-start | bytes 442376 | tf_op jit(solution)/shard_map/ppermute | solution.py:731
  53.9 2.9 %collective-permute-start.10 = (f32[288,128]{1,0:T(8,128)S(1)}, f32[288,128]{1,0:T(8,128)S(1)}, u32[]{:S(2)}, u32[]{:S(2)}) collective-permute-start(f32[288,128]{1,0:T(8,128)S(1)} %add.49.refs_3_.refs_1_), channel_id=1, source_target_pairs={{0,1},{1,0},{2,3},{3,2},{4,5},{5,4},{6,7},{7,6},{8,9},{9,8},{10,11... | collective-permute-start | bytes 442376 | tf_op jit(solution)/shard_map/ppermute | solution.py:731
  55.3 20.1 %collective-permute-start.11 = (f32[288,128]{1,0:T(8,128)S(1)}, f32[288,128]{1,0:T(8,128)S(1)}, u32[]{:S(2)}, u32[]{:S(2)}) collective-permute-start(f32[288,128]{1,0:T(8,128)S(1)} %add.50), channel_id=1, source_target_pairs={{0,16},{2,18},{4,20},{6,22},{8,24},{10,26},{12,28},{14,30},{16,0},... | collective-permute-start | bytes 442376 | tf_op jit(solution)/shard_map/ppermute | solution.py:744
  75.3 1.4 %collective-permute-start.12 = (f32[288,128]{1,0:T(8,128)S(1)}, f32[288,128]{1,0:T(8,128)S(1)}, u32[]{:S(2)}, u32[]{:S(2)}) collective-permute-start(f32[288,128]{1,0:T(8,128)S(1)} %get-tuple-element.150), channel_id=1, source_target_pairs={{0,1},{1,0},{2,3},{3,2},{4,5},{5,4},{6,7},{7,6},{8,9},{9,8},{10,11... | collective-permute-start | bytes 442376 | tf_op jit(solution)/shard_map/ppermute | solution.py:731
  76.7 6.0 %collective-permute-start.13 = (f32[288,128]{1,0:T(8,128)S(1)}, f32[288,128]{1,0:T(8,128)S(1)}, u32[]{:S(2)}, u32[]{:S(2)}) collective-permute-start(f32[288,128]{1,0:T(8,128)S(1)} %add.52), channel_id=1, source_target_pairs={{0,2},{2,0},{4,6},{6,4},{8,10},{10,8},{12,14},{14,12},{16,18},{18,... | collective-permute-start | bytes 442376 | tf_op jit(solution)/shard_map/ppermute | solution.py:744
  78.3 6.5 %collective-permute-start.18 = (f32[288,128]{1,0:T(8,128)S(1)}, f32[288,128]{1,0:T(8,128)S(1)}, u32[]{:S(2)}, u32[]{:S(2)}) collective-permute-start(f32[288,128]{1,0:T(8,128)S(1)} %add.51), channel_id=1, source_target_pairs={{0,8},{2,10},{4,12},{6,14},{8,0},{10,2},{12,4},{14,6},{16,24},{18,... | collective-permute-start | bytes 442376 | tf_op jit(solution)/shard_map/ppermute | solution.py:744
  82.7 5.2 %collective-permute-start.14 = (f32[288,128]{1,0:T(8,128)S(1)}, f32[288,128]{1,0:T(8,128)S(1)}, u32[]{:S(2)}, u32[]{:S(2)}) collective-permute-start(f32[288,128]{1,0:T(8,128)S(1)} %add.53), channel_id=1, source_target_pairs={{0,4},{2,6},{4,0},{6,2},{8,12},{10,14},{12,8},{14,10},{16,20},{18,... | collective-permute-start | bytes 442376 | tf_op jit(solution)/shard_map/ppermute | solution.py:744
  84.8 5.8 %collective-permute-start.19 = (f32[288,128]{1,0:T(8,128)S(1)}, f32[288,128]{1,0:T(8,128)S(1)}, u32[]{:S(2)}, u32[]{:S(2)}) collective-permute-start(f32[288,128]{1,0:T(8,128)S(1)} %add.57), channel_id=1, source_target_pairs={{0,2},{2,0},{4,6},{6,4},{8,10},{10,8},{12,14},{14,12},{16,18},{18,... | collective-permute-start | bytes 442376 | tf_op jit(solution)/shard_map/ppermute | solution.py:744
  87.9 6.6 %collective-permute-start.15 = (f32[288,128]{1,0:T(8,128)S(1)}, f32[288,128]{1,0:T(8,128)S(1)}, u32[]{:S(2)}, u32[]{:S(2)}) collective-permute-start(f32[288,128]{1,0:T(8,128)S(1)} %add.54), channel_id=1, source_target_pairs={{0,8},{2,10},{4,12},{6,14},{8,0},{10,2},{12,4},{14,6},{16,24},{18,... | collective-permute-start | bytes 442376 | tf_op jit(solution)/shard_map/ppermute | solution.py:744
  90.7 11.7 %copy-start.2 = (f32[71942]{0:T(1024)S(1)}, f32[71942]{0:T(1024)}, u32[]{:S(2)}) copy-start(f32[71942]{0:T(1024)} %refs_6_.2) | copy-start | bytes 863308
  90.7 11.7 %copy-start.3 = (f32[71942]{0:T(1024)S(1)}, f32[71942]{0:T(1024)}, u32[]{:S(2)}) copy-start(f32[71942]{0:T(1024)} %refs_4_.3) | copy-start | bytes 863308
  90.7 11.7 %copy-start.4 = (f32[71942]{0:T(1024)S(1)}, f32[71942]{0:T(1024)}, u32[]{:S(2)}) copy-start(f32[71942]{0:T(1024)} %refs_5_.4) | copy-start | bytes 863308
  90.7 5.2 %collective-permute-start.20 = (f32[288,128]{1,0:T(8,128)S(1)}, f32[288,128]{1,0:T(8,128)S(1)}, u32[]{:S(2)}, u32[]{:S(2)}) collective-permute-start(f32[288,128]{1,0:T(8,128)S(1)} %add.58), channel_id=1, source_target_pairs={{0,4},{2,6},{4,0},{6,2},{8,12},{10,14},{12,8},{14,10},{16,20},{18,... | collective-permute-start | bytes 442376 | tf_op jit(solution)/shard_map/ppermute | solution.py:744
  94.6 6.1 %collective-permute-start.16 = (f32[288,128]{1,0:T(8,128)S(1)}, f32[288,128]{1,0:T(8,128)S(1)}, u32[]{:S(2)}, u32[]{:S(2)}) collective-permute-start(f32[288,128]{1,0:T(8,128)S(1)} %add.55), channel_id=1, source_target_pairs={{0,16},{2,18},{4,20},{6,22},{8,24},{10,26},{12,28},{14,30},{16,0},... | collective-permute-start | bytes 442376 | tf_op jit(solution)/shard_map/ppermute | solution.py:744
  95.9 4.9 %collective-permute-start.21 = (f32[288,128]{1,0:T(8,128)S(1)}, f32[288,128]{1,0:T(8,128)S(1)}, u32[]{:S(2)}, u32[]{:S(2)}) collective-permute-start(f32[288,128]{1,0:T(8,128)S(1)} %add.59.refs_3_), channel_id=1, source_target_pairs={{0,1},{2,3},{4,5},{6,7},{8,9},{10,11},{12,13},{14,15},{16,17},{18,... | collective-permute-start | bytes 442376 | tf_op jit(solution)/shard_map/ppermute | solution.py:735
  100.7 1.7 %collective-permute-start.17 = (f32[288,128]{1,0:T(8,128)S(1)}, f32[288,128]{1,0:T(8,128)S(1)}, u32[]{:S(2)}, u32[]{:S(2)}) collective-permute-start(f32[288,128]{1,0:T(8,128)S(1)} %add.56.refs_1_), channel_id=1, source_target_pairs={{0,1},{1,0},{2,3},{3,2},{4,5},{5,4},{6,7},{7,6},{8,9},{9,8},{10,11... | collective-permute-start | bytes 442376 | tf_op jit(solution)/shard_map/ppermute | solution.py:731

commit v4 on v3

--- a/solution.py
+++ b/solution.py
@@ -29,7 +29,8 @@
 TARGET_LAG = 1
 CRITIC_PART = 1024
 CRITIC_LAG = 3
-ACTOR_TILE = 2048
+FORWARD_PART = 2048
+FORWARD_LAG = 1
 ACTOR_PART = 1024
 ACTOR_LAG = 3
 ONES_ROW = 17
@@ -38,6 +39,9 @@
 FLAT_ROWS = 576
 HALF_ROWS = FLAT_ROWS // 2
 VMEM_BYTES = 24 * 2**20
+SMALL_VMEM_BYTES = 2**21
+FORWARD_VMEM = 8 * 2**20
+ACTOR_VMEM = 16 * 2**20
 
 F32 = jnp.float32
 BF16 = jnp.bfloat16
@@ -440,6 +444,9 @@
     far_lagged,
     own_critic,
     far_critic,
+    actor_weights,
+    mask_actor,
+    units_actor,
     target_out,
     keep,
     send,
@@ -448,10 +455,12 @@
     *rest,
 ):
     next_critic, next_second_t, next_column, next_tail = rest[0:4], rest[4], rest[5], rest[6]
-    inputs, hidden1, tail_sums, flat, spread, tails, next_inputs = rest[7:14]
-    lag_one, lag_two, critic = rest[14:18], rest[18:22], rest[22:26]
-    back = (rest[26], rest[27], None, None)
-    sums = rest[28:31]
+    actor, actor_tail, actor_second_t, actor_third_t = rest[7:11], rest[11], rest[12], rest[13]
+    rest = rest[14:]
+    inputs, hidden1, tail_sums, flat, spread, spread_actor, tails, next_inputs = rest[0:8]
+    lag_one, lag_two, critic = rest[8:12], rest[12:16], rest[16:20]
+    back = (rest[20], rest[21], None, None)
+    sums = rest[22:25]
     core = core_ref[0]
     step = pl.program_id(0)
     width = inputs.shape[1]
@@ -488,6 +497,18 @@
         tails[16:24, 0:1] = tail_column(tail_of(CRITIC, far_lagged))
         tails[24:32, 0:1] = tail_column(chosen(tail_of, 0))
         next_tail[...] = jnp.broadcast_to(tail_column(chosen(tail_of, 1)), (8, LANES))
+        unpack_nets(
+            ACTOR,
+            [lambda: body_of(ACTOR, actor_weights)],
+            flat,
+            mask_actor,
+            units_actor,
+            spread_actor,
+            [actor],
+            [(actor_second_t, None, None, actor_third_t)],
+        )
+        tail = tail_column(tail_of(ACTOR, actor_weights))
+        actor_tail[...] = jnp.broadcast_to(tail, (8, LANES))
 
     next_inputs[0:SDIM, :] = next_states[...]
     next_inputs[ACTION_ROW : ACTION_ROW + ADIM, :] = next_action[...]
@@ -529,28 +550,31 @@
         split_halves(flat, core, keep, send)
 
 
-def critic_kernel(row_total, is_first, is_last, core_ref, *refs):
+def critic_kernel(row_total, start, width, is_first, is_last, core_ref, *refs):
     states, actions, target = refs[0:3]
     critic, second_t, third_column, tail = refs[3:7], refs[7], refs[8], refs[9]
     refs = refs[10:]
     if is_last:
         mask, units = refs[0:2]
         refs = refs[2:]
-    before = () if is_first else refs[0:4]
-    refs = refs[len(before) :]
+    before = ()
+    if not is_first:
+        before = refs[0:4]
+        refs = refs[4:]
     if is_last:
         keep, send, inputs, hidden1 = refs[0:4]
         sums, tail_sums, flat = refs[4:7], refs[7], refs[8]
     else:
         sums, tail_sums, inputs, hidden1 = refs[0:3], refs[3], refs[4], refs[5]
     start_inputs(inputs)
-    hidden1[HID : HID + 16, :] = jnp.ones((16, TILE), BF16)
+    hidden1[HID : HID + 16, :] = jnp.ones((16, width), BF16)
     if is_first:
         clear([*sums, tail_sums])
     for after, value in zip([*sums, tail_sums], before):
         after[...] = value[...]
-    inputs[0:SDIM, :] = states[...]
-    inputs[ACTION_ROW : ACTION_ROW + ADIM, :] = actions[...]
+    first_column = pl.multiple_of(core_ref[0] * target.shape[1] + start, LANES)
+    inputs[0:SDIM, :] = states[:, pl.ds(first_column, width)]
+    inputs[ACTION_ROW : ACTION_ROW + ADIM, :] = actions[:, pl.ds(first_column, width)]
 
     def part(columns):
         return critic_part(
@@ -558,25 +582,62 @@
             (second_t, third_column),
             tail[0:1, 0:1],
             inputs[:, columns].astype(BF16),
-            target[:, columns],
+            target[:, start + columns.start : start + columns.stop],
             2.0 / row_total,
             hidden1.at[:, columns],
             sums,
             tail_sums.at[:, columns],
         )
 
-    staggered([part(columns) for columns in column_parts(TILE, CRITIC_PART)], CRITIC_LAG)
+    staggered([part(columns) for columns in column_parts(width, width // 2)], CRITIC_LAG)
     if is_last:
         last = critic_last_row(tail_sums)
         write_gradient(CRITIC, sums, last, flat, mask, units)
         split_halves(flat, core_ref[0], keep, send)
 
 
+def forward_kernel(
+    core_ref,
+    states,
+    first,
+    second,
+    bias2,
+    third,
+    tail,
+    kept_low1,
+    kept_slope1,
+    kept_low2,
+    kept_slope2,
+    kept_action,
+    inputs,
+):
+    step = pl.program_id(0)
+
+    @pl.when(step == 0)
+    def _():
+        start_inputs(inputs)
+
+    inputs[0:SDIM, :] = states[...]
+    kept_low1[step, HID : HID + 16, :] = jnp.ones((16, TILE), BF16)
+
+    def part(columns):
+        out, slope1, low2, slope2 = yield from forward_kept(
+            (first, second, bias2, third),
+            inputs[:, columns].astype(BF16),
+            kept_low1.at[step, :, columns],
+        )
+        kept_slope1[step, :, columns] = slope1
+        kept_low2[step, :, columns] = low2
+        kept_slope2[step, :, columns] = slope2
+        kept_action[step, :, columns] = jnp.tanh(out + tail[0:8, 0:1])
+
+    staggered([part(columns) for columns in column_parts(TILE, FORWARD_PART)], FORWARD_LAG)
+
+
 def actor_kernel(
     row_total,
     core_ref,
     states,
-    actor_weights,
     mine,
     other,
     own_critic,
@@ -589,21 +650,25 @@
     units_actor,
     mask_critic,
     units_critic,
+    actor_second_t,
+    actor_third_t,
+    kept_low1,
+    kept_slope1,
+    kept_low2,
+    kept_slope2,
+    kept_action,
     keep,
     send,
     inputs,
-    hidden1,
     tail_sums,
     flat,
     gradient,
-    spread_actor,
     spread_critic,
     tails,
     *rest,
 ):
-    actor, actor_back = rest[0:4], (rest[4], None, None, rest[5])
-    judge, judge_back = rest[6:10], (rest[10], rest[11], rest[12], None)
-    sums = rest[13:16]
+    judge, judge_back = rest[0:4], (rest[4], rest[5], rest[6], None)
+    sums = rest[7:10]
     core = core_ref[0]
     step = pl.program_id(0)
     width = inputs.shape[1]
@@ -611,20 +676,8 @@
     @pl.when(step == 0)
     def _():
         start_inputs(inputs)
-        hidden1[HID : HID + 16, :] = jnp.ones((16, width), BF16)
         clear(sums)
         clear([tail_sums])
-        unpack_nets(
-            ACTOR,
-            [lambda: body_of(ACTOR, actor_weights)],
-            flat,
-            mask_actor,
-            units_actor,
-            spread_actor,
-            [actor],
-            [actor_back],
-        )
-        tails[0:8, 0:1] = tail_column(tail_of(ACTOR, actor_weights))
         join_halves(core, mine, other, gradient)
 
         def chosen(part, own, far):
@@ -652,20 +705,15 @@
         tails[8:16, 0:1] = tail_column(tail)
 
     inputs[0:SDIM, :] = states[...]
+    inputs[ACTION_ROW:IN_ROWS, :] = kept_action[step]
     judge_second_t, judge_column, judge_rows, unused = judge_back
-    actor_second_t, unused, unused, actor_third_t = actor_back
     start = jnp.full((HID, LANES), -1.0 / row_total, F32).astype(BF16).astype(F32)
     start = judge_column[...] * start
 
     def part(columns):
         part_width = columns.stop - columns.start
-        state_low = inputs[:, columns].astype(BF16)
-        hidden = hidden1.at[:, columns]
-        out, slope1, low2, slope2 = yield from forward_kept(actor, state_low, hidden)
-        action = jnp.tanh(out + tails[0:8, 0:1])
-        inputs[ACTION_ROW:IN_ROWS, columns] = action
         joined = inputs[:, columns].astype(BF16)
-        yield
+        action = kept_action[step, :, columns]
         out, judge_slope1, unused, judge_slope2 = yield from forward_kept(judge, joined)
         tail_sums[8:9, columns] += out[0:1] + tails[8:9, 0:1]
         grad2 = (wide(start, part_width) * judge_slope2).astype(BF16)
@@ -681,15 +729,15 @@
         yield
         grad_low2 = dot(actor_third_t[...], grad3_low)
         yield
-        grad2 = (grad_low2 * slope2).astype(BF16)
-        sums[2][...] += dot_nt(grad3_low, low2)
+        grad2 = (grad_low2 * kept_slope2[step, :, columns]).astype(BF16)
+        sums[2][...] += dot_nt(grad3_low, kept_low2[step, :, columns])
         yield
         grad_low1 = dot(actor_second_t[...], grad2)
         yield
-        grad1 = (grad_low1 * slope1).astype(BF16)
-        sums[1][...] += dot_nt(hidden[...], grad2)
+        grad1 = (grad_low1 * kept_slope1[step, :, columns]).astype(BF16)
+        sums[1][...] += dot_nt(kept_low1[step, :, columns], grad2)
         yield
-        sums[0][...] += dot_nt(state_low, grad1)
+        sums[0][...] += dot_nt(joined, grad1)
 
     staggered([part(columns) for columns in column_parts(width, ACTOR_PART)], ACTOR_LAG)
 
@@ -742,6 +790,22 @@
 def partner(value, mask):
     pairs = [(source, source ^ mask) for source in range(lax.axis_size("dp"))]
     return lax.ppermute(value, "dp", pairs)
+
+
+def plus_kernel(left, right, out):
+    out[...] = left[...] + right[...]
+
+
+def plus(left, right):
+    vector = pl.BlockSpec(memory_space=pltpu.VMEM)
+    return pl.pallas_call(
+        plus_kernel,
+        in_specs=[vector] * 2,
+        out_specs=vector,
+        out_shape=jax.ShapeDtypeStruct(left.shape, F32),
+        compiler_params=pltpu.CompilerParams(vmem_limit_bytes=SMALL_VMEM_BYTES),
+        name="plus",
+    )(left, right)
 
 
 def in_hbm(value):
@@ -855,18 +919,26 @@
         "next_action",
         2 * tiles * unit_flops,
     )(core, in_hbm(next_states), in_hbm(smoothing), target_actor)
+    actor_passed = Weights.shapes + (((8, LANES), F32), Weights.back_shapes[0], Weights.back_shapes[3])
+    actor_shapes = [jax.ShapeDtypeStruct(shape, dtype) for shape, dtype in actor_passed]
     target, keep_one, send_one, *rest = call(
         lambda *refs: target_kernel(row_total, *refs),
         local_rows // 2 // TARGET_TILE,
         [mine(rows, None, TARGET_TILE) for rows in (SDIM, ADIM, 1, SDIM, 1)]
         + [local(ADIM, None, TARGET_TILE)]
-        + [critic_flat] * 4,
-        [local(1, None, TARGET_TILE), half, half] + place_specs + passed_specs,
+        + [critic_flat] * 4
+        + [actor_flat]
+        + place_specs,
+        [local(1, None, TARGET_TILE), half, half]
+        + place_specs
+        + passed_specs
+        + [whole(None)] * len(actor_shapes),
         [jax.ShapeDtypeStruct((1, local_rows // 2), F32), half_shape, half_shape]
         + places(CRITIC)
-        + passed_shapes,
+        + passed_shapes
+        + actor_shapes,
         tile_scratch(TARGET_TILE)
-        + [spread(CRITIC, 4), tails, pltpu.VMEM((IN_ROWS, TARGET_TILE), F32)]
+        + [spread(CRITIC, 4), spread(ACTOR, 1), tails, pltpu.VMEM((IN_ROWS, TARGET_TILE), F32)]
         + net * 3
         + back[0:2]
         + sums,
@@ -884,80 +956,112 @@
         far_lagged,
         critic_weights,
         far_weights,
+        actor_weights,
+        *places_actor,
     )
-    places_critic, critic_two = rest[0:2], rest[2:]
-
+    places_critic, critic_two, actor_net = rest[0:2], rest[2 : 2 + len(passed)], rest[2 + len(passed) :]
+    kept_shapes = [
+        pltpu.VMEM((tiles, rows, TILE), dtype)
+        for rows, dtype in ((HID + 16, BF16), (HID, F32), (HID, BF16), (HID, F32), (8, F32))
+    ]
+    kept_specs = [whole(None)] * len(kept_shapes)
+
+    columns = local_rows // 2
+    step_columns = columns // 3 // 512 * 512
+    pieces = [(columns - 2 * step_columns, 0)]
+    pieces = pieces + [(step_columns, columns - i * step_columns) for i in (2, 1)]
+    tail_shapes = (((16, pieces[0][0]), F32),)
     carried = SUM_SHAPES + tail_shapes
     carried_specs = [whole(shape) for shape, dtype in carried]
     carried_shapes = [jax.ShapeDtypeStruct(shape, dtype) for shape, dtype in carried]
 
-    def second_critic(tile, tied_target, state):
-        is_first, is_last = tile == 0, tile == tiles - 1
-        in_specs = [mine(SDIM, tile), mine(ADIM, tile), local(1, tile)] + passed_specs
+    def second_critic(piece, tied_target, state):
+        is_first, is_last = piece == 0, piece == len(pieces) - 1
+        width, start = pieces[piece]
         operands = [core, states, actions, tied_target, *critic_two]
+        scratch = tile_scratch(width)[0:2]
+        out_shape = carried_shapes
         if is_last:
-            in_specs = in_specs + place_specs
             operands = operands + places_critic
-        scratch = tile_scratch(TILE)[0:2]
-        out_specs, out_shape = carried_specs, carried_shapes
+            out_shape = [half_shape, half_shape]
+            scratch = scratch + sums + scratch_of(tail_shapes) + [flat]
         aliases = []
-        if not is_first:
-            aliases = [(1 + len(in_specs) + i, i) for i in range(len(carried))]
-            in_specs = in_specs + carried_specs
-        if is_last:
-            out_specs, out_shape, aliases = [half, half], [half_shape, half_shape], []
-            scratch = scratch + sums + scratch_of(tail_shapes) + [flat]
+        if not is_first and not is_last:
+            aliases = [(len(operands) + i, i) for i in range(len(state))]
+        operands = operands + list(state)
         return call(
-            lambda *refs: critic_kernel(row_total, is_first, is_last, *refs),
+            lambda *refs: critic_kernel(row_total, start, width, is_first, is_last, *refs),
             1,
-            in_specs,
-            out_specs,
+            [whole(None)] * (len(operands) - 1),
+            [whole(None)] * len(out_shape),
             out_shape,
             scratch,
             "second_critic",
             8 * unit_flops,
             aliases,
-        )(*operands, *state)
+        )(*operands)
+
+    def actor_forward(tied_tail):
+        return call(
+            forward_kernel,
+            tiles,
+            [mine(SDIM)] + [whole(None)] * 5,
+            kept_specs,
+            kept_shapes,
+            [pltpu.VMEM((IN_ROWS, TILE), F32)],
+            "actor_forward",
+            12 * unit_flops,
+            vmem=FORWARD_VMEM,
+        )(core, states, *actor_net[0:4], tied_tail)
 
     masks = chip_masks()
     state = ()
     one = keep_one + twin_swap(send_one)
-    tile = 0
+    piece = 0
     for mask in masks:
         moved = partner(one, mask)
-        if tile < tiles:
+        if mask == masks[-1]:
+            one, tied_tail = lax.optimization_barrier((one, actor_net[4]))
+            kept = actor_forward(tied_tail)
+            *kept, last = kept
+            one, last = lax.optimization_barrier((plus(one, moved), last))
+            kept = [*kept, last]
+        elif piece < len(pieces):
             one, tied_target = lax.optimization_barrier((one, target))
-            state = second_critic(tile, tied_target, state)
-            tile += 1
-        one = one + moved
-        one, state = lax.optimization_barrier((one, state))
-    while tile < tiles:
-        state = second_critic(tile, target, state)
-        tile += 1
+            state = second_critic(piece, tied_target, state)
+            piece += 1
+            one, state = lax.optimization_barrier((one + moved, state))
+        else:
+            one = one + moved
+    while piece < len(pieces):
+        state = second_critic(piece, target, state)
+        piece += 1
     keep_two, send_two = state
     one_other = twin_swap(one)
-    two = keep_two + twin_swap(send_two)
+    two = plus(keep_two, twin_swap(send_two))
     two_moved = partner(two, masks[-1])
     two, one, one_other = lax.optimization_barrier((two, one, one_other))
     keep_actor, send_actor = call(
         lambda *refs: actor_kernel(row_total, *refs),
-        local_rows // 2 // ACTOR_TILE,
-        [mine(SDIM, None, ACTOR_TILE), actor_flat, half, half] + [critic_flat] * 6 + place_specs * 2,
+        tiles,
+        [mine(SDIM), half, half]
+        + [critic_flat] * 6
+        + place_specs * 2
+        + [whole(None)] * 2
+        + kept_specs,
         [half, half],
         [half_shape, half_shape],
-        tile_scratch(ACTOR_TILE)
-        + [pltpu.VMEM((FLAT_ROWS, LANES), F32), spread(ACTOR, 1), spread(CRITIC, 1), tails]
-        + net
-        + [back[0], back[3]]
+        [tile_scratch(TILE)[i] for i in (0, 2, 3)]
+        + [pltpu.VMEM((FLAT_ROWS, LANES), F32), spread(CRITIC, 1), tails]
         + net
         + back[0:3]
         + sums,
         "actor",
-        10 * tiles * unit_flops,
+        8 * tiles * unit_flops,
+        vmem=ACTOR_VMEM,
     )(
         core,
         states,
-        actor_weights,
         one,
         one_other,
         critic_weights,
@@ -968,6 +1072,8 @@
         far_second,
         *places_actor,
         *places_critic,
+        *actor_net[5:7],
+        *[pltpu.with_memory_space_constraint(value, pltpu.VMEM) for value in kept],
     )
     actor_moved = twin_swap(send_actor)
     two = two + two_moved

time: 105 us -> 102 us (0.971)
  waiting for transfers between devices: 20.2 us -> 17.2 us
  Pallas kernels: 55.8 us -> 58.1 us
  starting transfers between devices: 25.8 us -> 24.2 us
    ppermute x12, waiting for transfers between devices: 17 us -> 13.7 us  [partner(): return lax.ppermute(value, 'dp', pairs)]
    pallas_call x5 -> x7, Pallas kernels: 28.8 us -> 31 us  [the longest x1 14.4 us: on_device(): call(lambda *refs: actor_kernel(row_total, *refs), tiles, [mine(SDIM), ha...]
    ppermute x12, starting transfers between devices: 22.2 us -> 20.9 us  [partner(): return lax.ppermute(value, 'dp', pairs)]
  transfers between devices with their start and end apart: 22 -> 22, of which waited for: 13 -> 12; matrix products, arithmetic and copies ran while one was open for 0% -> 0% of each run, Pallas kernels for 34% -> 37%
where the time goes in v4:
time: 102 us
  Pallas kernels  58.1 us (57%)
  starting transfers between devices  24.2 us (24%)
  waiting for transfers between devices  17.2 us (17%)
  between operations  1.11 us (1%)
    ppermute x12, starting transfers between devices, partner(): return lax.ppermute(value, 'dp', pairs)  20.9 us
    pallas_call x1, Pallas kernels, on_device(): call(lambda *refs: target_kernel(row_total, *refs), local_rows // 2 // TA...  18.7 us
    pallas_call x1, Pallas kernels, on_device(): call(lambda *refs: actor_kernel(row_total, *refs), tiles, [mine(SDIM), ha...  14.4 us
    ppermute x12, waiting for transfers between devices, partner(): return lax.ppermute(value, 'dp', pairs)  13.7 us
    pallas_call x3, Pallas kernels, second_critic(): call(lambda *refs: critic_kernel(row_total, start, width, is_first, is_la...  10.5 us
    pallas_call x1, Pallas kernels, actor_forward(): call(forward_kernel, tiles, [mine(SDIM)] + [whole(None)] * 5, kept_specs,...  5.98 us
    pallas_call x1, Pallas kernels, on_device(): call(action_kernel, tiles, [mine(SDIM), mine(ADIM), actor_flat], [local(A...  5.23 us
    ppermute x9, waiting for transfers between devices, twin_swap(): return lax.ppermute(value, 'twin', [(0, 1), (1, 0)])  3.47 us
  transfers between devices with their start and end apart: 22, of which 12 were waited for; matrix products, arithmetic and copies ran while one was open for 0% of the time, Pallas kernels for 37%

profile of v4, /device:TPU:0, one launch (start us, length us, event | category | flops | bytes accessed | tf_op | source)
XLA Modules:
  0.0 101.9 jit_solution(9720362515840961749)
XLA Ops:
  0.6 0.5 collective-permute-start
  1.2 0.1 collective-permute-start.1
  1.2 0.4 collective-permute-start.2
  1.7 0.1 collective-permute-start.3
  1.8 1.0 copy-done
  2.7 5.2 %next_action.1 = (f32[6,8192]{1,0:T(8,128)S(1)}, f32[32,2176]{1,0:T(8,128)S(1)}, bf16[2176,128]{1,0:T(8,128)(2,1)S(1)}) custom-call(s32[1]{0:T(128)} %bitcast.core_ref.refs_0_, f32[17,16384]{1,0:T(8,128)} %refs_4_.3, f32[6,16384]{1,0:T(8,128)} %smoothing.1, f32[71942]{0:T(1024)S(1)} %copy-done), custom_call_target="tpu_custom_call" | custom-call | flops 2147483648 | bytes 1000000 | tf_op jit(solution)/shard_map/next_action/pallas_call | solution.py:912
  8.0 0.0 copy-start.9
  8.0 0.0 copy-start.10
  8.0 18.7 %target_and_first_critic.1 = (f32[1,8192]{1,0:T(1,128)S(1)}, f32[288,128]{1,0:T(8,128)S(1)}, f32[288,128]{1,0:T(8,128)S(1)}, f32[32,2944]{1,0:T(8,128)S(1)}, bf1...) custom-call(s32[1]{0:T(128)} %bitcast.core_ref.refs_0_, ...), custom_call_target="tpu_custom_call" | custom-call | flops 15032385536 | bytes 1000000 | tf_op jit(solution)/shard_map/target_and_first_critic/pallas_call | solution.py:924
  26.8 0.5 collective-permute-start.4
  27.3 1.0 collective-permute-done.4
  28.3 2.9 %collective-permute-start.5 = (f32[288,128]{1,0:T(8,128)S(1)}, f32[288,128]{1,0:T(8,128)S(1)}, u32[]{:S(2)}, u32[]{:S(2)}) collective-permute-start(f32[288,128]{1,0:T(8,128)S(1)} %add.39), channel_id=1, source_target_pairs={{0,2},{2,0},{4,6},{6,4},{8,10},{10,8},{12,14},{14,12},{16,18},{18,... | collective-permute-start | bytes 442376 | tf_op jit(solution)/shard_map/ppermute | solution.py:792
  31.2 3.7 %second_critic.3 = (f32[32,256]{1,0:T(8,128)S(1)}, f32[272,256]{1,0:T(8,128)S(1)}, f32[16,256]{1,0:T(8,128)S(1)}, f32[16,3072]{1,0:T(8,128)S(1)}) custom-call(s32[1]{0:T(128)} %bitcast.core_ref.refs_0_, f32[17,16384]{1,0:T(8,128)S(1)} %copy-done.9, f32[6,16384]{1,0:T(8,128)S(1)} %copy-done.10, f32[1,8192]{1,0:T(1,128)S(1)} %get-tuple-element.126.refs_3_, ...), custom_call_target="tpu_custom_call" | custom-call | flops 2147483648 | bytes 1000000 | tf_op jit(solution)/shard_map/second_critic/pallas_call | solution.py:992
  34.9 0.5 collective-permute-done.5
  35.4 1.8 %collective-permute-start.6 = (f32[288,128]{1,0:T(8,128)S(1)}, f32[288,128]{1,0:T(8,128)S(1)}, u32[]{:S(2)}, u32[]{:S(2)}) collective-permute-start(f32[288,128]{1,0:T(8,128)S(1)} %add.40), channel_id=1, source_target_pairs={{0,4},{2,6},{4,0},{6,2},{8,12},{10,14},{12,8},{14,10},{16,20},{18,... | collective-permute-start | bytes 442376 | tf_op jit(solution)/shard_map/ppermute | solution.py:792
  37.3 3.1 %second_critic.4 = (f32[32,256]{1,0:T(8,128)S(1)}, f32[272,256]{1,0:T(8,128)S(1)}, f32[16,256]{1,0:T(8,128)S(1)}, f32[16,3072]{1,0:T(8,128)S(1)}) custom-call(s32[1]{0:T(128)} %bitcast.core_ref.refs_0_, f32[17,16384]{1,0:T(8,128)S(1)} %copy-done.9, ...), custom_call_target="tpu_custom_call", output_to_operand_aliasing={{0}: (11, {}), {1}: (12, {}), {2}: (13, {}), {3}: (14, {})} | custom-call | flops 2147483648 | bytes 1000000 | tf_op jit(solution)/shard_map/second_critic/pallas_call | solution.py:992
  40.4 0.5 collective-permute-done.6
  40.9 1.6 %collective-permute-start.7 = (f32[288,128]{1,0:T(8,128)S(1)}, f32[288,128]{1,0:T(8,128)S(1)}, u32[]{:S(2)}, u32[]{:S(2)}) collective-permute-start(f32[288,128]{1,0:T(8,128)S(1)} %add.41), channel_id=1, source_target_pairs={{0,8},{2,10},{4,12},{6,14},{8,0},{10,2},{12,4},{14,6},{16,24},{18,... | collective-permute-start | bytes 442376 | tf_op jit(solution)/shard_map/ppermute | solution.py:792
  42.5 3.7 %second_critic.5 = (f32[288,128]{1,0:T(8,128)S(1)}, f32[288,128]{1,0:T(8,128)S(1)}) custom-call(s32[1]{0:T(128)} %bitcast.core_ref.refs_0_, f32[17,16384]{1,0:T(8,128)S(1)} %copy-done.9, f32[6,16384]{1,0:T(8,128)S(1)} %copy-done.10, f32[1,8192]{1,0:T(1,128)S(1)} %get-tuple-element.126.refs_3_, bf16[256,32]{1,0:T(8,128)(2,1)S(1)} %get-tuple-element.102.refs_4_, ...), custom_call_target="tpu_custom_call" | custom-call | flops 2147483648 | bytes 1000000 | tf_op jit(solution)/shard_map/second_critic/pallas_call | solution.py:992
  46.3 0.1 collective-permute-start.8
  46.4 2.7 %collective-permute-start.9 = (f32[288,128]{1,0:T(8,128)S(1)}, f32[288,128]{1,0:T(8,128)S(1)}, u32[]{:S(2)}, u32[]{:S(2)}) collective-permute-start(f32[288,128]{1,0:T(8,128)S(1)} %add.42.left), channel_id=1, source_target_pairs={{0,16},{2,18},{4,20},{6,22},{8,24},{10,26},{12,28},{14,30},{16,0},... | collective-permute-start | bytes 442376 | tf_op jit(solution)/shard_map/ppermute | solution.py:792
  49.0 6.0 %actor_forward.1 = (bf16[4,272,2048]{2,1,0:T(8,128)(2,1)S(1)}, f32[4,256,2048]{2,1,0:T(8,128)S(1)}, bf16[4,256,2048]{2,1,0:T(8,128)(2,1)S(1)}, f32[4,256,2048]{2,1,0:T(8,128)S(1)}, f32[4,8,2048]{2,1,0:T(8,128)S(1)}) custom-call(s32[1]{0:T(128)} %bitcast.core_ref.refs_0_, f32[17,16384]{1,0:T(8,128)S(1)} %copy-done.9, ...), custom_call_target="tpu_custom_call" | custom-call | flops 3221225472 | bytes 1000000 | tf_op jit(solution)/shard_map/actor_forward/pallas_call | solution.py:1005
  55.0 1.7 %collective-permute-done.9.right = f32[288,128]{1,0:T(8,128)S(1)} collective-permute-done((f32[288,128]{1,0:T(8,128)S(1)}, f32[288,128]{1,0:T(8,128)S(1)}, u32[]{:S(2)}, u32[]{:S(2)}) %collective-permute-start.9) | collective-permute-done | bytes 147488 | tf_op jit(solution)/shard_map/ppermute | solution.py:792
  56.7 0.1 collective-permute-start.10
  56.8 0.1 collective-permute-start.11
  56.9 1.2 %collective-permute-done.10.refs_3_.refs_2_ = f32[288,128]{1,0:T(8,128)S(1)} collective-permute-done((f32[288,128]{1,0:T(8,128)S(1)}, f32[288,128]{1,0:T(8,128)S(1)}, u32[]{:S(2)}, u32[]{:S(2)}) %collective-permute-start.10) | collective-permute-done | bytes 147488 | tf_op jit(solution)/shard_map/ppermute | solution.py:779
  58.2 14.4 %actor.1 = (f32[288,128]{1,0:T(8,128)S(1)}, f32[288,128]{1,0:T(8,128)S(1)}) custom-call(s32[1]{0:T(128)} %bitcast.core_ref.refs_0_, f32[17,16384]{1,0:T(8,128)S(1)} %copy-done.9, f32[288,128]{1,0:T(8,128)S(1)} %plus.3.refs_2_.refs_1_, f32[288,128]{1,0:T(8,128)S(1)} %collective-permute-done.10.refs_3_.refs_2_, f32[1,72193]{1,0:T(1,128)S(1)} %copy-done.6, ...), custom_call_target="tpu_custom_call" | custom-call | flops 8589934592 | bytes 1000000 | tf_op jit(solution)/shard_map/actor/pallas_call | solution.py:1044
  72.6 0.0 copy-start.3
  72.6 0.0 copy-start.4
  72.6 0.2 collective-permute-start.12
  72.9 1.2 %collective-permute-done.12 = f32[288,128]{1,0:T(8,128)S(1)} collective-permute-done((f32[288,128]{1,0:T(8,128)S(1)}, f32[288,128]{1,0:T(8,128)S(1)}, u32[]{:S(2)}, u32[]{:S(2)}) %collective-permute-start.12) | collective-permute-done | bytes 147488 | tf_op jit(solution)/shard_map/ppermute | solution.py:779
  74.1 1.6 %collective-permute-start.13 = (f32[288,128]{1,0:T(8,128)S(1)}, f32[288,128]{1,0:T(8,128)S(1)}, u32[]{:S(2)}, u32[]{:S(2)}) collective-permute-start(f32[288,128]{1,0:T(8,128)S(1)} %add.44), channel_id=1, source_target_pairs={{0,2},{2,0},{4,6},{6,4},{8,10},{10,8},{12,14},{14,12},{16,18},{18,... | collective-permute-start | bytes 442376 | tf_op jit(solution)/shard_map/ppermute | solution.py:792
  75.6 3.0 %collective-permute-start.18 = (f32[288,128]{1,0:T(8,128)S(1)}, f32[288,128]{1,0:T(8,128)S(1)}, u32[]{:S(2)}, u32[]{:S(2)}) collective-permute-start(f32[288,128]{1,0:T(8,128)S(1)} %add.43), channel_id=1, source_target_pairs={{0,8},{2,10},{4,12},{6,14},{8,0},{10,2},{12,4},{14,6},{16,24},{18,... | collective-permute-start | bytes 442376 | tf_op jit(solution)/shard_map/ppermute | solution.py:792
  78.6 1.4 %collective-permute-done.13 = f32[288,128]{1,0:T(8,128)S(1)} collective-permute-done((f32[288,128]{1,0:T(8,128)S(1)}, f32[288,128]{1,0:T(8,128)S(1)}, u32[]{:S(2)}, u32[]{:S(2)}) %collective-permute-start.13) | collective-permute-done | bytes 147488 | tf_op jit(solution)/shard_map/ppermute | solution.py:792
  80.1 1.6 %collective-permute-start.14 = (f32[288,128]{1,0:T(8,128)S(1)}, f32[288,128]{1,0:T(8,128)S(1)}, u32[]{:S(2)}, u32[]{:S(2)}) collective-permute-start(f32[288,128]{1,0:T(8,128)S(1)} %add.45), channel_id=1, source_target_pairs={{0,4},{2,6},{4,0},{6,2},{8,12},{10,14},{12,8},{14,10},{16,20},{18,... | collective-permute-start | bytes 442376 | tf_op jit(solution)/shard_map/ppermute | solution.py:792
  81.7 0.9 collective-permute-done.18
  82.6 0.7 collective-permute-start.19
  83.2 2.0 %collective-permute-done.14 = f32[288,128]{1,0:T(8,128)S(1)} collective-permute-done((f32[288,128]{1,0:T(8,128)S(1)}, f32[288,128]{1,0:T(8,128)S(1)}, u32[]{:S(2)}, u32[]{:S(2)}) %collective-permute-start.14) | collective-permute-done | bytes 147488 | tf_op jit(solution)/shard_map/ppermute | solution.py:792
  85.3 3.1 %collective-permute-start.15 = (f32[288,128]{1,0:T(8,128)S(1)}, f32[288,128]{1,0:T(8,128)S(1)}, u32[]{:S(2)}, u32[]{:S(2)}) collective-permute-start(f32[288,128]{1,0:T(8,128)S(1)} %add.46), channel_id=1, source_target_pairs={{0,8},{2,10},{4,12},{6,14},{8,0},{10,2},{12,4},{14,6},{16,24},{18,... | collective-permute-start | bytes 442376 | tf_op jit(solution)/shard_map/ppermute | solution.py:792
  88.4 1.6 %collective-permute-start.20 = (f32[288,128]{1,0:T(8,128)S(1)}, f32[288,128]{1,0:T(8,128)S(1)}, u32[]{:S(2)}, u32[]{:S(2)}) collective-permute-start(f32[288,128]{1,0:T(8,128)S(1)} %add.50), channel_id=1, source_target_pairs={{0,4},{2,6},{4,0},{6,2},{8,12},{10,14},{12,8},{14,10},{16,20},{18,... | collective-permute-start | bytes 442376 | tf_op jit(solution)/shard_map/ppermute | solution.py:792
  90.0 2.2 %collective-permute-done.15 = f32[288,128]{1,0:T(8,128)S(1)} collective-permute-done((f32[288,128]{1,0:T(8,128)S(1)}, f32[288,128]{1,0:T(8,128)S(1)}, u32[]{:S(2)}, u32[]{:S(2)}) %collective-permute-start.15) | collective-permute-done | bytes 147488 | tf_op jit(solution)/shard_map/ppermute | solution.py:792
  92.3 0.3 collective-permute-start.16
  92.6 1.1 %collective-permute-done.20 = f32[288,128]{1,0:T(8,128)S(1)} collective-permute-done((f32[288,128]{1,0:T(8,128)S(1)}, f32[288,128]{1,0:T(8,128)S(1)}, u32[]{:S(2)}, u32[]{:S(2)}) %collective-permute-start.20) | collective-permute-done | bytes 147488 | tf_op jit(solution)/shard_map/ppermute | solution.py:792
  93.7 1.3 %collective-permute-start.21 = (f32[288,128]{1,0:T(8,128)S(1)}, f32[288,128]{1,0:T(8,128)S(1)}, u32[]{:S(2)}, u32[]{:S(2)}) collective-permute-start(f32[288,128]{1,0:T(8,128)S(1)} %add.51.refs_3_), channel_id=1, source_target_pairs={{0,1},{2,3},{4,5},{6,7},{8,9},{10,11},{12,13},{14,15},{16,17},{18,... | collective-permute-start | bytes 442376 | tf_op jit(solution)/shard_map/ppermute | solution.py:783
  95.0 3.4 %collective-permute-done.16 = f32[288,128]{1,0:T(8,128)S(1)} collective-permute-done((f32[288,128]{1,0:T(8,128)S(1)}, f32[288,128]{1,0:T(8,128)S(1)}, u32[]{:S(2)}, u32[]{:S(2)}) %collective-permute-start.16) | collective-permute-done | bytes 147488 | tf_op jit(solution)/shard_map/ppermute | solution.py:792
  98.4 0.1 collective-permute-start.17
  98.5 1.6 %critic_step.1 = (f32[1,72193]{1,0:T(1,128)}, f32[1,72193]{1,0:T(1,128)}, f32[1,72193]{1,0:T(1,128)}, f32[1,72193]{1,0:T(1,128)}, f32[1]{0:T(128)}) custom-call(s32[1]{0:T(128)} %bitcast.core_ref.refs_0_, f32[288,128]{1,0:T(8,128)S(1)} %plus.3.refs_2_.refs_1_, f32[288,128]{1,0:T(8,128)S(1)} %collective-permute-done.10.refs_3_.refs_2_, ...), custom_call_target="tpu_custom_call" | custom-call | tf_op jit(solution)/shard_map/critic_step/pallas_call | solution.py:1093
  100.1 1.5 %actor_step.1 = (f32[71942]{0:T(1024)}, f32[71942]{0:T(1024)}, f32[71942]{0:T(1024)}, f32[71942]{0:T(1024)}, f32[1]{0:T(128)}) custom-call(s32[1]{0:T(128)} %bitcast.core_ref.refs_0_, f32[288,128]{1,0:T(8,128)S(1)} %add.48.refs_1_, f32[288,128]{1,0:T(8,128)S(1)} %collective-permute-done.17.refs_2_, f32[71942]{0:T(1024)S(1)} %copy-done.2, ...), custom_call_target="tpu_custom_call" | custom-call | tf_op jit(solution)/shard_map/actor_step/pallas_call | solution.py:1093
  (42 shorter events, 0.3 us)
Async XLA Ops:
  0.6 7.3 %collective-permute-start = (f32[1,72193]{1,0:T(1,128)}, f32[1,72193]{1,0:T(1,128)S(1)}, u32[]{:S(2)}, u32[]{:S(2)}) collective-permute-start(f32[1,72193]{1,0:T(1,128)} %refs_8_.3), channel_id=1, source_target_pairs={{0,1},{1,0},{2,3},{3,2},{4,5},{5,4},{6,7},{7,6},{8,9},{9,8},{10,11... | collective-permute-start | bytes 866324 | tf_op jit(solution)/shard_map/ppermute | solution.py:779
  1.2 6.8 %collective-permute-start.1 = (f32[1,72193]{1,0:T(1,128)}, f32[1,72193]{1,0:T(1,128)S(1)}, u32[]{:S(2)}, u32[]{:S(2)}) collective-permute-start(f32[1,72193]{1,0:T(1,128)} %refs_5_.3), channel_id=1, source_target_pairs={{0,1},{1,0},{2,3},{3,2},{4,5},{5,4},{6,7},{7,6},{8,9},{9,8},{10,11... | collective-permute-start | bytes 866324 | tf_op jit(solution)/shard_map/ppermute | solution.py:779
  1.2 6.7 %collective-permute-start.2 = (f32[1,72193]{1,0:T(1,128)}, f32[1,72193]{1,0:T(1,128)S(1)}, u32[]{:S(2)}, u32[]{:S(2)}) collective-permute-start(f32[1,72193]{1,0:T(1,128)} %refs_6_.5), channel_id=1, source_target_pairs={{0,1},{1,0},{2,3},{3,2},{4,5},{5,4},{6,7},{7,6},{8,9},{9,8},{10,11... | collective-permute-start | bytes 866324 | tf_op jit(solution)/shard_map/ppermute | solution.py:779
  1.7 6.3 %collective-permute-start.3 = (f32[1,72193]{1,0:T(1,128)}, f32[1,72193]{1,0:T(1,128)S(1)}, u32[]{:S(2)}, u32[]{:S(2)}) collective-permute-start(f32[1,72193]{1,0:T(1,128)} %refs_7_.3), channel_id=1, source_target_pairs={{0,1},{1,0},{2,3},{3,2},{4,5},{5,4},{6,7},{7,6},{8,9},{9,8},{10,11... | collective-permute-start | bytes 866324 | tf_op jit(solution)/shard_map/ppermute | solution.py:779
  1.8 1.0 copy-start
  2.7 5.3 %copy-start.2 = (f32[71942]{0:T(1024)S(1)}, f32[71942]{0:T(1024)}, u32[]{:S(2)}) copy-start(f32[71942]{0:T(1024)} %refs_3_.1) | copy-start | bytes 863308
  2.7 5.3 %copy-start.5 = (f32[1,72193]{1,0:T(1,128)S(1)}, f32[1,72193]{1,0:T(1,128)}, u32[]{:S(2)}) copy-start(f32[1,72193]{1,0:T(1,128)} %refs_8_.3) | copy-start | bytes 866320
  2.7 5.3 %copy-start.6 = (f32[1,72193]{1,0:T(1,128)S(1)}, f32[1,72193]{1,0:T(1,128)}, u32[]{:S(2)}) copy-start(f32[1,72193]{1,0:T(1,128)} %refs_5_.3) | copy-start | bytes 866320
  8.0 23.2 %copy-start.9 = (f32[17,16384]{1,0:T(8,128)S(1)}, f32[17,16384]{1,0:T(8,128)}, u32[]{:S(2)}) copy-start(f32[17,16384]{1,0:T(8,128)} %refs_1_.9) | copy-start | bytes 3342340
  8.0 23.2 %copy-start.10 = (f32[6,16384]{1,0:T(8,128)S(1)}, f32[6,16384]{1,0:T(8,128)}, u32[]{:S(2)}) copy-start(f32[6,16384]{1,0:T(8,128)} %refs_2_.7) | copy-start | bytes 1179652
  26.8 1.5 %collective-permute-start.4 = (f32[288,128]{1,0:T(8,128)S(1)}, f32[288,128]{1,0:T(8,128)S(1)}, u32[]{:S(2)}, u32[]{:S(2)}) collective-permute-start(f32[288,128]{1,0:T(8,128)S(1)} %get-tuple-element.98), channel_id=1, source_target_pairs={{0,1},{1,0},{2,3},{3,2},{4,5},{5,4},{6,7},{7,6},{8,9},{9,8},{10,11... | collective-permute-start | bytes 442376 | tf_op jit(solution)/shard_map/ppermute | solution.py:779
  28.3 7.1 %collective-permute-start.5 = (f32[288,128]{1,0:T(8,128)S(1)}, f32[288,128]{1,0:T(8,128)S(1)}, u32[]{:S(2)}, u32[]{:S(2)}) collective-permute-start(f32[288,128]{1,0:T(8,128)S(1)} %add.39), channel_id=1, source_target_pairs={{0,2},{2,0},{4,6},{6,4},{8,10},{10,8},{12,14},{14,12},{16,18},{18,... | collective-permute-start | bytes 442376 | tf_op jit(solution)/shard_map/ppermute | solution.py:792
  35.4 5.5 %collective-permute-start.6 = (f32[288,128]{1,0:T(8,128)S(1)}, f32[288,128]{1,0:T(8,128)S(1)}, u32[]{:S(2)}, u32[]{:S(2)}) collective-permute-start(f32[288,128]{1,0:T(8,128)S(1)} %add.40), channel_id=1, source_target_pairs={{0,4},{2,6},{4,0},{6,2},{8,12},{10,14},{12,8},{14,10},{16,20},{18,... | collective-permute-start | bytes 442376 | tf_op jit(solution)/shard_map/ppermute | solution.py:792
  40.9 5.4 %collective-permute-start.7 = (f32[288,128]{1,0:T(8,128)S(1)}, f32[288,128]{1,0:T(8,128)S(1)}, u32[]{:S(2)}, u32[]{:S(2)}) collective-permute-start(f32[288,128]{1,0:T(8,128)S(1)} %add.41), channel_id=1, source_target_pairs={{0,8},{2,10},{4,12},{6,14},{8,0},{10,2},{12,4},{14,6},{16,24},{18,... | collective-permute-start | bytes 442376 | tf_op jit(solution)/shard_map/ppermute | solution.py:792
  46.3 10.5 %collective-permute-start.8 = (f32[288,128]{1,0:T(8,128)S(1)}, f32[288,128]{1,0:T(8,128)S(1)}, u32[]{:S(2)}, u32[]{:S(2)}) collective-permute-start(f32[288,128]{1,0:T(8,128)S(1)} %get-tuple-element.136), channel_id=1, source_target_pairs={{0,1},{1,0},{2,3},{3,2},{4,5},{5,4},{6,7},{7,6},{8,9},{9,8},{10,11... | collective-permute-start | bytes 442376 | tf_op jit(solution)/shard_map/ppermute | solution.py:779
  46.4 10.3 %collective-permute-start.9 = (f32[288,128]{1,0:T(8,128)S(1)}, f32[288,128]{1,0:T(8,128)S(1)}, u32[]{:S(2)}, u32[]{:S(2)}) collective-permute-start(f32[288,128]{1,0:T(8,128)S(1)} %add.42.left), channel_id=1, source_target_pairs={{0,16},{2,18},{4,20},{6,22},{8,24},{10,26},{12,28},{14,30},{16,0},... | collective-permute-start | bytes 442376 | tf_op jit(solution)/shard_map/ppermute | solution.py:792
  49.0 9.1 %copy-start.7 = (f32[1,72193]{1,0:T(1,128)S(1)}, f32[1,72193]{1,0:T(1,128)}, u32[]{:S(2)}) copy-start(f32[1,72193]{1,0:T(1,128)} %refs_6_.5) | copy-start | bytes 866320
  49.0 9.1 %copy-start.8 = (f32[1,72193]{1,0:T(1,128)S(1)}, f32[1,72193]{1,0:T(1,128)}, u32[]{:S(2)}) copy-start(f32[1,72193]{1,0:T(1,128)} %refs_7_.3) | copy-start | bytes 866320
  56.7 1.4 %collective-permute-start.10 = (f32[288,128]{1,0:T(8,128)S(1)}, f32[288,128]{1,0:T(8,128)S(1)}, u32[]{:S(2)}, u32[]{:S(2)}) collective-permute-start(f32[288,128]{1,0:T(8,128)S(1)} %plus.3.refs_2_.refs_1_), channel_id=1, source_target_pairs={{0,1},{1,0},{2,3},{3,2},{4,5},{5,4},{6,7},{7,6},{8,9},{9,8},{10,11... | collective-permute-start | bytes 442376 | tf_op jit(solution)/shard_map/ppermute | solution.py:779
  56.8 16.0 %collective-permute-start.11 = (f32[288,128]{1,0:T(8,128)S(1)}, f32[288,128]{1,0:T(8,128)S(1)}, u32[]{:S(2)}, u32[]{:S(2)}) collective-permute-start(f32[288,128]{1,0:T(8,128)S(1)} %plus.2), channel_id=1, source_target_pairs={{0,16},{2,18},{4,20},{6,22},{8,24},{10,26},{12,28},{14,30},{16,0},... | collective-permute-start | bytes 442376 | tf_op jit(solution)/shard_map/ppermute | solution.py:792
  72.6 27.5 %copy-start.1 = (f32[71942]{0:T(1024)S(1)}, f32[71942]{0:T(1024)}, u32[]{:S(2)}) copy-start(f32[71942]{0:T(1024)} %refs_6_.4) | copy-start | bytes 863308
  72.6 27.5 %copy-start.3 = (f32[71942]{0:T(1024)S(1)}, f32[71942]{0:T(1024)}, u32[]{:S(2)}) copy-start(f32[71942]{0:T(1024)} %refs_4_.5) | copy-start | bytes 863308
  72.6 27.5 %copy-start.4 = (f32[71942]{0:T(1024)S(1)}, f32[71942]{0:T(1024)}, u32[]{:S(2)}) copy-start(f32[71942]{0:T(1024)} %refs_5_.2) | copy-start | bytes 863308
  72.6 1.4 %collective-permute-start.12 = (f32[288,128]{1,0:T(8,128)S(1)}, f32[288,128]{1,0:T(8,128)S(1)}, u32[]{:S(2)}, u32[]{:S(2)}) collective-permute-start(f32[288,128]{1,0:T(8,128)S(1)} %get-tuple-element.160), channel_id=1, source_target_pairs={{0,1},{1,0},{2,3},{3,2},{4,5},{5,4},{6,7},{7,6},{8,9},{9,8},{10,11... | collective-permute-start | bytes 442376 | tf_op jit(solution)/shard_map/ppermute | solution.py:779
  74.1 6.0 %collective-permute-start.13 = (f32[288,128]{1,0:T(8,128)S(1)}, f32[288,128]{1,0:T(8,128)S(1)}, u32[]{:S(2)}, u32[]{:S(2)}) collective-permute-start(f32[288,128]{1,0:T(8,128)S(1)} %add.44), channel_id=1, source_target_pairs={{0,2},{2,0},{4,6},{6,4},{8,10},{10,8},{12,14},{14,12},{16,18},{18,... | collective-permute-start | bytes 442376 | tf_op jit(solution)/shard_map/ppermute | solution.py:792
  75.6 6.9 %collective-permute-start.18 = (f32[288,128]{1,0:T(8,128)S(1)}, f32[288,128]{1,0:T(8,128)S(1)}, u32[]{:S(2)}, u32[]{:S(2)}) collective-permute-start(f32[288,128]{1,0:T(8,128)S(1)} %add.43), channel_id=1, source_target_pairs={{0,8},{2,10},{4,12},{6,14},{8,0},{10,2},{12,4},{14,6},{16,24},{18,... | collective-permute-start | bytes 442376 | tf_op jit(solution)/shard_map/ppermute | solution.py:792
  80.1 5.2 %collective-permute-start.14 = (f32[288,128]{1,0:T(8,128)S(1)}, f32[288,128]{1,0:T(8,128)S(1)}, u32[]{:S(2)}, u32[]{:S(2)}) collective-permute-start(f32[288,128]{1,0:T(8,128)S(1)} %add.45), channel_id=1, source_target_pairs={{0,4},{2,6},{4,0},{6,2},{8,12},{10,14},{12,8},{14,10},{16,20},{18,... | collective-permute-start | bytes 442376 | tf_op jit(solution)/shard_map/ppermute | solution.py:792
  82.6 5.8 %collective-permute-start.19 = (f32[288,128]{1,0:T(8,128)S(1)}, f32[288,128]{1,0:T(8,128)S(1)}, u32[]{:S(2)}, u32[]{:S(2)}) collective-permute-start(f32[288,128]{1,0:T(8,128)S(1)} %add.49), channel_id=1, source_target_pairs={{0,2},{2,0},{4,6},{6,4},{8,10},{10,8},{12,14},{14,12},{16,18},{18,... | collective-permute-start | bytes 442376 | tf_op jit(solution)/shard_map/ppermute | solution.py:792
  85.3 7.0 %collective-permute-start.15 = (f32[288,128]{1,0:T(8,128)S(1)}, f32[288,128]{1,0:T(8,128)S(1)}, u32[]{:S(2)}, u32[]{:S(2)}) collective-permute-start(f32[288,128]{1,0:T(8,128)S(1)} %add.46), channel_id=1, source_target_pairs={{0,8},{2,10},{4,12},{6,14},{8,0},{10,2},{12,4},{14,6},{16,24},{18,... | collective-permute-start | bytes 442376 | tf_op jit(solution)/shard_map/ppermute | solution.py:792
  88.4 5.2 %collective-permute-start.20 = (f32[288,128]{1,0:T(8,128)S(1)}, f32[288,128]{1,0:T(8,128)S(1)}, u32[]{:S(2)}, u32[]{:S(2)}) collective-permute-start(f32[288,128]{1,0:T(8,128)S(1)} %add.50), channel_id=1, source_target_pairs={{0,4},{2,6},{4,0},{6,2},{8,12},{10,14},{12,8},{14,10},{16,20},{18,... | collective-permute-start | bytes 442376 | tf_op jit(solution)/shard_map/ppermute | solution.py:792
  92.3 6.1 %collective-permute-start.16 = (f32[288,128]{1,0:T(8,128)S(1)}, f32[288,128]{1,0:T(8,128)S(1)}, u32[]{:S(2)}, u32[]{:S(2)}) collective-permute-start(f32[288,128]{1,0:T(8,128)S(1)} %add.47), channel_id=1, source_target_pairs={{0,16},{2,18},{4,20},{6,22},{8,24},{10,26},{12,28},{14,30},{16,0},... | collective-permute-start | bytes 442376 | tf_op jit(solution)/shard_map/ppermute | solution.py:792
  93.7 4.8 %collective-permute-start.21 = (f32[288,128]{1,0:T(8,128)S(1)}, f32[288,128]{1,0:T(8,128)S(1)}, u32[]{:S(2)}, u32[]{:S(2)}) collective-permute-start(f32[288,128]{1,0:T(8,128)S(1)} %add.51.refs_3_), channel_id=1, source_target_pairs={{0,1},{2,3},{4,5},{6,7},{8,9},{10,11},{12,13},{14,15},{16,17},{18,... | collective-permute-start | bytes 442376 | tf_op jit(solution)/shard_map/ppermute | solution.py:783
  98.4 1.7 %collective-permute-start.17 = (f32[288,128]{1,0:T(8,128)S(1)}, f32[288,128]{1,0:T(8,128)S(1)}, u32[]{:S(2)}, u32[]{:S(2)}) collective-permute-start(f32[288,128]{1,0:T(8,128)S(1)} %add.48.refs_1_), channel_id=1, source_target_pairs={{0,1},{1,0},{2,3},{3,2},{4,5},{5,4},{6,7},{7,6},{8,9},{9,8},{10,11... | collective-permute-start | bytes 442376 | tf_op jit(solution)/shard_map/ppermute | solution.py:779

commit v5 on v4

--- a/solution.py
+++ b/solution.py
@@ -790,6 +790,15 @@
 def partner(value, mask):
     pairs = [(source, source ^ mask) for source in range(lax.axis_size("dp"))]
     return lax.ppermute(value, "dp", pairs)
+
+
+def partner_by_core(value, masks):
+    pairs = [
+        (2 * source + core, 2 * (source ^ masks[core]) + core)
+        for source in range(lax.axis_size("dp"))
+        for core in range(2)
+    ]
+    return lax.ppermute(value, ("dp", "twin"), pairs)
 
 
 def plus_kernel(left, right, out):
@@ -1018,8 +1027,8 @@
     state = ()
     one = keep_one + twin_swap(send_one)
     piece = 0
-    for mask in masks:
-        moved = partner(one, mask)
+    for mask, other in zip(masks, masks[len(masks) // 2 :] + masks[: len(masks) // 2]):
+        moved = partner_by_core(one, (mask, other))
         if mask == masks[-1]:
             one, tied_tail = lax.optimization_barrier((one, actor_net[4]))
             kept = actor_forward(tied_tail)
@@ -1079,10 +1088,12 @@
     two = two + two_moved
     two, keep_actor, actor_moved = lax.optimization_barrier((two, keep_actor, actor_moved))
     actor = keep_actor + actor_moved
-    for mask, other_mask in zip(masks, masks[-2:-1] + masks[:-2] + [None]):
-        moved = partner(actor, mask)
-        if other_mask is not None:
-            two = two + partner(two, other_mask)
+    turned = masks[len(masks) // 2 :] + masks[: len(masks) // 2]
+    later = masks[:-1]
+    for index, pair in enumerate(zip(masks, turned)):
+        moved = partner_by_core(actor, pair)
+        if index < len(later):
+            two = two + partner(two, later[index - 1])
         actor = actor + moved
     actor_other = twin_swap(actor)
     two_other = to_second(two)

time: 102 us -> 99.5 us (0.975)
  waiting for transfers between devices: 17.2 us -> 15.2 us
    ppermute x12 -> x4, starting transfers between devices: 20.9 us -> 5.89 us  [partner(): return lax.ppermute(value, 'dp', pairs)]
    ppermute x0 -> x8, starting transfers between devices: none -> 13.3 us  [partner_by_core(): return lax.ppermute(value, ('dp', 'twin'), pairs)]
    ppermute x12 -> x4, waiting for transfers between devices: 13.7 us -> 3.77 us  [partner(): return lax.ppermute(value, 'dp', pairs)]
    ppermute x0 -> x8, waiting for transfers between devices: none -> 9.04 us  [partner_by_core(): return lax.ppermute(value, ('dp', 'twin'), pairs)]
    ppermute x9, waiting for transfers between devices: 3.47 us -> 2.35 us  [twin_swap(): return lax.ppermute(value, 'twin', [(0, 1), (1, 0)])]
  transfers between devices with their start and end apart: 22 -> 22, of which waited for: 12 -> 10; matrix products, arithmetic and copies ran while one was open for 0% -> 0% of each run, Pallas kernels for 37% -> 38%
where the time goes in v5:
time: 99.5 us; the launch traced here: 99.2 us
  Pallas kernels  58.3 us (59%)
  starting transfers between devices  23.3 us (23%)
  waiting for transfers between devices  15.2 us (15%)
  between operations  1.13 us (1%)
  local copies, waits for them, and re-layouts  1.01 us (1%)
    pallas_call x1, Pallas kernels, on_device(): call(lambda *refs: target_kernel(row_total, *refs), local_rows // 2 // TA...  18.7 us
    pallas_call x1, Pallas kernels, on_device(): call(lambda *refs: actor_kernel(row_total, *refs), tiles, [mine(SDIM), ha...  14.7 us
    ppermute x8, starting transfers between devices, partner_by_core(): return lax.ppermute(value, ('dp', 'twin'), pairs)  13.3 us
    pallas_call x3, Pallas kernels, second_critic(): call(lambda *refs: critic_kernel(row_total, start, width, is_first, is_la...  10.5 us
    ppermute x8, waiting for transfers between devices, partner_by_core(): return lax.ppermute(value, ('dp', 'twin'), pairs)  9.04 us
    pallas_call x1, Pallas kernels, actor_forward(): call(forward_kernel, tiles, [mine(SDIM)] + [whole(None)] * 5, kept_specs,...  5.99 us
    ppermute x4, starting transfers between devices, partner(): return lax.ppermute(value, 'dp', pairs)  5.89 us
    pallas_call x1, Pallas kernels, on_device(): call(action_kernel, tiles, [mine(SDIM), mine(ADIM), actor_flat], [local(A...  5.23 us
  transfers between devices with their start and end apart: 22, of which 10 were waited for; matrix products, arithmetic and copies ran while one was open for 0% of the time, Pallas kernels for 38%

profile of v5, /device:TPU:0, one launch (start us, length us, event | category | flops | bytes accessed | tf_op | source)
XLA Modules:
  0.0 99.2 jit_solution(3615551542246107228)
XLA Ops:
  0.6 0.5 collective-permute-start
  1.2 0.1 collective-permute-start.1
  1.2 0.4 collective-permute-start.2
  1.7 0.1 collective-permute-start.3
  1.8 1.0 copy-done
  2.7 5.2 %next_action.1 = (f32[6,8192]{1,0:T(8,128)S(1)}, f32[32,2176]{1,0:T(8,128)S(1)}, bf16[2176,128]{1,0:T(8,128)(2,1)S(1)}) custom-call(s32[1]{0:T(128)} %bitcast.core_ref.refs_0_, f32[17,16384]{1,0:T(8,128)} %refs_4_.3, f32[6,16384]{1,0:T(8,128)} %smoothing.1, f32[71942]{0:T(1024)S(1)} %copy-done), custom_call_target="tpu_custom_call" | custom-call | flops 2147483648 | bytes 1000000 | tf_op jit(solution)/shard_map/next_action/pallas_call | solution.py:921
  8.0 0.0 collective-permute-done.1.refs_10_.refs_5_
  8.0 0.0 copy-start.9
  8.0 0.0 copy-start.10
  8.0 18.7 %target_and_first_critic.1 = (f32[1,8192]{1,0:T(1,128)S(1)}, f32[288,128]{1,0:T(8,128)S(1)}, f32[288,128]{1,0:T(8,128)S(1)}, f32[32,2944]{1,0:T(8,128)S(1)}, bf1...) custom-call(s32[1]{0:T(128)} %bitcast.core_ref.refs_0_, ...), custom_call_target="tpu_custom_call" | custom-call | flops 15032385536 | bytes 1000000 | tf_op jit(solution)/shard_map/target_and_first_critic/pallas_call | solution.py:933
  26.8 0.5 collective-permute-start.4
  27.3 1.0 %collective-permute-done.4 = f32[288,128]{1,0:T(8,128)S(1)} collective-permute-done((f32[288,128]{1,0:T(8,128)S(1)}, f32[288,128]{1,0:T(8,128)S(1)}, u32[]{:S(2)}, u32[]{:S(2)}) %collective-permute-start.4) | collective-permute-done | bytes 147488 | tf_op jit(solution)/shard_map/ppermute | solution.py:779
  28.3 2.9 %collective-permute-start.5 = (f32[288,128]{1,0:T(8,128)S(1)}, f32[288,128]{1,0:T(8,128)S(1)}, u32[]{:S(2)}, u32[]{:S(2)}) collective-permute-start(f32[288,128]{1,0:T(8,128)S(1)} %add.39), channel_id=1, source_target_pairs={{0,2},{1,9},{2,0},{3,11},{4,6},{5,13},{6,4},{7,15},{8,10},{9,1},{1... | collective-permute-start | bytes 442376 | tf_op jit(solution)/shard_map/ppermute | solution.py:801
  31.2 3.7 %second_critic.3 = (f32[32,256]{1,0:T(8,128)S(1)}, f32[272,256]{1,0:T(8,128)S(1)}, f32[16,256]{1,0:T(8,128)S(1)}, f32[16,3072]{1,0:T(8,128)S(1)}) custom-call(s32[1]{0:T(128)} %bitcast.core_ref.refs_0_, f32[17,16384]{1,0:T(8,128)S(1)} %copy-done.9, f32[6,16384]{1,0:T(8,128)S(1)} %copy-done.10, f32[1,8192]{1,0:T(1,128)S(1)} %get-tuple-element.126.refs_3_, ...), custom_call_target="tpu_custom_call" | custom-call | flops 2147483648 | bytes 1000000 | tf_op jit(solution)/shard_map/second_critic/pallas_call | solution.py:1001
  35.0 1.6 %collective-permute-start.6 = (f32[288,128]{1,0:T(8,128)S(1)}, f32[288,128]{1,0:T(8,128)S(1)}, u32[]{:S(2)}, u32[]{:S(2)}) collective-permute-start(f32[288,128]{1,0:T(8,128)S(1)} %add.40), channel_id=1, source_target_pairs={{0,4},{1,17},{2,6},{3,19},{4,0},{5,21},{6,2},{7,23},{8,12},{9,25},... | collective-permute-start | bytes 442376 | tf_op jit(solution)/shard_map/ppermute | solution.py:801
  36.5 3.1 %second_critic.4 = (f32[32,256]{1,0:T(8,128)S(1)}, f32[272,256]{1,0:T(8,128)S(1)}, f32[16,256]{1,0:T(8,128)S(1)}, f32[16,3072]{1,0:T(8,128)S(1)}) custom-call(s32[1]{0:T(128)} %bitcast.core_ref.refs_0_, f32[17,16384]{1,0:T(8,128)S(1)} %copy-done.9, ...), custom_call_target="tpu_custom_call", output_to_operand_aliasing={{0}: (11, {}), {1}: (12, {}), {2}: (13, {}), {3}: (14, {})} | custom-call | flops 2147483648 | bytes 1000000 | tf_op jit(solution)/shard_map/second_critic/pallas_call | solution.py:1001
  39.7 0.5 collective-permute-done.6
  40.2 1.6 %collective-permute-start.7 = (f32[288,128]{1,0:T(8,128)S(1)}, f32[288,128]{1,0:T(8,128)S(1)}, u32[]{:S(2)}, u32[]{:S(2)}) collective-permute-start(f32[288,128]{1,0:T(8,128)S(1)} %add.41), channel_id=1, source_target_pairs={{0,8},{1,3},{2,10},{3,1},{4,12},{5,7},{6,14},{7,5},{8,0},{9,11},{1... | collective-permute-start | bytes 442376 | tf_op jit(solution)/shard_map/ppermute | solution.py:801
  41.8 3.7 %second_critic.5 = (f32[288,128]{1,0:T(8,128)S(1)}, f32[288,128]{1,0:T(8,128)S(1)}) custom-call(s32[1]{0:T(128)} %bitcast.core_ref.refs_0_, f32[17,16384]{1,0:T(8,128)S(1)} %copy-done.9, f32[6,16384]{1,0:T(8,128)S(1)} %copy-done.10, f32[1,8192]{1,0:T(1,128)S(1)} %get-tuple-element.126.refs_3_, bf16[256,32]{1,0:T(8,128)(2,1)S(1)} %get-tuple-element.102.refs_4_, ...), custom_call_target="tpu_custom_call" | custom-call | flops 2147483648 | bytes 1000000 | tf_op jit(solution)/shard_map/second_critic/pallas_call | solution.py:1001
  45.6 1.0 collective-permute-start.8
  46.6 1.7 %collective-permute-start.9 = (f32[288,128]{1,0:T(8,128)S(1)}, f32[288,128]{1,0:T(8,128)S(1)}, u32[]{:S(2)}, u32[]{:S(2)}) collective-permute-start(f32[288,128]{1,0:T(8,128)S(1)} %add.42.left), channel_id=1, source_target_pairs={{0,16},{1,5},{2,18},{3,7},{4,20},{5,1},{6,22},{7,3},{8,24},{9,13},... | collective-permute-start | bytes 442376 | tf_op jit(solution)/shard_map/ppermute | solution.py:801
  48.3 6.0 %actor_forward.1 = (bf16[4,272,2048]{2,1,0:T(8,128)(2,1)S(1)}, f32[4,256,2048]{2,1,0:T(8,128)S(1)}, bf16[4,256,2048]{2,1,0:T(8,128)(2,1)S(1)}, f32[4,256,2048]{2,1,0:T(8,128)S(1)}, f32[4,8,2048]{2,1,0:T(8,128)S(1)}) custom-call(s32[1]{0:T(128)} %bitcast.core_ref.refs_0_, f32[17,16384]{1,0:T(8,128)S(1)} %copy-done.9, ...), custom_call_target="tpu_custom_call" | custom-call | flops 3221225472 | bytes 1000000 | tf_op jit(solution)/shard_map/actor_forward/pallas_call | solution.py:1014
  54.3 0.1 collective-permute-start.10
  54.5 1.7 %collective-permute-start.11 = (f32[288,128]{1,0:T(8,128)S(1)}, f32[288,128]{1,0:T(8,128)S(1)}, u32[]{:S(2)}, u32[]{:S(2)}) collective-permute-start(f32[288,128]{1,0:T(8,128)S(1)} %plus.2), channel_id=1, source_target_pairs={{0,16},{2,18},{4,20},{6,22},{8,24},{10,26},{12,28},{14,30},{16,0},... | collective-permute-start | bytes 442376 | tf_op jit(solution)/shard_map/ppermute | solution.py:792
  56.2 14.7 %actor.1 = (f32[288,128]{1,0:T(8,128)S(1)}, f32[288,128]{1,0:T(8,128)S(1)}) custom-call(s32[1]{0:T(128)} %bitcast.core_ref.refs_0_, f32[17,16384]{1,0:T(8,128)S(1)} %copy-done.9, f32[288,128]{1,0:T(8,128)S(1)} %plus.3.refs_2_.refs_1_, f32[288,128]{1,0:T(8,128)S(1)} %collective-permute-done.10.refs_3_.refs_2_, f32[1,72193]{1,0:T(1,128)S(1)} %copy-done.6, ...), custom_call_target="tpu_custom_call" | custom-call | flops 8589934592 | bytes 1000000 | tf_op jit(solution)/shard_map/actor/pallas_call | solution.py:1053
  70.8 0.0 copy-start.1
  70.9 0.0 copy-start.3
  70.9 0.0 copy-start.4
  70.9 0.1 collective-permute-start.12
  71.0 1.3 %collective-permute-done.12 = f32[288,128]{1,0:T(8,128)S(1)} collective-permute-done((f32[288,128]{1,0:T(8,128)S(1)}, f32[288,128]{1,0:T(8,128)S(1)}, u32[]{:S(2)}, u32[]{:S(2)}) %collective-permute-start.12) | collective-permute-done | bytes 147488 | tf_op jit(solution)/shard_map/ppermute | solution.py:779
  72.3 1.5 %collective-permute-start.13 = (f32[288,128]{1,0:T(8,128)S(1)}, f32[288,128]{1,0:T(8,128)S(1)}, u32[]{:S(2)}, u32[]{:S(2)}) collective-permute-start(f32[288,128]{1,0:T(8,128)S(1)} %add.44), channel_id=1, source_target_pairs={{0,2},{1,9},{2,0},{3,11},{4,6},{5,13},{6,4},{7,15},{8,10},{9,1},{1... | collective-permute-start | bytes 442376 | tf_op jit(solution)/shard_map/ppermute | solution.py:801
  73.9 1.4 %collective-permute-start.18 = (f32[288,128]{1,0:T(8,128)S(1)}, f32[288,128]{1,0:T(8,128)S(1)}, u32[]{:S(2)}, u32[]{:S(2)}) collective-permute-start(f32[288,128]{1,0:T(8,128)S(1)} %add.43), channel_id=1, source_target_pairs={{0,8},{2,10},{4,12},{6,14},{8,0},{10,2},{12,4},{14,6},{16,24},{18,... | collective-permute-start | bytes 442376 | tf_op jit(solution)/shard_map/ppermute | solution.py:792
  75.3 2.3 %collective-permute-done.13 = f32[288,128]{1,0:T(8,128)S(1)} collective-permute-done((f32[288,128]{1,0:T(8,128)S(1)}, f32[288,128]{1,0:T(8,128)S(1)}, u32[]{:S(2)}, u32[]{:S(2)}) %collective-permute-start.13) | collective-permute-done | bytes 147488 | tf_op jit(solution)/shard_map/ppermute | solution.py:801
  77.6 1.1 %collective-permute-start.14 = (f32[288,128]{1,0:T(8,128)S(1)}, f32[288,128]{1,0:T(8,128)S(1)}, u32[]{:S(2)}, u32[]{:S(2)}) collective-permute-start(f32[288,128]{1,0:T(8,128)S(1)} %add.45), channel_id=1, source_target_pairs={{0,4},{1,17},{2,6},{3,19},{4,0},{5,21},{6,2},{7,23},{8,12},{9,25},... | collective-permute-start | bytes 442376 | tf_op jit(solution)/shard_map/ppermute | solution.py:801
  78.7 1.2 %collective-permute-done.18 = f32[288,128]{1,0:T(8,128)S(1)} collective-permute-done((f32[288,128]{1,0:T(8,128)S(1)}, f32[288,128]{1,0:T(8,128)S(1)}, u32[]{:S(2)}, u32[]{:S(2)}) %collective-permute-start.18) | collective-permute-done | bytes 147488 | tf_op jit(solution)/shard_map/ppermute | solution.py:792
  79.9 1.4 %collective-permute-start.19 = (f32[288,128]{1,0:T(8,128)S(1)}, f32[288,128]{1,0:T(8,128)S(1)}, u32[]{:S(2)}, u32[]{:S(2)}) collective-permute-start(f32[288,128]{1,0:T(8,128)S(1)} %add.49), channel_id=1, source_target_pairs={{0,2},{2,0},{4,6},{6,4},{8,10},{10,8},{12,14},{14,12},{16,18},{18,... | collective-permute-start | bytes 442376 | tf_op jit(solution)/shard_map/ppermute | solution.py:792
  81.3 1.5 %collective-permute-done.14 = f32[288,128]{1,0:T(8,128)S(1)} collective-permute-done((f32[288,128]{1,0:T(8,128)S(1)}, f32[288,128]{1,0:T(8,128)S(1)}, u32[]{:S(2)}, u32[]{:S(2)}) %collective-permute-start.14) | collective-permute-done | bytes 147488 | tf_op jit(solution)/shard_map/ppermute | solution.py:801
  82.8 1.5 %collective-permute-start.15 = (f32[288,128]{1,0:T(8,128)S(1)}, f32[288,128]{1,0:T(8,128)S(1)}, u32[]{:S(2)}, u32[]{:S(2)}) collective-permute-start(f32[288,128]{1,0:T(8,128)S(1)} %add.46), channel_id=1, source_target_pairs={{0,8},{1,3},{2,10},{3,1},{4,12},{5,7},{6,14},{7,5},{8,0},{9,11},{1... | collective-permute-start | bytes 442376 | tf_op jit(solution)/shard_map/ppermute | solution.py:801
  84.3 1.1 %collective-permute-done.19 = f32[288,128]{1,0:T(8,128)S(1)} collective-permute-done((f32[288,128]{1,0:T(8,128)S(1)}, f32[288,128]{1,0:T(8,128)S(1)}, u32[]{:S(2)}, u32[]{:S(2)}) %collective-permute-start.19) | collective-permute-done | bytes 147488 | tf_op jit(solution)/shard_map/ppermute | solution.py:792
  85.4 1.4 %collective-permute-start.20 = (f32[288,128]{1,0:T(8,128)S(1)}, f32[288,128]{1,0:T(8,128)S(1)}, u32[]{:S(2)}, u32[]{:S(2)}) collective-permute-start(f32[288,128]{1,0:T(8,128)S(1)} %add.50), channel_id=1, source_target_pairs={{0,4},{2,6},{4,0},{6,2},{8,12},{10,14},{12,8},{14,10},{16,20},{18,... | collective-permute-start | bytes 442376 | tf_op jit(solution)/shard_map/ppermute | solution.py:792
  86.8 1.2 %collective-permute-done.15 = f32[288,128]{1,0:T(8,128)S(1)} collective-permute-done((f32[288,128]{1,0:T(8,128)S(1)}, f32[288,128]{1,0:T(8,128)S(1)}, u32[]{:S(2)}, u32[]{:S(2)}) %collective-permute-start.15) | collective-permute-done | bytes 147488 | tf_op jit(solution)/shard_map/ppermute | solution.py:801
  88.0 1.3 %collective-permute-start.16 = (f32[288,128]{1,0:T(8,128)S(1)}, f32[288,128]{1,0:T(8,128)S(1)}, u32[]{:S(2)}, u32[]{:S(2)}) collective-permute-start(f32[288,128]{1,0:T(8,128)S(1)} %add.47), channel_id=1, source_target_pairs={{0,16},{1,5},{2,18},{3,7},{4,20},{5,1},{6,22},{7,3},{8,24},{9,13},... | collective-permute-start | bytes 442376 | tf_op jit(solution)/shard_map/ppermute | solution.py:801
  89.4 1.4 %collective-permute-done.20 = f32[288,128]{1,0:T(8,128)S(1)} collective-permute-done((f32[288,128]{1,0:T(8,128)S(1)}, f32[288,128]{1,0:T(8,128)S(1)}, u32[]{:S(2)}, u32[]{:S(2)}) %collective-permute-start.20) | collective-permute-done | bytes 147488 | tf_op jit(solution)/shard_map/ppermute | solution.py:792
  90.8 1.3 %collective-permute-start.21 = (f32[288,128]{1,0:T(8,128)S(1)}, f32[288,128]{1,0:T(8,128)S(1)}, u32[]{:S(2)}, u32[]{:S(2)}) collective-permute-start(f32[288,128]{1,0:T(8,128)S(1)} %add.51.refs_3_), channel_id=1, source_target_pairs={{0,1},{2,3},{4,5},{6,7},{8,9},{10,11},{12,13},{14,15},{16,17},{18,... | collective-permute-start | bytes 442376 | tf_op jit(solution)/shard_map/ppermute | solution.py:783
  92.1 3.6 %collective-permute-done.16 = f32[288,128]{1,0:T(8,128)S(1)} collective-permute-done((f32[288,128]{1,0:T(8,128)S(1)}, f32[288,128]{1,0:T(8,128)S(1)}, u32[]{:S(2)}, u32[]{:S(2)}) %collective-permute-start.16) | collective-permute-done | bytes 147488 | tf_op jit(solution)/shard_map/ppermute | solution.py:801
  95.7 0.1 collective-permute-start.17
  95.8 1.6 %critic_step.1 = (f32[1,72193]{1,0:T(1,128)}, f32[1,72193]{1,0:T(1,128)}, f32[1,72193]{1,0:T(1,128)}, f32[1,72193]{1,0:T(1,128)}, f32[1]{0:T(128)}) custom-call(s32[1]{0:T(128)} %bitcast.core_ref.refs_0_, f32[288,128]{1,0:T(8,128)S(1)} %plus.3.refs_2_.refs_1_, f32[288,128]{1,0:T(8,128)S(1)} %collective-permute-done.10.refs_3_.refs_2_, ...), custom_call_target="tpu_custom_call" | custom-call | tf_op jit(solution)/shard_map/critic_step/pallas_call | solution.py:1104
  97.5 1.5 %actor_step.1 = (f32[71942]{0:T(1024)}, f32[71942]{0:T(1024)}, f32[71942]{0:T(1024)}, f32[71942]{0:T(1024)}, f32[1]{0:T(128)}) custom-call(s32[1]{0:T(128)} %bitcast.core_ref.refs_0_, f32[288,128]{1,0:T(8,128)S(1)} %add.48.refs_1_, f32[288,128]{1,0:T(8,128)S(1)} %collective-permute-done.17.refs_2_, f32[71942]{0:T(1024)S(1)} %copy-done.2, ...), custom_call_target="tpu_custom_call" | custom-call | tf_op jit(solution)/shard_map/actor_step/pallas_call | solution.py:1104
  (42 shorter events, 0.4 us)
Async XLA Ops:
  0.6 7.3 %collective-permute-start = (f32[1,72193]{1,0:T(1,128)}, f32[1,72193]{1,0:T(1,128)S(1)}, u32[]{:S(2)}, u32[]{:S(2)}) collective-permute-start(f32[1,72193]{1,0:T(1,128)} %refs_8_.3), channel_id=1, source_target_pairs={{0,1},{1,0},{2,3},{3,2},{4,5},{5,4},{6,7},{7,6},{8,9},{9,8},{10,11... | collective-permute-start | bytes 866324 | tf_op jit(solution)/shard_map/ppermute | solution.py:779
  1.2 6.8 %collective-permute-start.1 = (f32[1,72193]{1,0:T(1,128)}, f32[1,72193]{1,0:T(1,128)S(1)}, u32[]{:S(2)}, u32[]{:S(2)}) collective-permute-start(f32[1,72193]{1,0:T(1,128)} %refs_5_.3), channel_id=1, source_target_pairs={{0,1},{1,0},{2,3},{3,2},{4,5},{5,4},{6,7},{7,6},{8,9},{9,8},{10,11... | collective-permute-start | bytes 866324 | tf_op jit(solution)/shard_map/ppermute | solution.py:779
  1.2 6.7 %collective-permute-start.2 = (f32[1,72193]{1,0:T(1,128)}, f32[1,72193]{1,0:T(1,128)S(1)}, u32[]{:S(2)}, u32[]{:S(2)}) collective-permute-start(f32[1,72193]{1,0:T(1,128)} %refs_6_.5), channel_id=1, source_target_pairs={{0,1},{1,0},{2,3},{3,2},{4,5},{5,4},{6,7},{7,6},{8,9},{9,8},{10,11... | collective-permute-start | bytes 866324 | tf_op jit(solution)/shard_map/ppermute | solution.py:779
  1.7 6.3 %collective-permute-start.3 = (f32[1,72193]{1,0:T(1,128)}, f32[1,72193]{1,0:T(1,128)S(1)}, u32[]{:S(2)}, u32[]{:S(2)}) collective-permute-start(f32[1,72193]{1,0:T(1,128)} %refs_7_.3), channel_id=1, source_target_pairs={{0,1},{1,0},{2,3},{3,2},{4,5},{5,4},{6,7},{7,6},{8,9},{9,8},{10,11... | collective-permute-start | bytes 866324 | tf_op jit(solution)/shard_map/ppermute | solution.py:779
  1.8 1.0 copy-start
  2.7 5.3 %copy-start.2 = (f32[71942]{0:T(1024)S(1)}, f32[71942]{0:T(1024)}, u32[]{:S(2)}) copy-start(f32[71942]{0:T(1024)} %refs_3_.1) | copy-start | bytes 863308
  2.7 5.3 %copy-start.5 = (f32[1,72193]{1,0:T(1,128)S(1)}, f32[1,72193]{1,0:T(1,128)}, u32[]{:S(2)}) copy-start(f32[1,72193]{1,0:T(1,128)} %refs_8_.3) | copy-start | bytes 866320
  2.7 5.3 %copy-start.6 = (f32[1,72193]{1,0:T(1,128)S(1)}, f32[1,72193]{1,0:T(1,128)}, u32[]{:S(2)}) copy-start(f32[1,72193]{1,0:T(1,128)} %refs_5_.3) | copy-start | bytes 866320
  8.0 23.2 %copy-start.9 = (f32[17,16384]{1,0:T(8,128)S(1)}, f32[17,16384]{1,0:T(8,128)}, u32[]{:S(2)}) copy-start(f32[17,16384]{1,0:T(8,128)} %refs_1_.9) | copy-start | bytes 3342340
  8.0 23.2 %copy-start.10 = (f32[6,16384]{1,0:T(8,128)S(1)}, f32[6,16384]{1,0:T(8,128)}, u32[]{:S(2)}) copy-start(f32[6,16384]{1,0:T(8,128)} %refs_2_.7) | copy-start | bytes 1179652
  26.8 1.5 %collective-permute-start.4 = (f32[288,128]{1,0:T(8,128)S(1)}, f32[288,128]{1,0:T(8,128)S(1)}, u32[]{:S(2)}, u32[]{:S(2)}) collective-permute-start(f32[288,128]{1,0:T(8,128)S(1)} %get-tuple-element.98), channel_id=1, source_target_pairs={{0,1},{1,0},{2,3},{3,2},{4,5},{5,4},{6,7},{7,6},{8,9},{9,8},{10,11... | collective-permute-start | bytes 442376 | tf_op jit(solution)/shard_map/ppermute | solution.py:779
  28.3 6.6 %collective-permute-start.5 = (f32[288,128]{1,0:T(8,128)S(1)}, f32[288,128]{1,0:T(8,128)S(1)}, u32[]{:S(2)}, u32[]{:S(2)}) collective-permute-start(f32[288,128]{1,0:T(8,128)S(1)} %add.39), channel_id=1, source_target_pairs={{0,2},{1,9},{2,0},{3,11},{4,6},{5,13},{6,4},{7,15},{8,10},{9,1},{1... | collective-permute-start | bytes 442376 | tf_op jit(solution)/shard_map/ppermute | solution.py:801
  35.0 5.2 %collective-permute-start.6 = (f32[288,128]{1,0:T(8,128)S(1)}, f32[288,128]{1,0:T(8,128)S(1)}, u32[]{:S(2)}, u32[]{:S(2)}) collective-permute-start(f32[288,128]{1,0:T(8,128)S(1)} %add.40), channel_id=1, source_target_pairs={{0,4},{1,17},{2,6},{3,19},{4,0},{5,21},{6,2},{7,23},{8,12},{9,25},... | collective-permute-start | bytes 442376 | tf_op jit(solution)/shard_map/ppermute | solution.py:801
  40.2 5.4 %collective-permute-start.7 = (f32[288,128]{1,0:T(8,128)S(1)}, f32[288,128]{1,0:T(8,128)S(1)}, u32[]{:S(2)}, u32[]{:S(2)}) collective-permute-start(f32[288,128]{1,0:T(8,128)S(1)} %add.41), channel_id=1, source_target_pairs={{0,8},{1,3},{2,10},{3,1},{4,12},{5,7},{6,14},{7,5},{8,0},{9,11},{1... | collective-permute-start | bytes 442376 | tf_op jit(solution)/shard_map/ppermute | solution.py:801
  45.6 8.8 %collective-permute-start.8 = (f32[288,128]{1,0:T(8,128)S(1)}, f32[288,128]{1,0:T(8,128)S(1)}, u32[]{:S(2)}, u32[]{:S(2)}) collective-permute-start(f32[288,128]{1,0:T(8,128)S(1)} %get-tuple-element.136), channel_id=1, source_target_pairs={{0,1},{1,0},{2,3},{3,2},{4,5},{5,4},{6,7},{7,6},{8,9},{9,8},{10,11... | collective-permute-start | bytes 442376 | tf_op jit(solution)/shard_map/ppermute | solution.py:779
  46.6 7.7 %collective-permute-start.9 = (f32[288,128]{1,0:T(8,128)S(1)}, f32[288,128]{1,0:T(8,128)S(1)}, u32[]{:S(2)}, u32[]{:S(2)}) collective-permute-start(f32[288,128]{1,0:T(8,128)S(1)} %add.42.left), channel_id=1, source_target_pairs={{0,16},{1,5},{2,18},{3,7},{4,20},{5,1},{6,22},{7,3},{8,24},{9,13},... | collective-permute-start | bytes 442376 | tf_op jit(solution)/shard_map/ppermute | solution.py:801
  48.3 7.9 %copy-start.7 = (f32[1,72193]{1,0:T(1,128)S(1)}, f32[1,72193]{1,0:T(1,128)}, u32[]{:S(2)}) copy-start(f32[1,72193]{1,0:T(1,128)} %refs_6_.5) | copy-start | bytes 866320
  48.3 7.9 %copy-start.8 = (f32[1,72193]{1,0:T(1,128)S(1)}, f32[1,72193]{1,0:T(1,128)}, u32[]{:S(2)}) copy-start(f32[1,72193]{1,0:T(1,128)} %refs_7_.3) | copy-start | bytes 866320
  54.3 1.8 %collective-permute-start.10 = (f32[288,128]{1,0:T(8,128)S(1)}, f32[288,128]{1,0:T(8,128)S(1)}, u32[]{:S(2)}, u32[]{:S(2)}) collective-permute-start(f32[288,128]{1,0:T(8,128)S(1)} %plus.3.refs_2_.refs_1_), channel_id=1, source_target_pairs={{0,1},{1,0},{2,3},{3,2},{4,5},{5,4},{6,7},{7,6},{8,9},{9,8},{10,11... | collective-permute-start | bytes 442376 | tf_op jit(solution)/shard_map/ppermute | solution.py:779
  54.5 16.5 %collective-permute-start.11 = (f32[288,128]{1,0:T(8,128)S(1)}, f32[288,128]{1,0:T(8,128)S(1)}, u32[]{:S(2)}, u32[]{:S(2)}) collective-permute-start(f32[288,128]{1,0:T(8,128)S(1)} %plus.2), channel_id=1, source_target_pairs={{0,16},{2,18},{4,20},{6,22},{8,24},{10,26},{12,28},{14,30},{16,0},... | collective-permute-start | bytes 442376 | tf_op jit(solution)/shard_map/ppermute | solution.py:792
  70.8 26.6 %copy-start.1 = (f32[71942]{0:T(1024)S(1)}, f32[71942]{0:T(1024)}, u32[]{:S(2)}) copy-start(f32[71942]{0:T(1024)} %refs_6_.4) | copy-start | bytes 863308
  70.9 26.6 %copy-start.3 = (f32[71942]{0:T(1024)S(1)}, f32[71942]{0:T(1024)}, u32[]{:S(2)}) copy-start(f32[71942]{0:T(1024)} %refs_4_.5) | copy-start | bytes 863308
  70.9 26.6 %copy-start.4 = (f32[71942]{0:T(1024)S(1)}, f32[71942]{0:T(1024)}, u32[]{:S(2)}) copy-start(f32[71942]{0:T(1024)} %refs_5_.2) | copy-start | bytes 863308
  70.9 1.4 %collective-permute-start.12 = (f32[288,128]{1,0:T(8,128)S(1)}, f32[288,128]{1,0:T(8,128)S(1)}, u32[]{:S(2)}, u32[]{:S(2)}) collective-permute-start(f32[288,128]{1,0:T(8,128)S(1)} %get-tuple-element.160), channel_id=1, source_target_pairs={{0,1},{1,0},{2,3},{3,2},{4,5},{5,4},{6,7},{7,6},{8,9},{9,8},{10,11... | collective-permute-start | bytes 442376 | tf_op jit(solution)/shard_map/ppermute | solution.py:779
  72.3 5.2 %collective-permute-start.13 = (f32[288,128]{1,0:T(8,128)S(1)}, f32[288,128]{1,0:T(8,128)S(1)}, u32[]{:S(2)}, u32[]{:S(2)}) collective-permute-start(f32[288,128]{1,0:T(8,128)S(1)} %add.44), channel_id=1, source_target_pairs={{0,2},{1,9},{2,0},{3,11},{4,6},{5,13},{6,4},{7,15},{8,10},{9,1},{1... | collective-permute-start | bytes 442376 | tf_op jit(solution)/shard_map/ppermute | solution.py:801
  73.9 6.0 %collective-permute-start.18 = (f32[288,128]{1,0:T(8,128)S(1)}, f32[288,128]{1,0:T(8,128)S(1)}, u32[]{:S(2)}, u32[]{:S(2)}) collective-permute-start(f32[288,128]{1,0:T(8,128)S(1)} %add.43), channel_id=1, source_target_pairs={{0,8},{2,10},{4,12},{6,14},{8,0},{10,2},{12,4},{14,6},{16,24},{18,... | collective-permute-start | bytes 442376 | tf_op jit(solution)/shard_map/ppermute | solution.py:792
  77.6 5.2 %collective-permute-start.14 = (f32[288,128]{1,0:T(8,128)S(1)}, f32[288,128]{1,0:T(8,128)S(1)}, u32[]{:S(2)}, u32[]{:S(2)}) collective-permute-start(f32[288,128]{1,0:T(8,128)S(1)} %add.45), channel_id=1, source_target_pairs={{0,4},{1,17},{2,6},{3,19},{4,0},{5,21},{6,2},{7,23},{8,12},{9,25},... | collective-permute-start | bytes 442376 | tf_op jit(solution)/shard_map/ppermute | solution.py:801
  79.9 5.5 %collective-permute-start.19 = (f32[288,128]{1,0:T(8,128)S(1)}, f32[288,128]{1,0:T(8,128)S(1)}, u32[]{:S(2)}, u32[]{:S(2)}) collective-permute-start(f32[288,128]{1,0:T(8,128)S(1)} %add.49), channel_id=1, source_target_pairs={{0,2},{2,0},{4,6},{6,4},{8,10},{10,8},{12,14},{14,12},{16,18},{18,... | collective-permute-start | bytes 442376 | tf_op jit(solution)/shard_map/ppermute | solution.py:792
  82.8 5.2 %collective-permute-start.15 = (f32[288,128]{1,0:T(8,128)S(1)}, f32[288,128]{1,0:T(8,128)S(1)}, u32[]{:S(2)}, u32[]{:S(2)}) collective-permute-start(f32[288,128]{1,0:T(8,128)S(1)} %add.46), channel_id=1, source_target_pairs={{0,8},{1,3},{2,10},{3,1},{4,12},{5,7},{6,14},{7,5},{8,0},{9,11},{1... | collective-permute-start | bytes 442376 | tf_op jit(solution)/shard_map/ppermute | solution.py:801
  85.4 5.4 %collective-permute-start.20 = (f32[288,128]{1,0:T(8,128)S(1)}, f32[288,128]{1,0:T(8,128)S(1)}, u32[]{:S(2)}, u32[]{:S(2)}) collective-permute-start(f32[288,128]{1,0:T(8,128)S(1)} %add.50), channel_id=1, source_target_pairs={{0,4},{2,6},{4,0},{6,2},{8,12},{10,14},{12,8},{14,10},{16,20},{18,... | collective-permute-start | bytes 442376 | tf_op jit(solution)/shard_map/ppermute | solution.py:792
  88.0 7.7 %collective-permute-start.16 = (f32[288,128]{1,0:T(8,128)S(1)}, f32[288,128]{1,0:T(8,128)S(1)}, u32[]{:S(2)}, u32[]{:S(2)}) collective-permute-start(f32[288,128]{1,0:T(8,128)S(1)} %add.47), channel_id=1, source_target_pairs={{0,16},{1,5},{2,18},{3,7},{4,20},{5,1},{6,22},{7,3},{8,24},{9,13},... | collective-permute-start | bytes 442376 | tf_op jit(solution)/shard_map/ppermute | solution.py:801
  90.8 5.0 %collective-permute-start.21 = (f32[288,128]{1,0:T(8,128)S(1)}, f32[288,128]{1,0:T(8,128)S(1)}, u32[]{:S(2)}, u32[]{:S(2)}) collective-permute-start(f32[288,128]{1,0:T(8,128)S(1)} %add.51.refs_3_), channel_id=1, source_target_pairs={{0,1},{2,3},{4,5},{6,7},{8,9},{10,11},{12,13},{14,15},{16,17},{18,... | collective-permute-start | bytes 442376 | tf_op jit(solution)/shard_map/ppermute | solution.py:783
  95.7 1.7 %collective-permute-start.17 = (f32[288,128]{1,0:T(8,128)S(1)}, f32[288,128]{1,0:T(8,128)S(1)}, u32[]{:S(2)}, u32[]{:S(2)}) collective-permute-start(f32[288,128]{1,0:T(8,128)S(1)} %add.48.refs_1_), channel_id=1, source_target_pairs={{0,1},{1,0},{2,3},{3,2},{4,5},{5,4},{6,7},{7,6},{8,9},{9,8},{10,11... | collective-permute-start | bytes 442376 | tf_op jit(solution)/shard_map/ppermute | solution.py:779

commit v6 on v5

--- a/solution.py
+++ b/solution.py
@@ -392,7 +392,7 @@
     next_states,
     smoothing,
     target_actor,
-    next_action,
+    joined,
     mask_actor,
     units_actor,
     inputs,
@@ -426,7 +426,9 @@
         out = yield from forward(actor, inputs[:, columns].astype(BF16))
         lagged_action = jnp.tanh(out + tails[0:8, 0:1])
         jitter = jnp.clip(NOISE_SCALE * smoothing[:, columns], -NOISE_CLIP, NOISE_CLIP)
-        next_action[:, columns] = jnp.clip(lagged_action[0:ADIM] + jitter, -1.0, 1.0)
+        next_action = jnp.clip(lagged_action[0:ADIM] + jitter, -1.0, 1.0)
+        inputs[ACTION_ROW : ACTION_ROW + ADIM, columns] = next_action
+        joined[:, columns] = inputs[:, columns].astype(BF16)
 
     staggered([part(columns) for columns in column_parts(TILE, ACTION_PART)], LAG)
 
@@ -437,9 +439,8 @@
     states,
     actions,
     rewards,
-    next_states,
     done_flags,
-    next_action,
+    next_joined,
     own_lagged,
     far_lagged,
     own_critic,
@@ -457,10 +458,10 @@
     next_critic, next_second_t, next_column, next_tail = rest[0:4], rest[4], rest[5], rest[6]
     actor, actor_tail, actor_second_t, actor_third_t = rest[7:11], rest[11], rest[12], rest[13]
     rest = rest[14:]
-    inputs, hidden1, tail_sums, flat, spread, spread_actor, tails, next_inputs = rest[0:8]
-    lag_one, lag_two, critic = rest[8:12], rest[12:16], rest[16:20]
-    back = (rest[20], rest[21], None, None)
-    sums = rest[22:25]
+    inputs, hidden1, tail_sums, flat, spread, spread_actor, tails = rest[0:7]
+    lag_one, lag_two, critic = rest[7:11], rest[11:15], rest[15:19]
+    back = (rest[19], rest[20], None, None)
+    sums = rest[21:24]
     core = core_ref[0]
     step = pl.program_id(0)
     width = inputs.shape[1]
@@ -468,7 +469,6 @@
     @pl.when(step == 0)
     def _():
         start_inputs(inputs)
-        start_inputs(next_inputs)
         hidden1[HID : HID + 16, :] = jnp.ones((16, width), BF16)
         clear(sums)
         clear([tail_sums])
@@ -510,22 +510,27 @@
         tail = tail_column(tail_of(ACTOR, actor_weights))
         actor_tail[...] = jnp.broadcast_to(tail, (8, LANES))
 
-    next_inputs[0:SDIM, :] = next_states[...]
-    next_inputs[ACTION_ROW : ACTION_ROW + ADIM, :] = next_action[...]
-    inputs[0:SDIM, :] = states[...]
-    inputs[ACTION_ROW : ACTION_ROW + ADIM, :] = actions[...]
+    own = core * target_out.shape[1] + step * width
+
+    def span(start, columns):
+        start = pl.multiple_of(start + columns.start, LANES)
+        return pl.ds(start, columns.stop - columns.start)
+
+    tile = span(own, slice(0, width))
+    inputs[0:SDIM, :] = states[:, tile]
+    inputs[ACTION_ROW : ACTION_ROW + ADIM, :] = actions[:, tile]
 
     def part(columns):
-        joined = next_inputs[:, columns].astype(BF16)
+        joined = next_joined[:, span(step * width, columns)]
         out_one = yield from forward(lag_one, joined)
         yield
         out_two = yield from forward(lag_two, joined)
         value_one = out_one[0:1] + tails[8:9, 0:1]
         value_two = out_two[0:1] + tails[16:17, 0:1]
-        keep_going = 1.0 - done_flags[:, columns].astype(F32)
+        keep_going = 1.0 - done_flags[:, span(own, columns)].astype(F32)
         lagged = jnp.minimum(value_one, value_two)
-        target = rewards[:, columns] + DISCOUNT * keep_going * lagged
-        target_out[:, columns] = target
+        target = rewards[:, span(own, columns)] + DISCOUNT * keep_going * lagged
+        target_out[:, span(step * width, columns)] = target
 
     def next_part(columns):
         return critic_part(
@@ -533,7 +538,7 @@
             back,
             tails[24:25, 0:1],
             inputs[:, columns].astype(BF16),
-            target_out[:, columns],
+            target_out[:, span(step * width, columns)],
             2.0 / row_total,
             hidden1.at[:, columns],
             sums,
@@ -617,7 +622,9 @@
     def _():
         start_inputs(inputs)
 
-    inputs[0:SDIM, :] = states[...]
+    columns = TILE * pl.num_programs(0)
+    first_column = pl.multiple_of(core_ref[0] * columns + step * TILE, LANES)
+    inputs[0:SDIM, :] = states[:, pl.ds(first_column, TILE)]
     kept_low1[step, HID : HID + 16, :] = jnp.ones((16, TILE), BF16)
 
     def part(columns):
@@ -704,7 +711,9 @@
         tail = fresh(tail_of, gradient[CRITIC.rows : CRITIC.rows + 1, 0:1])
         tails[8:16, 0:1] = tail_column(tail)
 
-    inputs[0:SDIM, :] = states[...]
+    columns = width * pl.num_programs(0)
+    first_column = pl.multiple_of(core * columns + step * width, LANES)
+    inputs[0:SDIM, :] = states[:, pl.ds(first_column, width)]
     inputs[ACTION_ROW:IN_ROWS, :] = kept_action[step]
     judge_second_t, judge_column, judge_rows, unused = judge_back
     start = jnp.full((HID, LANES), -1.0 / row_total, F32).astype(BF16).astype(F32)
@@ -918,12 +927,12 @@
     passed = Weights.shapes + Weights.back_shapes[0:2] + (((8, LANES), F32),)
     passed_specs = [whole(shape) for shape, dtype in passed]
     passed_shapes = [jax.ShapeDtypeStruct(shape, dtype) for shape, dtype in passed]
-    next_action, *places_actor = call(
+    next_joined, *places_actor = call(
         action_kernel,
         tiles,
         [mine(SDIM), mine(ADIM), actor_flat],
-        [local(ADIM)] + place_specs,
-        [jax.ShapeDtypeStruct((ADIM, local_rows // 2), F32)] + places(ACTOR),
+        [local(IN_ROWS)] + place_specs,
+        [jax.ShapeDtypeStruct((IN_ROWS, local_rows // 2), BF16)] + places(ACTOR),
         [pltpu.VMEM((IN_ROWS, TILE), F32), flat, spread(ACTOR, 1), tails] + net,
         "next_action",
         2 * tiles * unit_flops,
@@ -933,12 +942,11 @@
     target, keep_one, send_one, *rest = call(
         lambda *refs: target_kernel(row_total, *refs),
         local_rows // 2 // TARGET_TILE,
-        [mine(rows, None, TARGET_TILE) for rows in (SDIM, ADIM, 1, SDIM, 1)]
-        + [local(ADIM, None, TARGET_TILE)]
+        [whole(None)] * 5
         + [critic_flat] * 4
         + [actor_flat]
         + place_specs,
-        [local(1, None, TARGET_TILE), half, half]
+        [whole(None), half, half]
         + place_specs
         + passed_specs
         + [whole(None)] * len(actor_shapes),
@@ -947,7 +955,7 @@
         + passed_shapes
         + actor_shapes,
         tile_scratch(TARGET_TILE)
-        + [spread(CRITIC, 4), spread(ACTOR, 1), tails, pltpu.VMEM((IN_ROWS, TARGET_TILE), F32)]
+        + [spread(CRITIC, 4), spread(ACTOR, 1), tails]
         + net * 3
         + back[0:2]
         + sums,
@@ -955,12 +963,11 @@
         14 * tiles * unit_flops,
     )(
         core,
-        in_hbm(states),
-        in_hbm(actions),
-        in_hbm(rewards),
-        in_hbm(next_states),
-        in_hbm(done_flags),
-        next_action,
+        states,
+        actions,
+        rewards,
+        done_flags,
+        next_joined,
         target_critic,
         far_lagged,
         critic_weights,
@@ -1014,7 +1021,7 @@
         return call(
             forward_kernel,
             tiles,
-            [mine(SDIM)] + [whole(None)] * 5,
+            [whole(None)] * 6,
             kept_specs,
             kept_shapes,
             [pltpu.VMEM((IN_ROWS, TILE), F32)],
@@ -1053,7 +1060,7 @@
     keep_actor, send_actor = call(
         lambda *refs: actor_kernel(row_total, *refs),
         tiles,
-        [mine(SDIM), half, half]
+        [whole(None), half, half]
         + [critic_flat] * 6
         + place_specs * 2
         + [whole(None)] * 2

time: 99.5 us -> 98.3 us (0.988)
  Pallas kernels: 58.3 us -> 57.2 us
    pallas_call x1, Pallas kernels: 18.7 us -> 17.4 us  [on_device(): call(lambda *refs: target_kernel(row_total, *refs), local_rows // 2 // TA...]
  transfers between devices with their start and end apart: 22 -> 22, of which waited for: 10 -> 10; matrix products, arithmetic and copies ran while one was open for 0% -> 0% of each run, Pallas kernels for 38% -> 39%
where the time goes in v6:
time: 98.3 us; the launch traced here: 98.1 us
  Pallas kernels  57.2 us (58%)
  starting transfers between devices  23.6 us (24%)
  waiting for transfers between devices  14.9 us (15%)
  between operations  1.16 us (1%)
  local copies, waits for them, and re-layouts  1.01 us (1%)
    pallas_call x1, Pallas kernels, on_device(): call(lambda *refs: target_kernel(row_total, *refs), local_rows // 2 // TA...  17.4 us
    pallas_call x1, Pallas kernels, on_device(): call(lambda *refs: actor_kernel(row_total, *refs), tiles, [whole(None), h...  14.7 us
    ppermute x8, starting transfers between devices, partner_by_core(): return lax.ppermute(value, ('dp', 'twin'), pairs)  13.5 us
    pallas_call x3, Pallas kernels, second_critic(): call(lambda *refs: critic_kernel(row_total, start, width, is_first, is_la...  10.5 us
    ppermute x8, waiting for transfers between devices, partner_by_core(): return lax.ppermute(value, ('dp', 'twin'), pairs)  8.89 us
    ppermute x4, starting transfers between devices, partner(): return lax.ppermute(value, 'dp', pairs)  6.03 us
    pallas_call x1, Pallas kernels, actor_forward(): call(forward_kernel, tiles, [whole(None)] * 6, kept_specs, kept_shapes, [...  5.9 us
    pallas_call x1, Pallas kernels, on_device(): call(action_kernel, tiles, [mine(SDIM), mine(ADIM), actor_flat], [local(I...  5.43 us
  transfers between devices with their start and end apart: 22, of which 10 were waited for; matrix products, arithmetic and copies ran while one was open for 0% of the time, Pallas kernels for 39%

profile of v6, /device:TPU:0, one launch (start us, length us, event | category | flops | bytes accessed | tf_op | source)
XLA Modules:
  0.0 98.1 jit_solution(1929472825632316420)
XLA Ops:
  0.6 0.5 collective-permute-start
  1.2 0.1 collective-permute-start.1
  1.2 0.4 collective-permute-start.2
  1.7 0.1 collective-permute-start.3
  1.8 1.0 copy-done
  2.8 5.4 %next_action.1 = (bf16[32,8192]{1,0:T(8,128)(2,1)S(1)}, f32[32,2176]{1,0:T(8,128)S(1)}, bf16[2176,128]{1,0:T(8,128)(2,1)S(1)}) custom-call(s32[1]{0:T(128)} %bitcast.core_ref.refs_0_, f32[17,16384]{1,0:T(8,128)} %next_states.1, f32[6,16384]{1,0:T(8,128)} %smoothing.1, f32[71942]{0:T(1024)S(1)} %copy-done), custom_call_target="tpu_custom_call" | custom-call | flops 2147483648 | bytes 1000000 | tf_op jit(solution)/shard_map/next_action/pallas_call | solution.py:930
  8.2 0.0 collective-permute-done.refs_7_
  8.2 0.0 collective-permute-done.2.refs_7_
  8.2 0.0 collective-permute-done.3.refs_9_
  8.3 17.4 %target_and_first_critic.1 = (f32[1,8192]{1,0:T(1,128)S(1)}, f32[288,128]{1,0:T(8,128)S(1)}, f32[288,128]{1,0:T(8,128)S(1)}, f32[32,2944]{1,0:T(8,128)S(1)}, bf1...) custom-call(s32[1]{0:T(128)} %bitcast.core_ref.refs_0_, ...), custom_call_target="tpu_custom_call" | custom-call | flops 15032385536 | bytes 1000000 | tf_op jit(solution)/shard_map/target_and_first_critic/pallas_call | solution.py:942
  25.8 0.5 collective-permute-start.4
  26.2 1.0 %collective-permute-done.4 = f32[288,128]{1,0:T(8,128)S(1)} collective-permute-done((f32[288,128]{1,0:T(8,128)S(1)}, f32[288,128]{1,0:T(8,128)S(1)}, u32[]{:S(2)}, u32[]{:S(2)}) %collective-permute-start.4) | collective-permute-done | bytes 147488 | tf_op jit(solution)/shard_map/ppermute | solution.py:788
  27.3 2.9 %collective-permute-start.5 = (f32[288,128]{1,0:T(8,128)S(1)}, f32[288,128]{1,0:T(8,128)S(1)}, u32[]{:S(2)}, u32[]{:S(2)}) collective-permute-start(f32[288,128]{1,0:T(8,128)S(1)} %add.39), channel_id=1, source_target_pairs={{0,2},{1,9},{2,0},{3,11},{4,6},{5,13},{6,4},{7,15},{8,10},{9,1},{1... | collective-permute-start | bytes 442376 | tf_op jit(solution)/shard_map/ppermute | solution.py:810
  30.2 3.7 %second_critic.3 = (f32[32,256]{1,0:T(8,128)S(1)}, f32[272,256]{1,0:T(8,128)S(1)}, f32[16,256]{1,0:T(8,128)S(1)}, f32[16,3072]{1,0:T(8,128)S(1)}) custom-call(s32[1]{0:T(128)} %bitcast.core_ref.refs_0_, f32[17,16384]{1,0:T(8,128)S(1)} %copy-done.9, f32[6,16384]{1,0:T(8,128)S(1)} %copy-done.10, f32[1,8192]{1,0:T(1,128)S(1)} %get-tuple-element.126.refs_3_, ...), custom_call_target="tpu_custom_call" | custom-call | flops 2147483648 | bytes 1000000 | tf_op jit(solution)/shard_map/second_critic/pallas_call | solution.py:1008
  33.9 1.6 %collective-permute-start.6 = (f32[288,128]{1,0:T(8,128)S(1)}, f32[288,128]{1,0:T(8,128)S(1)}, u32[]{:S(2)}, u32[]{:S(2)}) collective-permute-start(f32[288,128]{1,0:T(8,128)S(1)} %add.40), channel_id=1, source_target_pairs={{0,4},{1,17},{2,6},{3,19},{4,0},{5,21},{6,2},{7,23},{8,12},{9,25},... | collective-permute-start | bytes 442376 | tf_op jit(solution)/shard_map/ppermute | solution.py:810
  35.5 3.1 %second_critic.4 = (f32[32,256]{1,0:T(8,128)S(1)}, f32[272,256]{1,0:T(8,128)S(1)}, f32[16,256]{1,0:T(8,128)S(1)}, f32[16,3072]{1,0:T(8,128)S(1)}) custom-call(s32[1]{0:T(128)} %bitcast.core_ref.refs_0_, f32[17,16384]{1,0:T(8,128)S(1)} %copy-done.9, ...), custom_call_target="tpu_custom_call", output_to_operand_aliasing={{0}: (11, {}), {1}: (12, {}), {2}: (13, {}), {3}: (14, {})} | custom-call | flops 2147483648 | bytes 1000000 | tf_op jit(solution)/shard_map/second_critic/pallas_call | solution.py:1008
  38.6 0.5 collective-permute-done.6
  39.1 1.6 %collective-permute-start.7 = (f32[288,128]{1,0:T(8,128)S(1)}, f32[288,128]{1,0:T(8,128)S(1)}, u32[]{:S(2)}, u32[]{:S(2)}) collective-permute-start(f32[288,128]{1,0:T(8,128)S(1)} %add.41), channel_id=1, source_target_pairs={{0,8},{1,3},{2,10},{3,1},{4,12},{5,7},{6,14},{7,5},{8,0},{9,11},{1... | collective-permute-start | bytes 442376 | tf_op jit(solution)/shard_map/ppermute | solution.py:810
  40.8 3.7 %second_critic.5 = (f32[288,128]{1,0:T(8,128)S(1)}, f32[288,128]{1,0:T(8,128)S(1)}) custom-call(s32[1]{0:T(128)} %bitcast.core_ref.refs_0_, f32[17,16384]{1,0:T(8,128)S(1)} %copy-done.9, f32[6,16384]{1,0:T(8,128)S(1)} %copy-done.10, f32[1,8192]{1,0:T(1,128)S(1)} %get-tuple-element.126.refs_3_, bf16[256,32]{1,0:T(8,128)(2,1)S(1)} %get-tuple-element.102.refs_4_, ...), custom_call_target="tpu_custom_call" | custom-call | flops 2147483648 | bytes 1000000 | tf_op jit(solution)/shard_map/second_critic/pallas_call | solution.py:1008
  44.5 1.0 %collective-permute-start.8 = (f32[288,128]{1,0:T(8,128)S(1)}, f32[288,128]{1,0:T(8,128)S(1)}, u32[]{:S(2)}, u32[]{:S(2)}) collective-permute-start(f32[288,128]{1,0:T(8,128)S(1)} %get-tuple-element.136), channel_id=1, source_target_pairs={{0,1},{1,0},{2,3},{3,2},{4,5},{5,4},{6,7},{7,6},{8,9},{9,8},{10,11... | collective-permute-start | bytes 442376 | tf_op jit(solution)/shard_map/ppermute | solution.py:788
  45.5 1.7 %collective-permute-start.9 = (f32[288,128]{1,0:T(8,128)S(1)}, f32[288,128]{1,0:T(8,128)S(1)}, u32[]{:S(2)}, u32[]{:S(2)}) collective-permute-start(f32[288,128]{1,0:T(8,128)S(1)} %add.42.left), channel_id=1, source_target_pairs={{0,16},{1,5},{2,18},{3,7},{4,20},{5,1},{6,22},{7,3},{8,24},{9,13},... | collective-permute-start | bytes 442376 | tf_op jit(solution)/shard_map/ppermute | solution.py:810
  47.3 5.9 %actor_forward.1 = (bf16[4,272,2048]{2,1,0:T(8,128)(2,1)S(1)}, f32[4,256,2048]{2,1,0:T(8,128)S(1)}, bf16[4,256,2048]{2,1,0:T(8,128)(2,1)S(1)}, f32[4,256,2048]{2,1,0:T(8,128)S(1)}, f32[4,8,2048]{2,1,0:T(8,128)S(1)}) custom-call(s32[1]{0:T(128)} %bitcast.core_ref.refs_0_, f32[17,16384]{1,0:T(8,128)S(1)} %copy-done.9, ...), custom_call_target="tpu_custom_call" | custom-call | flops 3221225472 | bytes 1000000 | tf_op jit(solution)/shard_map/actor_forward/pallas_call | solution.py:1021
  53.2 0.1 collective-permute-start.10
  53.3 1.7 %collective-permute-start.11 = (f32[288,128]{1,0:T(8,128)S(1)}, f32[288,128]{1,0:T(8,128)S(1)}, u32[]{:S(2)}, u32[]{:S(2)}) collective-permute-start(f32[288,128]{1,0:T(8,128)S(1)} %plus.2), channel_id=1, source_target_pairs={{0,16},{2,18},{4,20},{6,22},{8,24},{10,26},{12,28},{14,30},{16,0},... | collective-permute-start | bytes 442376 | tf_op jit(solution)/shard_map/ppermute | solution.py:801
  55.0 14.7 %actor.1 = (f32[288,128]{1,0:T(8,128)S(1)}, f32[288,128]{1,0:T(8,128)S(1)}) custom-call(s32[1]{0:T(128)} %bitcast.core_ref.refs_0_, f32[17,16384]{1,0:T(8,128)S(1)} %copy-done.9, f32[288,128]{1,0:T(8,128)S(1)} %plus.3.refs_2_.refs_1_, f32[288,128]{1,0:T(8,128)S(1)} %collective-permute-done.10.refs_3_.refs_2_, f32[1,72193]{1,0:T(1,128)S(1)} %copy-done.6, ...), custom_call_target="tpu_custom_call" | custom-call | flops 8589934592 | bytes 1000000 | tf_op jit(solution)/shard_map/actor/pallas_call | solution.py:1060
  69.8 0.0 copy-start.1
  69.8 0.0 copy-start.3
  69.8 0.0 copy-start.4
  69.8 0.1 collective-permute-start.12
  69.9 1.3 %collective-permute-done.12 = f32[288,128]{1,0:T(8,128)S(1)} collective-permute-done((f32[288,128]{1,0:T(8,128)S(1)}, f32[288,128]{1,0:T(8,128)S(1)}, u32[]{:S(2)}, u32[]{:S(2)}) %collective-permute-start.12) | collective-permute-done | bytes 147488 | tf_op jit(solution)/shard_map/ppermute | solution.py:788
  71.3 1.5 %collective-permute-start.13 = (f32[288,128]{1,0:T(8,128)S(1)}, f32[288,128]{1,0:T(8,128)S(1)}, u32[]{:S(2)}, u32[]{:S(2)}) collective-permute-start(f32[288,128]{1,0:T(8,128)S(1)} %add.44), channel_id=1, source_target_pairs={{0,2},{1,9},{2,0},{3,11},{4,6},{5,13},{6,4},{7,15},{8,10},{9,1},{1... | collective-permute-start | bytes 442376 | tf_op jit(solution)/shard_map/ppermute | solution.py:810
  72.8 1.5 %collective-permute-start.18 = (f32[288,128]{1,0:T(8,128)S(1)}, f32[288,128]{1,0:T(8,128)S(1)}, u32[]{:S(2)}, u32[]{:S(2)}) collective-permute-start(f32[288,128]{1,0:T(8,128)S(1)} %add.43), channel_id=1, source_target_pairs={{0,8},{2,10},{4,12},{6,14},{8,0},{10,2},{12,4},{14,6},{16,24},{18,... | collective-permute-start | bytes 442376 | tf_op jit(solution)/shard_map/ppermute | solution.py:801
  74.3 2.2 %collective-permute-done.13 = f32[288,128]{1,0:T(8,128)S(1)} collective-permute-done((f32[288,128]{1,0:T(8,128)S(1)}, f32[288,128]{1,0:T(8,128)S(1)}, u32[]{:S(2)}, u32[]{:S(2)}) %collective-permute-start.13) | collective-permute-done | bytes 147488 | tf_op jit(solution)/shard_map/ppermute | solution.py:810
  76.5 1.1 %collective-permute-start.14 = (f32[288,128]{1,0:T(8,128)S(1)}, f32[288,128]{1,0:T(8,128)S(1)}, u32[]{:S(2)}, u32[]{:S(2)}) collective-permute-start(f32[288,128]{1,0:T(8,128)S(1)} %add.45), channel_id=1, source_target_pairs={{0,4},{1,17},{2,6},{3,19},{4,0},{5,21},{6,2},{7,23},{8,12},{9,25},... | collective-permute-start | bytes 442376 | tf_op jit(solution)/shard_map/ppermute | solution.py:810
  77.6 1.2 %collective-permute-done.18 = f32[288,128]{1,0:T(8,128)S(1)} collective-permute-done((f32[288,128]{1,0:T(8,128)S(1)}, f32[288,128]{1,0:T(8,128)S(1)}, u32[]{:S(2)}, u32[]{:S(2)}) %collective-permute-start.18) | collective-permute-done | bytes 147488 | tf_op jit(solution)/shard_map/ppermute | solution.py:801
  78.8 1.4 %collective-permute-start.19 = (f32[288,128]{1,0:T(8,128)S(1)}, f32[288,128]{1,0:T(8,128)S(1)}, u32[]{:S(2)}, u32[]{:S(2)}) collective-permute-start(f32[288,128]{1,0:T(8,128)S(1)} %add.49), channel_id=1, source_target_pairs={{0,2},{2,0},{4,6},{6,4},{8,10},{10,8},{12,14},{14,12},{16,18},{18,... | collective-permute-start | bytes 442376 | tf_op jit(solution)/shard_map/ppermute | solution.py:801
  80.2 1.5 %collective-permute-done.14 = f32[288,128]{1,0:T(8,128)S(1)} collective-permute-done((f32[288,128]{1,0:T(8,128)S(1)}, f32[288,128]{1,0:T(8,128)S(1)}, u32[]{:S(2)}, u32[]{:S(2)}) %collective-permute-start.14) | collective-permute-done | bytes 147488 | tf_op jit(solution)/shard_map/ppermute | solution.py:810
  81.7 1.6 %collective-permute-start.15 = (f32[288,128]{1,0:T(8,128)S(1)}, f32[288,128]{1,0:T(8,128)S(1)}, u32[]{:S(2)}, u32[]{:S(2)}) collective-permute-start(f32[288,128]{1,0:T(8,128)S(1)} %add.46), channel_id=1, source_target_pairs={{0,8},{1,3},{2,10},{3,1},{4,12},{5,7},{6,14},{7,5},{8,0},{9,11},{1... | collective-permute-start | bytes 442376 | tf_op jit(solution)/shard_map/ppermute | solution.py:810
  83.3 1.0 %collective-permute-done.19 = f32[288,128]{1,0:T(8,128)S(1)} collective-permute-done((f32[288,128]{1,0:T(8,128)S(1)}, f32[288,128]{1,0:T(8,128)S(1)}, u32[]{:S(2)}, u32[]{:S(2)}) %collective-permute-start.19) | collective-permute-done | bytes 147488 | tf_op jit(solution)/shard_map/ppermute | solution.py:801
  84.4 1.5 %collective-permute-start.20 = (f32[288,128]{1,0:T(8,128)S(1)}, f32[288,128]{1,0:T(8,128)S(1)}, u32[]{:S(2)}, u32[]{:S(2)}) collective-permute-start(f32[288,128]{1,0:T(8,128)S(1)} %add.50), channel_id=1, source_target_pairs={{0,4},{2,6},{4,0},{6,2},{8,12},{10,14},{12,8},{14,10},{16,20},{18,... | collective-permute-start | bytes 442376 | tf_op jit(solution)/shard_map/ppermute | solution.py:801
  85.8 1.1 %collective-permute-done.15 = f32[288,128]{1,0:T(8,128)S(1)} collective-permute-done((f32[288,128]{1,0:T(8,128)S(1)}, f32[288,128]{1,0:T(8,128)S(1)}, u32[]{:S(2)}, u32[]{:S(2)}) %collective-permute-start.15) | collective-permute-done | bytes 147488 | tf_op jit(solution)/shard_map/ppermute | solution.py:810
  87.0 1.3 %collective-permute-start.16 = (f32[288,128]{1,0:T(8,128)S(1)}, f32[288,128]{1,0:T(8,128)S(1)}, u32[]{:S(2)}, u32[]{:S(2)}) collective-permute-start(f32[288,128]{1,0:T(8,128)S(1)} %add.47), channel_id=1, source_target_pairs={{0,16},{1,5},{2,18},{3,7},{4,20},{5,1},{6,22},{7,3},{8,24},{9,13},... | collective-permute-start | bytes 442376 | tf_op jit(solution)/shard_map/ppermute | solution.py:810
  88.3 1.4 %collective-permute-done.20 = f32[288,128]{1,0:T(8,128)S(1)} collective-permute-done((f32[288,128]{1,0:T(8,128)S(1)}, f32[288,128]{1,0:T(8,128)S(1)}, u32[]{:S(2)}, u32[]{:S(2)}) %collective-permute-start.20) | collective-permute-done | bytes 147488 | tf_op jit(solution)/shard_map/ppermute | solution.py:801
  89.7 1.3 %collective-permute-start.21 = (f32[288,128]{1,0:T(8,128)S(1)}, f32[288,128]{1,0:T(8,128)S(1)}, u32[]{:S(2)}, u32[]{:S(2)}) collective-permute-start(f32[288,128]{1,0:T(8,128)S(1)} %add.51.refs_3_), channel_id=1, source_target_pairs={{0,1},{2,3},{4,5},{6,7},{8,9},{10,11},{12,13},{14,15},{16,17},{18,... | collective-permute-start | bytes 442376 | tf_op jit(solution)/shard_map/ppermute | solution.py:792
  91.0 3.6 %collective-permute-done.16 = f32[288,128]{1,0:T(8,128)S(1)} collective-permute-done((f32[288,128]{1,0:T(8,128)S(1)}, f32[288,128]{1,0:T(8,128)S(1)}, u32[]{:S(2)}, u32[]{:S(2)}) %collective-permute-start.16) | collective-permute-done | bytes 147488 | tf_op jit(solution)/shard_map/ppermute | solution.py:810
  94.7 0.1 collective-permute-start.17
  94.8 1.6 %critic_step.1 = (f32[1,72193]{1,0:T(1,128)}, f32[1,72193]{1,0:T(1,128)}, f32[1,72193]{1,0:T(1,128)}, f32[1,72193]{1,0:T(1,128)}, f32[1]{0:T(128)}) custom-call(s32[1]{0:T(128)} %bitcast.core_ref.refs_0_, f32[288,128]{1,0:T(8,128)S(1)} %plus.3.refs_2_.refs_1_, f32[288,128]{1,0:T(8,128)S(1)} %collective-permute-done.10.refs_3_.refs_2_, ...), custom_call_target="tpu_custom_call" | custom-call | tf_op jit(solution)/shard_map/critic_step/pallas_call | solution.py:1111
  96.4 1.5 %actor_step.1 = (f32[71942]{0:T(1024)}, f32[71942]{0:T(1024)}, f32[71942]{0:T(1024)}, f32[71942]{0:T(1024)}, f32[1]{0:T(128)}) custom-call(s32[1]{0:T(128)} %bitcast.core_ref.refs_0_, f32[288,128]{1,0:T(8,128)S(1)} %add.48.refs_1_, f32[288,128]{1,0:T(8,128)S(1)} %collective-permute-done.17.refs_2_, f32[71942]{0:T(1024)S(1)} %copy-done.2, ...), custom_call_target="tpu_custom_call" | custom-call | tf_op jit(solution)/shard_map/actor_step/pallas_call | solution.py:1111
  (46 shorter events, 0.4 us)
Async XLA Ops:
  0.6 7.5 %collective-permute-start = (f32[1,72193]{1,0:T(1,128)}, f32[1,72193]{1,0:T(1,128)S(1)}, u32[]{:S(2)}, u32[]{:S(2)}) collective-permute-start(f32[1,72193]{1,0:T(1,128)} %refs_8_.5), channel_id=1, source_target_pairs={{0,1},{1,0},{2,3},{3,2},{4,5},{5,4},{6,7},{7,6},{8,9},{9,8},{10,11... | collective-permute-start | bytes 866324 | tf_op jit(solution)/shard_map/ppermute | solution.py:788
  1.2 7.0 %collective-permute-start.1 = (f32[1,72193]{1,0:T(1,128)}, f32[1,72193]{1,0:T(1,128)S(1)}, u32[]{:S(2)}, u32[]{:S(2)}) collective-permute-start(f32[1,72193]{1,0:T(1,128)} %refs_5_.3), channel_id=1, source_target_pairs={{0,1},{1,0},{2,3},{3,2},{4,5},{5,4},{6,7},{7,6},{8,9},{9,8},{10,11... | collective-permute-start | bytes 866324 | tf_op jit(solution)/shard_map/ppermute | solution.py:788
  1.2 7.0 %collective-permute-start.2 = (f32[1,72193]{1,0:T(1,128)}, f32[1,72193]{1,0:T(1,128)S(1)}, u32[]{:S(2)}, u32[]{:S(2)}) collective-permute-start(f32[1,72193]{1,0:T(1,128)} %refs_6_.7), channel_id=1, source_target_pairs={{0,1},{1,0},{2,3},{3,2},{4,5},{5,4},{6,7},{7,6},{8,9},{9,8},{10,11... | collective-permute-start | bytes 866324 | tf_op jit(solution)/shard_map/ppermute | solution.py:788
  1.7 6.6 %collective-permute-start.3 = (f32[1,72193]{1,0:T(1,128)}, f32[1,72193]{1,0:T(1,128)S(1)}, u32[]{:S(2)}, u32[]{:S(2)}) collective-permute-start(f32[1,72193]{1,0:T(1,128)} %refs_7_.1), channel_id=1, source_target_pairs={{0,1},{1,0},{2,3},{3,2},{4,5},{5,4},{6,7},{7,6},{8,9},{9,8},{10,11... | collective-permute-start | bytes 866324 | tf_op jit(solution)/shard_map/ppermute | solution.py:788
  1.8 1.0 copy-start
  2.7 5.5 %copy-start.2 = (f32[71942]{0:T(1024)S(1)}, f32[71942]{0:T(1024)}, u32[]{:S(2)}) copy-start(f32[71942]{0:T(1024)} %refs_3_.1) | copy-start | bytes 863308
  2.7 5.5 %copy-start.5 = (f32[1,72193]{1,0:T(1,128)S(1)}, f32[1,72193]{1,0:T(1,128)}, u32[]{:S(2)}) copy-start(f32[1,72193]{1,0:T(1,128)} %refs_8_.5) | copy-start | bytes 866320
  2.7 5.5 %copy-start.6 = (f32[1,72193]{1,0:T(1,128)S(1)}, f32[1,72193]{1,0:T(1,128)}, u32[]{:S(2)}) copy-start(f32[1,72193]{1,0:T(1,128)} %refs_5_.3) | copy-start | bytes 866320
  2.7 5.5 %copy-start.9 = (f32[17,16384]{1,0:T(8,128)S(1)}, f32[17,16384]{1,0:T(8,128)}, u32[]{:S(2)}) copy-start(f32[17,16384]{1,0:T(8,128)} %refs_1_.9) | copy-start | bytes 3342340
  2.7 5.6 %copy-start.10 = (f32[6,16384]{1,0:T(8,128)S(1)}, f32[6,16384]{1,0:T(8,128)}, u32[]{:S(2)}) copy-start(f32[6,16384]{1,0:T(8,128)} %refs_2_.7) | copy-start | bytes 1179652
  2.7 5.6 %copy-start.11 = (f32[16384]{0:T(1024)S(1)}, f32[16384]{0:T(1024)}, u32[]{:S(2)}) copy-start(f32[16384]{0:T(1024)} %param.16) | copy-start | bytes 196612
  2.7 5.6 %copy-start.12 = (s32[16384]{0:T(1024)S(1)}, s32[16384]{0:T(1024)}, u32[]{:S(2)}) copy-start(s32[16384]{0:T(1024)} %param.18) | copy-start | bytes 196612
  25.8 1.5 %collective-permute-start.4 = (f32[288,128]{1,0:T(8,128)S(1)}, f32[288,128]{1,0:T(8,128)S(1)}, u32[]{:S(2)}, u32[]{:S(2)}) collective-permute-start(f32[288,128]{1,0:T(8,128)S(1)} %get-tuple-element.98), channel_id=1, source_target_pairs={{0,1},{1,0},{2,3},{3,2},{4,5},{5,4},{6,7},{7,6},{8,9},{9,8},{10,11... | collective-permute-start | bytes 442376 | tf_op jit(solution)/shard_map/ppermute | solution.py:788
  27.3 6.6 %collective-permute-start.5 = (f32[288,128]{1,0:T(8,128)S(1)}, f32[288,128]{1,0:T(8,128)S(1)}, u32[]{:S(2)}, u32[]{:S(2)}) collective-permute-start(f32[288,128]{1,0:T(8,128)S(1)} %add.39), channel_id=1, source_target_pairs={{0,2},{1,9},{2,0},{3,11},{4,6},{5,13},{6,4},{7,15},{8,10},{9,1},{1... | collective-permute-start | bytes 442376 | tf_op jit(solution)/shard_map/ppermute | solution.py:810
  33.9 5.2 %collective-permute-start.6 = (f32[288,128]{1,0:T(8,128)S(1)}, f32[288,128]{1,0:T(8,128)S(1)}, u32[]{:S(2)}, u32[]{:S(2)}) collective-permute-start(f32[288,128]{1,0:T(8,128)S(1)} %add.40), channel_id=1, source_target_pairs={{0,4},{1,17},{2,6},{3,19},{4,0},{5,21},{6,2},{7,23},{8,12},{9,25},... | collective-permute-start | bytes 442376 | tf_op jit(solution)/shard_map/ppermute | solution.py:810
  39.1 5.4 %collective-permute-start.7 = (f32[288,128]{1,0:T(8,128)S(1)}, f32[288,128]{1,0:T(8,128)S(1)}, u32[]{:S(2)}, u32[]{:S(2)}) collective-permute-start(f32[288,128]{1,0:T(8,128)S(1)} %add.41), channel_id=1, source_target_pairs={{0,8},{1,3},{2,10},{3,1},{4,12},{5,7},{6,14},{7,5},{8,0},{9,11},{1... | collective-permute-start | bytes 442376 | tf_op jit(solution)/shard_map/ppermute | solution.py:810
  44.5 8.8 %collective-permute-start.8 = (f32[288,128]{1,0:T(8,128)S(1)}, f32[288,128]{1,0:T(8,128)S(1)}, u32[]{:S(2)}, u32[]{:S(2)}) collective-permute-start(f32[288,128]{1,0:T(8,128)S(1)} %get-tuple-element.136), channel_id=1, source_target_pairs={{0,1},{1,0},{2,3},{3,2},{4,5},{5,4},{6,7},{7,6},{8,9},{9,8},{10,11... | collective-permute-start | bytes 442376 | tf_op jit(solution)/shard_map/ppermute | solution.py:788
  45.5 7.7 %collective-permute-start.9 = (f32[288,128]{1,0:T(8,128)S(1)}, f32[288,128]{1,0:T(8,128)S(1)}, u32[]{:S(2)}, u32[]{:S(2)}) collective-permute-start(f32[288,128]{1,0:T(8,128)S(1)} %add.42.left), channel_id=1, source_target_pairs={{0,16},{1,5},{2,18},{3,7},{4,20},{5,1},{6,22},{7,3},{8,24},{9,13},... | collective-permute-start | bytes 442376 | tf_op jit(solution)/shard_map/ppermute | solution.py:810
  47.2 7.8 %copy-start.7 = (f32[1,72193]{1,0:T(1,128)S(1)}, f32[1,72193]{1,0:T(1,128)}, u32[]{:S(2)}) copy-start(f32[1,72193]{1,0:T(1,128)} %refs_6_.7) | copy-start | bytes 866320
  47.3 7.8 %copy-start.8 = (f32[1,72193]{1,0:T(1,128)S(1)}, f32[1,72193]{1,0:T(1,128)}, u32[]{:S(2)}) copy-start(f32[1,72193]{1,0:T(1,128)} %refs_7_.1) | copy-start | bytes 866320
  53.2 1.8 %collective-permute-start.10 = (f32[288,128]{1,0:T(8,128)S(1)}, f32[288,128]{1,0:T(8,128)S(1)}, u32[]{:S(2)}, u32[]{:S(2)}) collective-permute-start(f32[288,128]{1,0:T(8,128)S(1)} %plus.3.refs_2_.refs_1_), channel_id=1, source_target_pairs={{0,1},{1,0},{2,3},{3,2},{4,5},{5,4},{6,7},{7,6},{8,9},{9,8},{10,11... | collective-permute-start | bytes 442376 | tf_op jit(solution)/shard_map/ppermute | solution.py:788
  53.3 16.6 %collective-permute-start.11 = (f32[288,128]{1,0:T(8,128)S(1)}, f32[288,128]{1,0:T(8,128)S(1)}, u32[]{:S(2)}, u32[]{:S(2)}) collective-permute-start(f32[288,128]{1,0:T(8,128)S(1)} %plus.2), channel_id=1, source_target_pairs={{0,16},{2,18},{4,20},{6,22},{8,24},{10,26},{12,28},{14,30},{16,0},... | collective-permute-start | bytes 442376 | tf_op jit(solution)/shard_map/ppermute | solution.py:801
  69.8 26.6 %copy-start.1 = (f32[71942]{0:T(1024)S(1)}, f32[71942]{0:T(1024)}, u32[]{:S(2)}) copy-start(f32[71942]{0:T(1024)} %refs_6_.6) | copy-start | bytes 863308
  69.8 26.6 %copy-start.3 = (f32[71942]{0:T(1024)S(1)}, f32[71942]{0:T(1024)}, u32[]{:S(2)}) copy-start(f32[71942]{0:T(1024)} %refs_4_.3) | copy-start | bytes 863308
  69.8 26.6 %copy-start.4 = (f32[71942]{0:T(1024)S(1)}, f32[71942]{0:T(1024)}, u32[]{:S(2)}) copy-start(f32[71942]{0:T(1024)} %refs_5_.2) | copy-start | bytes 863308
  69.8 1.4 %collective-permute-start.12 = (f32[288,128]{1,0:T(8,128)S(1)}, f32[288,128]{1,0:T(8,128)S(1)}, u32[]{:S(2)}, u32[]{:S(2)}) collective-permute-start(f32[288,128]{1,0:T(8,128)S(1)} %get-tuple-element.160), channel_id=1, source_target_pairs={{0,1},{1,0},{2,3},{3,2},{4,5},{5,4},{6,7},{7,6},{8,9},{9,8},{10,11... | collective-permute-start | bytes 442376 | tf_op jit(solution)/shard_map/ppermute | solution.py:788
  71.3 5.2 %collective-permute-start.13 = (f32[288,128]{1,0:T(8,128)S(1)}, f32[288,128]{1,0:T(8,128)S(1)}, u32[]{:S(2)}, u32[]{:S(2)}) collective-permute-start(f32[288,128]{1,0:T(8,128)S(1)} %add.44), channel_id=1, source_target_pairs={{0,2},{1,9},{2,0},{3,11},{4,6},{5,13},{6,4},{7,15},{8,10},{9,1},{1... | collective-permute-start | bytes 442376 | tf_op jit(solution)/shard_map/ppermute | solution.py:810
  72.8 6.0 %collective-permute-start.18 = (f32[288,128]{1,0:T(8,128)S(1)}, f32[288,128]{1,0:T(8,128)S(1)}, u32[]{:S(2)}, u32[]{:S(2)}) collective-permute-start(f32[288,128]{1,0:T(8,128)S(1)} %add.43), channel_id=1, source_target_pairs={{0,8},{2,10},{4,12},{6,14},{8,0},{10,2},{12,4},{14,6},{16,24},{18,... | collective-permute-start | bytes 442376 | tf_op jit(solution)/shard_map/ppermute | solution.py:801
  76.5 5.2 %collective-permute-start.14 = (f32[288,128]{1,0:T(8,128)S(1)}, f32[288,128]{1,0:T(8,128)S(1)}, u32[]{:S(2)}, u32[]{:S(2)}) collective-permute-start(f32[288,128]{1,0:T(8,128)S(1)} %add.45), channel_id=1, source_target_pairs={{0,4},{1,17},{2,6},{3,19},{4,0},{5,21},{6,2},{7,23},{8,12},{9,25},... | collective-permute-start | bytes 442376 | tf_op jit(solution)/shard_map/ppermute | solution.py:810
  78.8 5.5 %collective-permute-start.19 = (f32[288,128]{1,0:T(8,128)S(1)}, f32[288,128]{1,0:T(8,128)S(1)}, u32[]{:S(2)}, u32[]{:S(2)}) collective-permute-start(f32[288,128]{1,0:T(8,128)S(1)} %add.49), channel_id=1, source_target_pairs={{0,2},{2,0},{4,6},{6,4},{8,10},{10,8},{12,14},{14,12},{16,18},{18,... | collective-permute-start | bytes 442376 | tf_op jit(solution)/shard_map/ppermute | solution.py:801
  81.7 5.2 %collective-permute-start.15 = (f32[288,128]{1,0:T(8,128)S(1)}, f32[288,128]{1,0:T(8,128)S(1)}, u32[]{:S(2)}, u32[]{:S(2)}) collective-permute-start(f32[288,128]{1,0:T(8,128)S(1)} %add.46), channel_id=1, source_target_pairs={{0,8},{1,3},{2,10},{3,1},{4,12},{5,7},{6,14},{7,5},{8,0},{9,11},{1... | collective-permute-start | bytes 442376 | tf_op jit(solution)/shard_map/ppermute | solution.py:810
  84.4 5.4 %collective-permute-start.20 = (f32[288,128]{1,0:T(8,128)S(1)}, f32[288,128]{1,0:T(8,128)S(1)}, u32[]{:S(2)}, u32[]{:S(2)}) collective-permute-start(f32[288,128]{1,0:T(8,128)S(1)} %add.50), channel_id=1, source_target_pairs={{0,4},{2,6},{4,0},{6,2},{8,12},{10,14},{12,8},{14,10},{16,20},{18,... | collective-permute-start | bytes 442376 | tf_op jit(solution)/shard_map/ppermute | solution.py:801
  87.0 7.7 %collective-permute-start.16 = (f32[288,128]{1,0:T(8,128)S(1)}, f32[288,128]{1,0:T(8,128)S(1)}, u32[]{:S(2)}, u32[]{:S(2)}) collective-permute-start(f32[288,128]{1,0:T(8,128)S(1)} %add.47), channel_id=1, source_target_pairs={{0,16},{1,5},{2,18},{3,7},{4,20},{5,1},{6,22},{7,3},{8,24},{9,13},... | collective-permute-start | bytes 442376 | tf_op jit(solution)/shard_map/ppermute | solution.py:810
  89.7 5.0 %collective-permute-start.21 = (f32[288,128]{1,0:T(8,128)S(1)}, f32[288,128]{1,0:T(8,128)S(1)}, u32[]{:S(2)}, u32[]{:S(2)}) collective-permute-start(f32[288,128]{1,0:T(8,128)S(1)} %add.51.refs_3_), channel_id=1, source_target_pairs={{0,1},{2,3},{4,5},{6,7},{8,9},{10,11},{12,13},{14,15},{16,17},{18,... | collective-permute-start | bytes 442376 | tf_op jit(solution)/shard_map/ppermute | solution.py:792
  94.7 1.7 %collective-permute-start.17 = (f32[288,128]{1,0:T(8,128)S(1)}, f32[288,128]{1,0:T(8,128)S(1)}, u32[]{:S(2)}, u32[]{:S(2)}) collective-permute-start(f32[288,128]{1,0:T(8,128)S(1)} %add.48.refs_1_), channel_id=1, source_target_pairs={{0,1},{1,0},{2,3},{3,2},{4,5},{5,4},{6,7},{7,6},{8,9},{9,8},{10,11... | collective-permute-start | bytes 442376 | tf_op jit(solution)/shard_map/ppermute | solution.py:788

commit v7 on v6

--- a/solution.py
+++ b/solution.py
@@ -40,6 +40,7 @@
 HALF_ROWS = FLAT_ROWS // 2
 VMEM_BYTES = 24 * 2**20
 SMALL_VMEM_BYTES = 2**21
+STEP_VMEM = 10 * 2**20
 FORWARD_VMEM = 8 * 2**20
 ACTOR_VMEM = 16 * 2**20
 
@@ -902,7 +903,7 @@
     back = scratch_of(Weights.back_shapes)
     sums = scratch_of(SUM_SHAPES)
     tails = pltpu.VMEM((32, LANES), F32)
-    params = pltpu.CompilerParams(vmem_limit_bytes=VMEM_BYTES)
+    params = pltpu.CompilerParams(vmem_limit_bytes=STEP_VMEM)
 
     def call(
         kernel, steps, in_specs, out_specs, out_shape, scratch, name, flops, aliases=(), vmem=VMEM_BYTES

time: 98.3 us -> 98.4 us (level)
  no operation moved by 1% of the time
where the time goes in v7:
time: 98.4 us; the launch traced here: 98.1 us
  Pallas kernels  57.2 us (58%)
  starting transfers between devices  23.6 us (24%)
  waiting for transfers between devices  14.9 us (15%)
  between operations  1.16 us (1%)
  local copies, waits for them, and re-layouts  1.01 us (1%)
    pallas_call x1, Pallas kernels, on_device(): call(lambda *refs: target_kernel(row_total, *refs), local_rows // 2 // TA...  17.4 us
    pallas_call x1, Pallas kernels, on_device(): call(lambda *refs: actor_kernel(row_total, *refs), tiles, [whole(None), h...  14.7 us
    ppermute x8, starting transfers between devices, partner_by_core(): return lax.ppermute(value, ('dp', 'twin'), pairs)  13.5 us
    pallas_call x3, Pallas kernels, second_critic(): call(lambda *refs: critic_kernel(row_total, start, width, is_first, is_la...  10.5 us
    ppermute x8, waiting for transfers between devices, partner_by_core(): return lax.ppermute(value, ('dp', 'twin'), pairs)  8.89 us
    ppermute x4, starting transfers between devices, partner(): return lax.ppermute(value, 'dp', pairs)  6.04 us
    pallas_call x1, Pallas kernels, actor_forward(): call(forward_kernel, tiles, [whole(None)] * 6, kept_specs, kept_shapes, [...  5.89 us
    pallas_call x1, Pallas kernels, on_device(): call(action_kernel, tiles, [mine(SDIM), mine(ADIM), actor_flat], [local(I...  5.43 us
  transfers between devices with their start and end apart: 22, of which 10 were waited for; matrix products, arithmetic and copies ran while one was open for 0% of the time, Pallas kernels for 39%

profile of v7, /device:TPU:0, one launch (start us, length us, event | category | flops | bytes accessed | tf_op | source)
XLA Modules:
  0.0 98.1 jit_solution(6526036578806892455)
XLA Ops:
  0.6 0.5 collective-permute-start
  1.2 0.1 collective-permute-start.1
  1.2 0.4 collective-permute-start.2
  1.7 0.1 collective-permute-start.3
  1.8 1.0 copy-done
  2.8 5.4 %next_action.1 = (bf16[32,8192]{1,0:T(8,128)(2,1)S(1)}, f32[32,2176]{1,0:T(8,128)S(1)}, bf16[2176,128]{1,0:T(8,128)(2,1)S(1)}) custom-call(s32[1]{0:T(128)} %bitcast.core_ref.refs_0_, f32[17,16384]{1,0:T(8,128)} %next_states.1, f32[6,16384]{1,0:T(8,128)} %smoothing.1, f32[71942]{0:T(1024)S(1)} %copy-done), custom_call_target="tpu_custom_call" | custom-call | flops 2147483648 | bytes 1000000 | tf_op jit(solution)/shard_map/next_action/pallas_call | solution.py:931
  8.2 0.0 collective-permute-done.refs_7_
  8.2 0.0 collective-permute-done.1.refs_9_.refs_5_
  8.2 0.0 collective-permute-done.3.refs_9_
  8.3 17.4 %target_and_first_critic.1 = (f32[1,8192]{1,0:T(1,128)S(1)}, f32[288,128]{1,0:T(8,128)S(1)}, f32[288,128]{1,0:T(8,128)S(1)}, f32[32,2944]{1,0:T(8,128)S(1)}, bf1...) custom-call(s32[1]{0:T(128)} %bitcast.core_ref.refs_0_, ...), custom_call_target="tpu_custom_call" | custom-call | flops 15032385536 | bytes 1000000 | tf_op jit(solution)/shard_map/target_and_first_critic/pallas_call | solution.py:943
  25.8 0.5 collective-permute-start.4
  26.3 1.0 %collective-permute-done.4 = f32[288,128]{1,0:T(8,128)S(1)} collective-permute-done((f32[288,128]{1,0:T(8,128)S(1)}, f32[288,128]{1,0:T(8,128)S(1)}, u32[]{:S(2)}, u32[]{:S(2)}) %collective-permute-start.4) | collective-permute-done | bytes 147488 | tf_op jit(solution)/shard_map/ppermute | solution.py:789
  27.3 2.9 %collective-permute-start.5 = (f32[288,128]{1,0:T(8,128)S(1)}, f32[288,128]{1,0:T(8,128)S(1)}, u32[]{:S(2)}, u32[]{:S(2)}) collective-permute-start(f32[288,128]{1,0:T(8,128)S(1)} %add.39), channel_id=1, source_target_pairs={{0,2},{1,9},{2,0},{3,11},{4,6},{5,13},{6,4},{7,15},{8,10},{9,1},{1... | collective-permute-start | bytes 442376 | tf_op jit(solution)/shard_map/ppermute | solution.py:811
  30.2 3.7 %second_critic.3 = (f32[32,256]{1,0:T(8,128)S(1)}, f32[272,256]{1,0:T(8,128)S(1)}, f32[16,256]{1,0:T(8,128)S(1)}, f32[16,3072]{1,0:T(8,128)S(1)}) custom-call(s32[1]{0:T(128)} %bitcast.core_ref.refs_0_, f32[17,16384]{1,0:T(8,128)S(1)} %copy-done.9, f32[6,16384]{1,0:T(8,128)S(1)} %copy-done.10, f32[1,8192]{1,0:T(1,128)S(1)} %get-tuple-element.126.refs_3_, ...), custom_call_target="tpu_custom_call" | custom-call | flops 2147483648 | bytes 1000000 | tf_op jit(solution)/shard_map/second_critic/pallas_call | solution.py:1009
  33.9 1.6 %collective-permute-start.6 = (f32[288,128]{1,0:T(8,128)S(1)}, f32[288,128]{1,0:T(8,128)S(1)}, u32[]{:S(2)}, u32[]{:S(2)}) collective-permute-start(f32[288,128]{1,0:T(8,128)S(1)} %add.40), channel_id=1, source_target_pairs={{0,4},{1,17},{2,6},{3,19},{4,0},{5,21},{6,2},{7,23},{8,12},{9,25},... | collective-permute-start | bytes 442376 | tf_op jit(solution)/shard_map/ppermute | solution.py:811
  35.5 3.1 %second_critic.4 = (f32[32,256]{1,0:T(8,128)S(1)}, f32[272,256]{1,0:T(8,128)S(1)}, f32[16,256]{1,0:T(8,128)S(1)}, f32[16,3072]{1,0:T(8,128)S(1)}) custom-call(s32[1]{0:T(128)} %bitcast.core_ref.refs_0_, f32[17,16384]{1,0:T(8,128)S(1)} %copy-done.9, ...), custom_call_target="tpu_custom_call", output_to_operand_aliasing={{0}: (11, {}), {1}: (12, {}), {2}: (13, {}), {3}: (14, {})} | custom-call | flops 2147483648 | bytes 1000000 | tf_op jit(solution)/shard_map/second_critic/pallas_call | solution.py:1009
  38.6 0.5 collective-permute-done.6
  39.1 1.6 %collective-permute-start.7 = (f32[288,128]{1,0:T(8,128)S(1)}, f32[288,128]{1,0:T(8,128)S(1)}, u32[]{:S(2)}, u32[]{:S(2)}) collective-permute-start(f32[288,128]{1,0:T(8,128)S(1)} %add.41), channel_id=1, source_target_pairs={{0,8},{1,3},{2,10},{3,1},{4,12},{5,7},{6,14},{7,5},{8,0},{9,11},{1... | collective-permute-start | bytes 442376 | tf_op jit(solution)/shard_map/ppermute | solution.py:811
  40.8 3.7 %second_critic.5 = (f32[288,128]{1,0:T(8,128)S(1)}, f32[288,128]{1,0:T(8,128)S(1)}) custom-call(s32[1]{0:T(128)} %bitcast.core_ref.refs_0_, f32[17,16384]{1,0:T(8,128)S(1)} %copy-done.9, f32[6,16384]{1,0:T(8,128)S(1)} %copy-done.10, f32[1,8192]{1,0:T(1,128)S(1)} %get-tuple-element.126.refs_3_, bf16[256,32]{1,0:T(8,128)(2,1)S(1)} %get-tuple-element.102.refs_4_, ...), custom_call_target="tpu_custom_call" | custom-call | flops 2147483648 | bytes 1000000 | tf_op jit(solution)/shard_map/second_critic/pallas_call | solution.py:1009
  44.5 1.0 collective-permute-start.8
  45.5 1.8 %collective-permute-start.9 = (f32[288,128]{1,0:T(8,128)S(1)}, f32[288,128]{1,0:T(8,128)S(1)}, u32[]{:S(2)}, u32[]{:S(2)}) collective-permute-start(f32[288,128]{1,0:T(8,128)S(1)} %add.42.left), channel_id=1, source_target_pairs={{0,16},{1,5},{2,18},{3,7},{4,20},{5,1},{6,22},{7,3},{8,24},{9,13},... | collective-permute-start | bytes 442376 | tf_op jit(solution)/shard_map/ppermute | solution.py:811
  47.3 5.9 %actor_forward.1 = (bf16[4,272,2048]{2,1,0:T(8,128)(2,1)S(1)}, f32[4,256,2048]{2,1,0:T(8,128)S(1)}, bf16[4,256,2048]{2,1,0:T(8,128)(2,1)S(1)}, f32[4,256,2048]{2,1,0:T(8,128)S(1)}, f32[4,8,2048]{2,1,0:T(8,128)S(1)}) custom-call(s32[1]{0:T(128)} %bitcast.core_ref.refs_0_, f32[17,16384]{1,0:T(8,128)S(1)} %copy-done.9, ...), custom_call_target="tpu_custom_call" | custom-call | flops 3221225472 | bytes 1000000 | tf_op jit(solution)/shard_map/actor_forward/pallas_call | solution.py:1022
  53.2 0.1 collective-permute-start.10
  53.3 1.7 %collective-permute-start.11 = (f32[288,128]{1,0:T(8,128)S(1)}, f32[288,128]{1,0:T(8,128)S(1)}, u32[]{:S(2)}, u32[]{:S(2)}) collective-permute-start(f32[288,128]{1,0:T(8,128)S(1)} %plus.2), channel_id=1, source_target_pairs={{0,16},{2,18},{4,20},{6,22},{8,24},{10,26},{12,28},{14,30},{16,0},... | collective-permute-start | bytes 442376 | tf_op jit(solution)/shard_map/ppermute | solution.py:802
  55.0 14.7 %actor.1 = (f32[288,128]{1,0:T(8,128)S(1)}, f32[288,128]{1,0:T(8,128)S(1)}) custom-call(s32[1]{0:T(128)} %bitcast.core_ref.refs_0_, f32[17,16384]{1,0:T(8,128)S(1)} %copy-done.9, f32[288,128]{1,0:T(8,128)S(1)} %plus.3.refs_2_.refs_1_, f32[288,128]{1,0:T(8,128)S(1)} %collective-permute-done.10.refs_3_.refs_2_, f32[1,72193]{1,0:T(1,128)S(1)} %copy-done.6, ...), custom_call_target="tpu_custom_call" | custom-call | flops 8589934592 | bytes 1000000 | tf_op jit(solution)/shard_map/actor/pallas_call | solution.py:1061
  69.8 0.0 copy-start.1
  69.8 0.0 copy-start.3
  69.8 0.0 copy-start.4
  69.8 0.1 collective-permute-start.12
  69.9 1.3 %collective-permute-done.12 = f32[288,128]{1,0:T(8,128)S(1)} collective-permute-done((f32[288,128]{1,0:T(8,128)S(1)}, f32[288,128]{1,0:T(8,128)S(1)}, u32[]{:S(2)}, u32[]{:S(2)}) %collective-permute-start.12) | collective-permute-done | bytes 147488 | tf_op jit(solution)/shard_map/ppermute | solution.py:789
  71.3 1.5 %collective-permute-start.13 = (f32[288,128]{1,0:T(8,128)S(1)}, f32[288,128]{1,0:T(8,128)S(1)}, u32[]{:S(2)}, u32[]{:S(2)}) collective-permute-start(f32[288,128]{1,0:T(8,128)S(1)} %add.44), channel_id=1, source_target_pairs={{0,2},{1,9},{2,0},{3,11},{4,6},{5,13},{6,4},{7,15},{8,10},{9,1},{1... | collective-permute-start | bytes 442376 | tf_op jit(solution)/shard_map/ppermute | solution.py:811
  72.8 1.5 %collective-permute-start.18 = (f32[288,128]{1,0:T(8,128)S(1)}, f32[288,128]{1,0:T(8,128)S(1)}, u32[]{:S(2)}, u32[]{:S(2)}) collective-permute-start(f32[288,128]{1,0:T(8,128)S(1)} %add.43), channel_id=1, source_target_pairs={{0,8},{2,10},{4,12},{6,14},{8,0},{10,2},{12,4},{14,6},{16,24},{18,... | collective-permute-start | bytes 442376 | tf_op jit(solution)/shard_map/ppermute | solution.py:802
  74.3 2.2 %collective-permute-done.13 = f32[288,128]{1,0:T(8,128)S(1)} collective-permute-done((f32[288,128]{1,0:T(8,128)S(1)}, f32[288,128]{1,0:T(8,128)S(1)}, u32[]{:S(2)}, u32[]{:S(2)}) %collective-permute-start.13) | collective-permute-done | bytes 147488 | tf_op jit(solution)/shard_map/ppermute | solution.py:811
  76.5 1.1 %collective-permute-start.14 = (f32[288,128]{1,0:T(8,128)S(1)}, f32[288,128]{1,0:T(8,128)S(1)}, u32[]{:S(2)}, u32[]{:S(2)}) collective-permute-start(f32[288,128]{1,0:T(8,128)S(1)} %add.45), channel_id=1, source_target_pairs={{0,4},{1,17},{2,6},{3,19},{4,0},{5,21},{6,2},{7,23},{8,12},{9,25},... | collective-permute-start | bytes 442376 | tf_op jit(solution)/shard_map/ppermute | solution.py:811
  77.6 1.2 %collective-permute-done.18 = f32[288,128]{1,0:T(8,128)S(1)} collective-permute-done((f32[288,128]{1,0:T(8,128)S(1)}, f32[288,128]{1,0:T(8,128)S(1)}, u32[]{:S(2)}, u32[]{:S(2)}) %collective-permute-start.18) | collective-permute-done | bytes 147488 | tf_op jit(solution)/shard_map/ppermute | solution.py:802
  78.8 1.4 %collective-permute-start.19 = (f32[288,128]{1,0:T(8,128)S(1)}, f32[288,128]{1,0:T(8,128)S(1)}, u32[]{:S(2)}, u32[]{:S(2)}) collective-permute-start(f32[288,128]{1,0:T(8,128)S(1)} %add.49), channel_id=1, source_target_pairs={{0,2},{2,0},{4,6},{6,4},{8,10},{10,8},{12,14},{14,12},{16,18},{18,... | collective-permute-start | bytes 442376 | tf_op jit(solution)/shard_map/ppermute | solution.py:802
  80.2 1.5 %collective-permute-done.14 = f32[288,128]{1,0:T(8,128)S(1)} collective-permute-done((f32[288,128]{1,0:T(8,128)S(1)}, f32[288,128]{1,0:T(8,128)S(1)}, u32[]{:S(2)}, u32[]{:S(2)}) %collective-permute-start.14) | collective-permute-done | bytes 147488 | tf_op jit(solution)/shard_map/ppermute | solution.py:811
  81.7 1.6 %collective-permute-start.15 = (f32[288,128]{1,0:T(8,128)S(1)}, f32[288,128]{1,0:T(8,128)S(1)}, u32[]{:S(2)}, u32[]{:S(2)}) collective-permute-start(f32[288,128]{1,0:T(8,128)S(1)} %add.46), channel_id=1, source_target_pairs={{0,8},{1,3},{2,10},{3,1},{4,12},{5,7},{6,14},{7,5},{8,0},{9,11},{1... | collective-permute-start | bytes 442376 | tf_op jit(solution)/shard_map/ppermute | solution.py:811
  83.3 1.0 %collective-permute-done.19 = f32[288,128]{1,0:T(8,128)S(1)} collective-permute-done((f32[288,128]{1,0:T(8,128)S(1)}, f32[288,128]{1,0:T(8,128)S(1)}, u32[]{:S(2)}, u32[]{:S(2)}) %collective-permute-start.19) | collective-permute-done | bytes 147488 | tf_op jit(solution)/shard_map/ppermute | solution.py:802
  84.4 1.5 %collective-permute-start.20 = (f32[288,128]{1,0:T(8,128)S(1)}, f32[288,128]{1,0:T(8,128)S(1)}, u32[]{:S(2)}, u32[]{:S(2)}) collective-permute-start(f32[288,128]{1,0:T(8,128)S(1)} %add.50), channel_id=1, source_target_pairs={{0,4},{2,6},{4,0},{6,2},{8,12},{10,14},{12,8},{14,10},{16,20},{18,... | collective-permute-start | bytes 442376 | tf_op jit(solution)/shard_map/ppermute | solution.py:802
  85.8 1.1 %collective-permute-done.15 = f32[288,128]{1,0:T(8,128)S(1)} collective-permute-done((f32[288,128]{1,0:T(8,128)S(1)}, f32[288,128]{1,0:T(8,128)S(1)}, u32[]{:S(2)}, u32[]{:S(2)}) %collective-permute-start.15) | collective-permute-done | bytes 147488 | tf_op jit(solution)/shard_map/ppermute | solution.py:811
  87.0 1.3 %collective-permute-start.16 = (f32[288,128]{1,0:T(8,128)S(1)}, f32[288,128]{1,0:T(8,128)S(1)}, u32[]{:S(2)}, u32[]{:S(2)}) collective-permute-start(f32[288,128]{1,0:T(8,128)S(1)} %add.47), channel_id=1, source_target_pairs={{0,16},{1,5},{2,18},{3,7},{4,20},{5,1},{6,22},{7,3},{8,24},{9,13},... | collective-permute-start | bytes 442376 | tf_op jit(solution)/shard_map/ppermute | solution.py:811
  88.3 1.4 %collective-permute-done.20 = f32[288,128]{1,0:T(8,128)S(1)} collective-permute-done((f32[288,128]{1,0:T(8,128)S(1)}, f32[288,128]{1,0:T(8,128)S(1)}, u32[]{:S(2)}, u32[]{:S(2)}) %collective-permute-start.20) | collective-permute-done | bytes 147488 | tf_op jit(solution)/shard_map/ppermute | solution.py:802
  89.8 1.3 %collective-permute-start.21 = (f32[288,128]{1,0:T(8,128)S(1)}, f32[288,128]{1,0:T(8,128)S(1)}, u32[]{:S(2)}, u32[]{:S(2)}) collective-permute-start(f32[288,128]{1,0:T(8,128)S(1)} %add.51.refs_3_), channel_id=1, source_target_pairs={{0,1},{2,3},{4,5},{6,7},{8,9},{10,11},{12,13},{14,15},{16,17},{18,... | collective-permute-start | bytes 442376 | tf_op jit(solution)/shard_map/ppermute | solution.py:793
  91.1 3.6 %collective-permute-done.16 = f32[288,128]{1,0:T(8,128)S(1)} collective-permute-done((f32[288,128]{1,0:T(8,128)S(1)}, f32[288,128]{1,0:T(8,128)S(1)}, u32[]{:S(2)}, u32[]{:S(2)}) %collective-permute-start.16) | collective-permute-done | bytes 147488 | tf_op jit(solution)/shard_map/ppermute | solution.py:811
  94.7 0.1 collective-permute-start.17
  94.8 1.6 %critic_step.1 = (f32[1,72193]{1,0:T(1,128)}, f32[1,72193]{1,0:T(1,128)}, f32[1,72193]{1,0:T(1,128)}, f32[1,72193]{1,0:T(1,128)}, f32[1]{0:T(128)}) custom-call(s32[1]{0:T(128)} %bitcast.core_ref.refs_0_, f32[288,128]{1,0:T(8,128)S(1)} %plus.3.refs_2_.refs_1_, f32[288,128]{1,0:T(8,128)S(1)} %collective-permute-done.10.refs_3_.refs_2_, ...), custom_call_target="tpu_custom_call" | custom-call | tf_op jit(solution)/shard_map/critic_step/pallas_call | solution.py:1112
  96.4 1.5 %actor_step.1 = (f32[71942]{0:T(1024)}, f32[71942]{0:T(1024)}, f32[71942]{0:T(1024)}, f32[71942]{0:T(1024)}, f32[1]{0:T(128)}) custom-call(s32[1]{0:T(128)} %bitcast.core_ref.refs_0_, f32[288,128]{1,0:T(8,128)S(1)} %add.48.refs_1_, f32[288,128]{1,0:T(8,128)S(1)} %collective-permute-done.17.refs_2_, f32[71942]{0:T(1024)S(1)} %copy-done.2, ...), custom_call_target="tpu_custom_call" | custom-call | tf_op jit(solution)/shard_map/actor_step/pallas_call | solution.py:1112
  (46 shorter events, 0.4 us)
Async XLA Ops:
  0.6 7.5 %collective-permute-start = (f32[1,72193]{1,0:T(1,128)}, f32[1,72193]{1,0:T(1,128)S(1)}, u32[]{:S(2)}, u32[]{:S(2)}) collective-permute-start(f32[1,72193]{1,0:T(1,128)} %refs_8_.5), channel_id=1, source_target_pairs={{0,1},{1,0},{2,3},{3,2},{4,5},{5,4},{6,7},{7,6},{8,9},{9,8},{10,11... | collective-permute-start | bytes 866324 | tf_op jit(solution)/shard_map/ppermute | solution.py:789
  1.2 7.0 %collective-permute-start.1 = (f32[1,72193]{1,0:T(1,128)}, f32[1,72193]{1,0:T(1,128)S(1)}, u32[]{:S(2)}, u32[]{:S(2)}) collective-permute-start(f32[1,72193]{1,0:T(1,128)} %refs_5_.3), channel_id=1, source_target_pairs={{0,1},{1,0},{2,3},{3,2},{4,5},{5,4},{6,7},{7,6},{8,9},{9,8},{10,11... | collective-permute-start | bytes 866324 | tf_op jit(solution)/shard_map/ppermute | solution.py:789
  1.2 7.0 %collective-permute-start.2 = (f32[1,72193]{1,0:T(1,128)}, f32[1,72193]{1,0:T(1,128)S(1)}, u32[]{:S(2)}, u32[]{:S(2)}) collective-permute-start(f32[1,72193]{1,0:T(1,128)} %refs_6_.7), channel_id=1, source_target_pairs={{0,1},{1,0},{2,3},{3,2},{4,5},{5,4},{6,7},{7,6},{8,9},{9,8},{10,11... | collective-permute-start | bytes 866324 | tf_op jit(solution)/shard_map/ppermute | solution.py:789
  1.7 6.6 %collective-permute-start.3 = (f32[1,72193]{1,0:T(1,128)}, f32[1,72193]{1,0:T(1,128)S(1)}, u32[]{:S(2)}, u32[]{:S(2)}) collective-permute-start(f32[1,72193]{1,0:T(1,128)} %refs_7_.1), channel_id=1, source_target_pairs={{0,1},{1,0},{2,3},{3,2},{4,5},{5,4},{6,7},{7,6},{8,9},{9,8},{10,11... | collective-permute-start | bytes 866324 | tf_op jit(solution)/shard_map/ppermute | solution.py:789
  1.8 1.0 copy-start
  2.7 5.5 %copy-start.2 = (f32[71942]{0:T(1024)S(1)}, f32[71942]{0:T(1024)}, u32[]{:S(2)}) copy-start(f32[71942]{0:T(1024)} %refs_3_.1) | copy-start | bytes 863308
  2.7 5.5 %copy-start.5 = (f32[1,72193]{1,0:T(1,128)S(1)}, f32[1,72193]{1,0:T(1,128)}, u32[]{:S(2)}) copy-start(f32[1,72193]{1,0:T(1,128)} %refs_8_.5) | copy-start | bytes 866320
  2.7 5.5 %copy-start.6 = (f32[1,72193]{1,0:T(1,128)S(1)}, f32[1,72193]{1,0:T(1,128)}, u32[]{:S(2)}) copy-start(f32[1,72193]{1,0:T(1,128)} %refs_5_.3) | copy-start | bytes 866320
  2.7 5.5 %copy-start.9 = (f32[17,16384]{1,0:T(8,128)S(1)}, f32[17,16384]{1,0:T(8,128)}, u32[]{:S(2)}) copy-start(f32[17,16384]{1,0:T(8,128)} %refs_1_.9) | copy-start | bytes 3342340
  2.7 5.6 %copy-start.10 = (f32[6,16384]{1,0:T(8,128)S(1)}, f32[6,16384]{1,0:T(8,128)}, u32[]{:S(2)}) copy-start(f32[6,16384]{1,0:T(8,128)} %refs_2_.7) | copy-start | bytes 1179652
  2.7 5.6 %copy-start.11 = (f32[16384]{0:T(1024)S(1)}, f32[16384]{0:T(1024)}, u32[]{:S(2)}) copy-start(f32[16384]{0:T(1024)} %param.16) | copy-start | bytes 196612
  2.7 5.6 %copy-start.12 = (s32[16384]{0:T(1024)S(1)}, s32[16384]{0:T(1024)}, u32[]{:S(2)}) copy-start(s32[16384]{0:T(1024)} %param.18) | copy-start | bytes 196612
  25.8 1.5 %collective-permute-start.4 = (f32[288,128]{1,0:T(8,128)S(1)}, f32[288,128]{1,0:T(8,128)S(1)}, u32[]{:S(2)}, u32[]{:S(2)}) collective-permute-start(f32[288,128]{1,0:T(8,128)S(1)} %get-tuple-element.98), channel_id=1, source_target_pairs={{0,1},{1,0},{2,3},{3,2},{4,5},{5,4},{6,7},{7,6},{8,9},{9,8},{10,11... | collective-permute-start | bytes 442376 | tf_op jit(solution)/shard_map/ppermute | solution.py:789
  27.3 6.6 %collective-permute-start.5 = (f32[288,128]{1,0:T(8,128)S(1)}, f32[288,128]{1,0:T(8,128)S(1)}, u32[]{:S(2)}, u32[]{:S(2)}) collective-permute-start(f32[288,128]{1,0:T(8,128)S(1)} %add.39), channel_id=1, source_target_pairs={{0,2},{1,9},{2,0},{3,11},{4,6},{5,13},{6,4},{7,15},{8,10},{9,1},{1... | collective-permute-start | bytes 442376 | tf_op jit(solution)/shard_map/ppermute | solution.py:811
  33.9 5.2 %collective-permute-start.6 = (f32[288,128]{1,0:T(8,128)S(1)}, f32[288,128]{1,0:T(8,128)S(1)}, u32[]{:S(2)}, u32[]{:S(2)}) collective-permute-start(f32[288,128]{1,0:T(8,128)S(1)} %add.40), channel_id=1, source_target_pairs={{0,4},{1,17},{2,6},{3,19},{4,0},{5,21},{6,2},{7,23},{8,12},{9,25},... | collective-permute-start | bytes 442376 | tf_op jit(solution)/shard_map/ppermute | solution.py:811
  39.1 5.4 %collective-permute-start.7 = (f32[288,128]{1,0:T(8,128)S(1)}, f32[288,128]{1,0:T(8,128)S(1)}, u32[]{:S(2)}, u32[]{:S(2)}) collective-permute-start(f32[288,128]{1,0:T(8,128)S(1)} %add.41), channel_id=1, source_target_pairs={{0,8},{1,3},{2,10},{3,1},{4,12},{5,7},{6,14},{7,5},{8,0},{9,11},{1... | collective-permute-start | bytes 442376 | tf_op jit(solution)/shard_map/ppermute | solution.py:811
  44.5 8.7 %collective-permute-start.8 = (f32[288,128]{1,0:T(8,128)S(1)}, f32[288,128]{1,0:T(8,128)S(1)}, u32[]{:S(2)}, u32[]{:S(2)}) collective-permute-start(f32[288,128]{1,0:T(8,128)S(1)} %get-tuple-element.136), channel_id=1, source_target_pairs={{0,1},{1,0},{2,3},{3,2},{4,5},{5,4},{6,7},{7,6},{8,9},{9,8},{10,11... | collective-permute-start | bytes 442376 | tf_op jit(solution)/shard_map/ppermute | solution.py:789
  45.5 7.7 %collective-permute-start.9 = (f32[288,128]{1,0:T(8,128)S(1)}, f32[288,128]{1,0:T(8,128)S(1)}, u32[]{:S(2)}, u32[]{:S(2)}) collective-permute-start(f32[288,128]{1,0:T(8,128)S(1)} %add.42.left), channel_id=1, source_target_pairs={{0,16},{1,5},{2,18},{3,7},{4,20},{5,1},{6,22},{7,3},{8,24},{9,13},... | collective-permute-start | bytes 442376 | tf_op jit(solution)/shard_map/ppermute | solution.py:811
  47.3 7.8 %copy-start.7 = (f32[1,72193]{1,0:T(1,128)S(1)}, f32[1,72193]{1,0:T(1,128)}, u32[]{:S(2)}) copy-start(f32[1,72193]{1,0:T(1,128)} %refs_6_.7) | copy-start | bytes 866320
  47.3 7.8 %copy-start.8 = (f32[1,72193]{1,0:T(1,128)S(1)}, f32[1,72193]{1,0:T(1,128)}, u32[]{:S(2)}) copy-start(f32[1,72193]{1,0:T(1,128)} %refs_7_.1) | copy-start | bytes 866320
  53.2 1.8 %collective-permute-start.10 = (f32[288,128]{1,0:T(8,128)S(1)}, f32[288,128]{1,0:T(8,128)S(1)}, u32[]{:S(2)}, u32[]{:S(2)}) collective-permute-start(f32[288,128]{1,0:T(8,128)S(1)} %plus.3.refs_2_.refs_1_), channel_id=1, source_target_pairs={{0,1},{1,0},{2,3},{3,2},{4,5},{5,4},{6,7},{7,6},{8,9},{9,8},{10,11... | collective-permute-start | bytes 442376 | tf_op jit(solution)/shard_map/ppermute | solution.py:789
  53.3 16.6 %collective-permute-start.11 = (f32[288,128]{1,0:T(8,128)S(1)}, f32[288,128]{1,0:T(8,128)S(1)}, u32[]{:S(2)}, u32[]{:S(2)}) collective-permute-start(f32[288,128]{1,0:T(8,128)S(1)} %plus.2), channel_id=1, source_target_pairs={{0,16},{2,18},{4,20},{6,22},{8,24},{10,26},{12,28},{14,30},{16,0},... | collective-permute-start | bytes 442376 | tf_op jit(solution)/shard_map/ppermute | solution.py:802
  69.8 26.6 %copy-start.1 = (f32[71942]{0:T(1024)S(1)}, f32[71942]{0:T(1024)}, u32[]{:S(2)}) copy-start(f32[71942]{0:T(1024)} %refs_6_.6) | copy-start | bytes 863308
  69.8 26.6 %copy-start.3 = (f32[71942]{0:T(1024)S(1)}, f32[71942]{0:T(1024)}, u32[]{:S(2)}) copy-start(f32[71942]{0:T(1024)} %refs_4_.3) | copy-start | bytes 863308
  69.8 26.6 %copy-start.4 = (f32[71942]{0:T(1024)S(1)}, f32[71942]{0:T(1024)}, u32[]{:S(2)}) copy-start(f32[71942]{0:T(1024)} %refs_5_.2) | copy-start | bytes 863308
  69.8 1.4 %collective-permute-start.12 = (f32[288,128]{1,0:T(8,128)S(1)}, f32[288,128]{1,0:T(8,128)S(1)}, u32[]{:S(2)}, u32[]{:S(2)}) collective-permute-start(f32[288,128]{1,0:T(8,128)S(1)} %get-tuple-element.160), channel_id=1, source_target_pairs={{0,1},{1,0},{2,3},{3,2},{4,5},{5,4},{6,7},{7,6},{8,9},{9,8},{10,11... | collective-permute-start | bytes 442376 | tf_op jit(solution)/shard_map/ppermute | solution.py:789
  71.3 5.2 %collective-permute-start.13 = (f32[288,128]{1,0:T(8,128)S(1)}, f32[288,128]{1,0:T(8,128)S(1)}, u32[]{:S(2)}, u32[]{:S(2)}) collective-permute-start(f32[288,128]{1,0:T(8,128)S(1)} %add.44), channel_id=1, source_target_pairs={{0,2},{1,9},{2,0},{3,11},{4,6},{5,13},{6,4},{7,15},{8,10},{9,1},{1... | collective-permute-start | bytes 442376 | tf_op jit(solution)/shard_map/ppermute | solution.py:811
  72.8 6.0 %collective-permute-start.18 = (f32[288,128]{1,0:T(8,128)S(1)}, f32[288,128]{1,0:T(8,128)S(1)}, u32[]{:S(2)}, u32[]{:S(2)}) collective-permute-start(f32[288,128]{1,0:T(8,128)S(1)} %add.43), channel_id=1, source_target_pairs={{0,8},{2,10},{4,12},{6,14},{8,0},{10,2},{12,4},{14,6},{16,24},{18,... | collective-permute-start | bytes 442376 | tf_op jit(solution)/shard_map/ppermute | solution.py:802
  76.5 5.2 %collective-permute-start.14 = (f32[288,128]{1,0:T(8,128)S(1)}, f32[288,128]{1,0:T(8,128)S(1)}, u32[]{:S(2)}, u32[]{:S(2)}) collective-permute-start(f32[288,128]{1,0:T(8,128)S(1)} %add.45), channel_id=1, source_target_pairs={{0,4},{1,17},{2,6},{3,19},{4,0},{5,21},{6,2},{7,23},{8,12},{9,25},... | collective-permute-start | bytes 442376 | tf_op jit(solution)/shard_map/ppermute | solution.py:811
  78.8 5.5 %collective-permute-start.19 = (f32[288,128]{1,0:T(8,128)S(1)}, f32[288,128]{1,0:T(8,128)S(1)}, u32[]{:S(2)}, u32[]{:S(2)}) collective-permute-start(f32[288,128]{1,0:T(8,128)S(1)} %add.49), channel_id=1, source_target_pairs={{0,2},{2,0},{4,6},{6,4},{8,10},{10,8},{12,14},{14,12},{16,18},{18,... | collective-permute-start | bytes 442376 | tf_op jit(solution)/shard_map/ppermute | solution.py:802
  81.7 5.2 %collective-permute-start.15 = (f32[288,128]{1,0:T(8,128)S(1)}, f32[288,128]{1,0:T(8,128)S(1)}, u32[]{:S(2)}, u32[]{:S(2)}) collective-permute-start(f32[288,128]{1,0:T(8,128)S(1)} %add.46), channel_id=1, source_target_pairs={{0,8},{1,3},{2,10},{3,1},{4,12},{5,7},{6,14},{7,5},{8,0},{9,11},{1... | collective-permute-start | bytes 442376 | tf_op jit(solution)/shard_map/ppermute | solution.py:811
  84.4 5.4 %collective-permute-start.20 = (f32[288,128]{1,0:T(8,128)S(1)}, f32[288,128]{1,0:T(8,128)S(1)}, u32[]{:S(2)}, u32[]{:S(2)}) collective-permute-start(f32[288,128]{1,0:T(8,128)S(1)} %add.50), channel_id=1, source_target_pairs={{0,4},{2,6},{4,0},{6,2},{8,12},{10,14},{12,8},{14,10},{16,20},{18,... | collective-permute-start | bytes 442376 | tf_op jit(solution)/shard_map/ppermute | solution.py:802
  87.0 7.7 %collective-permute-start.16 = (f32[288,128]{1,0:T(8,128)S(1)}, f32[288,128]{1,0:T(8,128)S(1)}, u32[]{:S(2)}, u32[]{:S(2)}) collective-permute-start(f32[288,128]{1,0:T(8,128)S(1)} %add.47), channel_id=1, source_target_pairs={{0,16},{1,5},{2,18},{3,7},{4,20},{5,1},{6,22},{7,3},{8,24},{9,13},... | collective-permute-start | bytes 442376 | tf_op jit(solution)/shard_map/ppermute | solution.py:811
  89.8 5.0 %collective-permute-start.21 = (f32[288,128]{1,0:T(8,128)S(1)}, f32[288,128]{1,0:T(8,128)S(1)}, u32[]{:S(2)}, u32[]{:S(2)}) collective-permute-start(f32[288,128]{1,0:T(8,128)S(1)} %add.51.refs_3_), channel_id=1, source_target_pairs={{0,1},{2,3},{4,5},{6,7},{8,9},{10,11},{12,13},{14,15},{16,17},{18,... | collective-permute-start | bytes 442376 | tf_op jit(solution)/shard_map/ppermute | solution.py:793
  94.7 1.7 %collective-permute-start.17 = (f32[288,128]{1,0:T(8,128)S(1)}, f32[288,128]{1,0:T(8,128)S(1)}, u32[]{:S(2)}, u32[]{:S(2)}) collective-permute-start(f32[288,128]{1,0:T(8,128)S(1)} %add.48.refs_1_), channel_id=1, source_target_pairs={{0,1},{1,0},{2,3},{3,2},{4,5},{5,4},{6,7},{7,6},{8,9},{9,8},{10,11... | collective-permute-start | bytes 442376 | tf_op jit(solution)/shard_map/ppermute | solution.py:789
